TPU v7x, 32 devices: a whole 2x2x4 slice. The times are simulated.
32 devices in a mesh: ch: 8 (over y, x, core), ta: 4 (over z).
Axes of the slice: x: 2, y: 2, z: 4, core: 2. Of those that a mesh axis runs over, the one named last changes fastest.
Arguments:
- samples: float32 [256, 8192], P('ch', 'ta'), may hold values from -80 to 80
- dead_mask: int32 [256], P('ch'), may hold values 0 or 1
- owners: int32 [2], replicated, may hold values from 0 to 7
Outputs:
- correlation: float32 [2, 32, 256, 128], P(None, None, 'ch', 'ta')
All inputs are finite; a program needn't handle non-finite values. No bound on the sum of `dead_mask` on one device may be relied on, other than what follows from the above.
Results may differ from a plain program's by a relative error of at most 0.0036.
Values may be sent and summed in bfloat16 or wider, within the bound.
No kernel may reach another device: no remote copies, remote signals or barrier semaphores. Data moves between devices by JAX's collectives and lax.ppermute only.
A program may use at most 64 MiB of HBM per device.

v0:
```python
import math

import jax
import jax.numpy as jnp
from jax import lax
from jax.sharding import PartitionSpec as P

NT = 8192
W = 32
LAGS = 128


epsilon = 1e-06
highest = lax.Precision.HIGHEST


def extended(block, sides, width):
    for axis, dim in sides:
        count = lax.axis_size(axis)
        forward = [(i, i + 1) for i in range(count - 1)]
        backward = [(target, source) for source, target in forward]
        low = lax.ppermute(
            lax.slice_in_dim(block, block.shape[dim] - width, None, axis=dim), axis, forward
        )
        high = lax.ppermute(lax.slice_in_dim(block, 0, width, axis=dim), axis, backward)
        block = jnp.concatenate([low, block, high], axis=dim)
    return block


def from_root(block, axis, source):
    block = jnp.where(lax.axis_index(axis) == source, block, jnp.zeros_like(block))
    return lax.psum(block, axis)


def phases(first_index, second_index, period):
    turn_count = first_index[:, None] * second_index[None, :] % period
    angles = turn_count.astype(jnp.float32) * (2.0 * math.pi / period)
    return (jnp.cos(angles), jnp.sin(angles))


def body(samples, dead_mask, owners):
    ch_rows, time_rows = samples.shape
    tparts = lax.axis_size("ta")
    bin_count = NT // 2
    local_bins = bin_count // tparts
    first_bin = lax.axis_index("ta") * local_bins
    frequency = first_bin + jnp.arange(local_bins, dtype=jnp.int32)
    row_span = min(time_rows, 512)
    span_cos, span_sin = phases(jnp.arange(row_span, dtype=jnp.int32), frequency, NT)
    dft_table = jnp.concatenate([span_cos, -span_sin], axis=1)
    empty_spec = jnp.zeros((ch_rows, local_bins), jnp.float32)
    pieces = lax.all_gather(samples, "ta", axis=1, tiled=True)
    row_count = pieces.shape[1]
    sub_rows = min(row_count, row_span)

    def add_block(block_index, running):
        offset = block_index * sub_rows
        sample_block = lax.dynamic_slice_in_dim(pieces, offset, sub_rows, 1)
        product = jnp.dot(
            sample_block, dft_table, precision=highest, preferred_element_type=jnp.float32
        )
        part_real = product[:, :local_bins]
        part_imag = product[:, local_bins:]
        time_anchor = jnp.reshape(offset, (1,))
        rot_cos, rot_sin = phases(time_anchor, frequency, NT)
        new_real = part_real * rot_cos + part_imag * rot_sin
        new_imag = part_imag * rot_cos - part_real * rot_sin
        return (running[0] + new_real, running[1] + new_imag)

    spec_real, spec_imag = lax.fori_loop(
        0, row_count // sub_rows, add_block, (empty_spec, empty_spec)
    )
    amplitude = jnp.sqrt(spec_real * spec_real + spec_imag * spec_imag)
    padded = extended(amplitude, (("ta", 1),), W)
    window = padded[:, 0:local_bins]
    for offset_index in range(1, 2 * W + 1):
        window = window + padded[:, offset_index : offset_index + local_bins]
    smooth = window / (2 * W + 1)
    alive_mask = dead_mask.astype(jnp.float32)[:, None]
    divisor = smooth + epsilon
    whitened = jnp.stack(
        [spec_real / divisor * alive_mask, spec_imag / divisor * alive_mask]
    ).astype(jnp.bfloat16)
    nsteps = owners.shape[0]
    panels = jnp.stack(
        [from_root(whitened, "ch", owners[step_index]) for step_index in range(nsteps)]
    )
    panel_values = panels.astype(jnp.float32)
    lag_turns = (jnp.arange(LAGS, dtype=jnp.int32) - LAGS // 2) % NT
    fblock = min(local_bins, 128)

    def corr_block(block_index, running):
        start_bin = block_index * fblock
        block_freq = lax.dynamic_slice_in_dim(frequency, start_bin, fblock)
        lag_cos, lag_sin = phases(block_freq, lag_turns, NT)
        resident = lax.dynamic_slice_in_dim(whitened, start_bin, fblock, 2).astype(jnp.float32)
        res_real = resident[0].T[:, :, None]
        res_imag = resident[1].T[:, :, None]
        first_half = res_real * lag_cos[:, None, :] + res_imag * lag_sin[:, None, :]
        second = res_imag * lag_cos[:, None, :] - res_real * lag_sin[:, None, :]
        kernel = jnp.stack([first_half, second]).reshape(2, fblock, ch_rows * LAGS)
        panel_block = lax.dynamic_slice_in_dim(panel_values, start_bin, fblock, 3)
        return running + lax.dot_general(
            panel_block,
            kernel,
            (((1, 3), (0, 1)), ((), ())),
            precision=highest,
            preferred_element_type=jnp.float32,
        )

    running = lax.fori_loop(
        0,
        local_bins // fblock,
        corr_block,
        jnp.zeros((nsteps, ch_rows, ch_rows * LAGS), jnp.float32),
    )
    running = running.reshape(nsteps, ch_rows, ch_rows, LAGS)
    shared = lax.psum_scatter(running, "ta", scatter_dimension=3, tiled=True)
    return shared * (1.0 / math.sqrt(bin_count))


def solution(mesh):
    return jax.shard_map(
        body,
        mesh=mesh,
        in_specs=(P("ch", "ta"), P("ch"), P()),
        out_specs=P(None, None, "ch", "ta"),
        check_vma=False,
    )
```

profile of v0, /device:TPU:0, one launch (start us, length us, event | category | flops | bytes accessed | tf_op | source)
XLA Modules:
  0.0 333.4 jit_solution(9591749879480689767)
XLA Ops:
  7.3 8.2 %fusion.30 = (f32[512,1024]{1,0:T(8,128)S(1)}, f32[512,1024]{1,0:T(8,128)S(1)}) fusion(s32[1024]{0:T(1024)S(1)} %iota_add_fusion), kind=kLoop, calls=%fused_computation.116 | loop fusion | flops 7864320 | bytes 4198400 | tf_op jit(solution)/shard_map/cos | solution.py:38
  15.6 2.4 pad_maximum_fusion
  18.0 21.6 %all-gather.2.cloned.1.call-done = f32[32,8192]{1,0:T(8,128)} async-done(((f32[32,2048]{1,0:T(8,128)}), f32[32,8192]{1,0:T(8,128)}) %all-gather.2.cloned.1.call-update) | async-done | bytes 1048592 | tf_op jit(solution)/shard_map/all_gather | solution.py:52
  39.6 78.3 %while.34 = (s32[]{:T(128)}, f32[32,1024]{1,0:T(8,128)S(1)}, f32[32,1024]{1,0:T(8,128)S(1)}, f32[32,8192]{1,0:T(8,128)}, f32[512,2048]{1,0:T(8,128)}, /*index=5*...) while((s32[]{:T(128)}, f32[32,1024]{1,0:T(8,128)S(1)}, f32[32,1024]{1,0:T(8,128)S(1)}, ...), condition=%wide.region_1.2_spmd.clone, body=%wide.region_0.1_spmd.clone.sunk | while | flops 402996224 | bytes 5324969 | solution.py:70
  39.6 4.7 %fusion.174 = f32[32,2048]{1,0:T(8,128)S(1)} fusion(f32[512,2048]{1,0:T(8,128)} %get-tuple-element.530, f32[32,8192]{1,0:T(8,128)} %get-tuple-element.529, s32[]{:T(128)S(6)} %select_n.164), kind=kOutput, calls=%fused_computation.4.clone.1 | convolution fusion | flops 402653184 | bytes 4521988 | tf_op jit(solution)/shard_map/while/body/eval_jaxpr/dot_general | solution.py:59
  44.5 4.7 %fusion.174 = f32[32,2048]{1,0:T(8,128)S(1)} fusion(f32[512,2048]{1,0:T(8,128)} %get-tuple-element.530, f32[32,8192]{1,0:T(8,128)} %get-tuple-element.529, s32[]{:T(128)S(6)} %select_n.164), kind=kOutput, calls=%fused_computation.4.clone.1 | convolution fusion | flops 402653184 | bytes 4521988 | tf_op jit(solution)/shard_map/while/body/eval_jaxpr/dot_general | solution.py:59
  49.4 4.7 %fusion.174 = f32[32,2048]{1,0:T(8,128)S(1)} fusion(f32[512,2048]{1,0:T(8,128)} %get-tuple-element.530, f32[32,8192]{1,0:T(8,128)} %get-tuple-element.529, s32[]{:T(128)S(6)} %select_n.164), kind=kOutput, calls=%fused_computation.4.clone.1 | convolution fusion | flops 402653184 | bytes 4521988 | tf_op jit(solution)/shard_map/while/body/eval_jaxpr/dot_general | solution.py:59
  54.3 4.7 %fusion.174 = f32[32,2048]{1,0:T(8,128)S(1)} fusion(f32[512,2048]{1,0:T(8,128)} %get-tuple-element.530, f32[32,8192]{1,0:T(8,128)} %get-tuple-element.529, s32[]{:T(128)S(6)} %select_n.164), kind=kOutput, calls=%fused_computation.4.clone.1 | convolution fusion | flops 402653184 | bytes 4521988 | tf_op jit(solution)/shard_map/while/body/eval_jaxpr/dot_general | solution.py:59
  59.2 4.7 %fusion.174 = f32[32,2048]{1,0:T(8,128)S(1)} fusion(f32[512,2048]{1,0:T(8,128)} %get-tuple-element.530, f32[32,8192]{1,0:T(8,128)} %get-tuple-element.529, s32[]{:T(128)S(6)} %select_n.164), kind=kOutput, calls=%fused_computation.4.clone.1 | convolution fusion | flops 402653184 | bytes 4521988 | tf_op jit(solution)/shard_map/while/body/eval_jaxpr/dot_general | solution.py:59
  64.1 4.7 %fusion.174 = f32[32,2048]{1,0:T(8,128)S(1)} fusion(f32[512,2048]{1,0:T(8,128)} %get-tuple-element.530, f32[32,8192]{1,0:T(8,128)} %get-tuple-element.529, s32[]{:T(128)S(6)} %select_n.164), kind=kOutput, calls=%fused_computation.4.clone.1 | convolution fusion | flops 402653184 | bytes 4521988 | tf_op jit(solution)/shard_map/while/body/eval_jaxpr/dot_general | solution.py:59
  69.0 4.7 %fusion.174 = f32[32,2048]{1,0:T(8,128)S(1)} fusion(f32[512,2048]{1,0:T(8,128)} %get-tuple-element.530, f32[32,8192]{1,0:T(8,128)} %get-tuple-element.529, s32[]{:T(128)S(6)} %select_n.164), kind=kOutput, calls=%fused_computation.4.clone.1 | convolution fusion | flops 402653184 | bytes 4521988 | tf_op jit(solution)/shard_map/while/body/eval_jaxpr/dot_general | solution.py:59
  73.9 4.7 %fusion.174 = f32[32,2048]{1,0:T(8,128)S(1)} fusion(f32[512,2048]{1,0:T(8,128)} %get-tuple-element.530, f32[32,8192]{1,0:T(8,128)} %get-tuple-element.529, s32[]{:T(128)S(6)} %select_n.164), kind=kOutput, calls=%fused_computation.4.clone.1 | convolution fusion | flops 402653184 | bytes 4521988 | tf_op jit(solution)/shard_map/while/body/eval_jaxpr/dot_general | solution.py:59
  78.8 4.7 %fusion.174 = f32[32,2048]{1,0:T(8,128)S(1)} fusion(f32[512,2048]{1,0:T(8,128)} %get-tuple-element.530, f32[32,8192]{1,0:T(8,128)} %get-tuple-element.529, s32[]{:T(128)S(6)} %select_n.164), kind=kOutput, calls=%fused_computation.4.clone.1 | convolution fusion | flops 402653184 | bytes 4521988 | tf_op jit(solution)/shard_map/while/body/eval_jaxpr/dot_general | solution.py:59
  83.6 4.7 %fusion.174 = f32[32,2048]{1,0:T(8,128)S(1)} fusion(f32[512,2048]{1,0:T(8,128)} %get-tuple-element.530, f32[32,8192]{1,0:T(8,128)} %get-tuple-element.529, s32[]{:T(128)S(6)} %select_n.164), kind=kOutput, calls=%fused_computation.4.clone.1 | convolution fusion | flops 402653184 | bytes 4521988 | tf_op jit(solution)/shard_map/while/body/eval_jaxpr/dot_general | solution.py:59
  88.5 4.7 %fusion.174 = f32[32,2048]{1,0:T(8,128)S(1)} fusion(f32[512,2048]{1,0:T(8,128)} %get-tuple-element.530, f32[32,8192]{1,0:T(8,128)} %get-tuple-element.529, s32[]{:T(128)S(6)} %select_n.164), kind=kOutput, calls=%fused_computation.4.clone.1 | convolution fusion | flops 402653184 | bytes 4521988 | tf_op jit(solution)/shard_map/while/body/eval_jaxpr/dot_general | solution.py:59
  93.4 4.7 %fusion.174 = f32[32,2048]{1,0:T(8,128)S(1)} fusion(f32[512,2048]{1,0:T(8,128)} %get-tuple-element.530, f32[32,8192]{1,0:T(8,128)} %get-tuple-element.529, s32[]{:T(128)S(6)} %select_n.164), kind=kOutput, calls=%fused_computation.4.clone.1 | convolution fusion | flops 402653184 | bytes 4521988 | tf_op jit(solution)/shard_map/while/body/eval_jaxpr/dot_general | solution.py:59
  98.3 4.7 %fusion.174 = f32[32,2048]{1,0:T(8,128)S(1)} fusion(f32[512,2048]{1,0:T(8,128)} %get-tuple-element.530, f32[32,8192]{1,0:T(8,128)} %get-tuple-element.529, s32[]{:T(128)S(6)} %select_n.164), kind=kOutput, calls=%fused_computation.4.clone.1 | convolution fusion | flops 402653184 | bytes 4521988 | tf_op jit(solution)/shard_map/while/body/eval_jaxpr/dot_general | solution.py:59
  103.2 4.7 %fusion.174 = f32[32,2048]{1,0:T(8,128)S(1)} fusion(f32[512,2048]{1,0:T(8,128)} %get-tuple-element.530, f32[32,8192]{1,0:T(8,128)} %get-tuple-element.529, s32[]{:T(128)S(6)} %select_n.164), kind=kOutput, calls=%fused_computation.4.clone.1 | convolution fusion | flops 402653184 | bytes 4521988 | tf_op jit(solution)/shard_map/while/body/eval_jaxpr/dot_general | solution.py:59
  108.1 4.7 %fusion.174 = f32[32,2048]{1,0:T(8,128)S(1)} fusion(f32[512,2048]{1,0:T(8,128)} %get-tuple-element.530, f32[32,8192]{1,0:T(8,128)} %get-tuple-element.529, s32[]{:T(128)S(6)} %select_n.164), kind=kOutput, calls=%fused_computation.4.clone.1 | convolution fusion | flops 402653184 | bytes 4521988 | tf_op jit(solution)/shard_map/while/body/eval_jaxpr/dot_general | solution.py:59
  113.0 4.7 %fusion.174 = f32[32,2048]{1,0:T(8,128)S(1)} fusion(f32[512,2048]{1,0:T(8,128)} %get-tuple-element.530, f32[32,8192]{1,0:T(8,128)} %get-tuple-element.529, s32[]{:T(128)S(6)} %select_n.164), kind=kOutput, calls=%fused_computation.4.clone.1 | convolution fusion | flops 402653184 | bytes 4521988 | tf_op jit(solution)/shard_map/while/body/eval_jaxpr/dot_general | solution.py:59
  118.0 3.3 %collective-permute-start = (f32[32,32]{1,0:T(8,128)S(1)}, f32[32,32]{1,0:T(8,128)S(1)}, u32[]{:S(2)}, u32[]{:S(2)}) collective-permute-start(f32[32,32]{1,0:T(8,128)S(1)} %get-tuple-element.412), channel_id=1, source_target_pairs={{0,1},{1,2},{2,3},{4,5},{5,6},{6,7},{8,9},{9,10},{10,11},{12,13},{... | collective-permute-start | bytes 12296 | tf_op jit(solution)/shard_map/ppermute | solution.py:22
  121.4 1.5 collective-permute-start.1
  124.8 2.2 collective-permute-done.1
  127.0 2.5 fusion.159
  130.4 52.4 %all-reduce.3.cloned.1.call-done = (bf16[1,2,32,1024]{3,2,1,0:T(8,128)(2,1)}, bf16[1,2,32,1024]{3,2,1,0:T(8,128)(2,1)}) async-done(((bf16[1,2,32,1024]{3,2,1,0:T(8,128)(2,1)}, bf16[1,2,32,1024]{3,2,1,0:T(8,128)(2,1)}), (bf16[1,2,32,1024]{3,2,1,0:T(8,128)(2,1)}, bf16[1,2,32,1024]{3,2,1,0:T(8,128)(2,1)})) %all-reduce.3.cloned.1.call-update) | async-done | bytes 262160 | tf_op jit(solution)/shard_map/psum | solution.py:32
  182.8 1.8 maximum_convert_fusion
  184.6 103.6 %while.35 = (s32[]{:T(128)}, f32[2,32,4096]{2,1,0:T(8,128)S(1)}, f32[2,2,32,1024]{3,2,1,0:T(8,128)}, bf16[2,32,1024]{2,1,0:T(8,128)(2,1)S(1)}, s32[1024]{0:T(102...) while((s32[]{:T(128)}, f32[2,32,4096]{2,1,0:T(8,128)S(1)}, ...), condition=%wide.region_5.6_spmd.clone, body=%wide.region_4.5_spmd.clone.sunk | while | flops 810264064 | bytes 19417760 | solution.py:111
  185.2 3.4 %multiply_add_fusion.2 = (f32[128,32,128]{2,1,0:T(8,128)}, f32[128,32,128]{2,1,0:T(8,128)}) fusion(f32[128,128]{1,0:T(8,128)S(1)} %get-tuple-element.500, f32[128,32]{1,0:T(8,128)S(1)} %get-tuple-element.501, f32[128,128]{1,0:T(8,128)S(1)} %get-tuple-element.502, f32[128,32]{1,0:T(8,128)S(1)} %get-tuple-element.503), kind=kLoop, calls=%fused_computation.22.clone.1 | loop fusion | flops 3145728 | bytes 4358144 | tf_op jit(solution)/shard_map/while/body/eval_jaxpr/add | solution.py:99
  188.6 1.7 add.1933
  190.3 2.7 sub.127
  193.0 4.4 %fusion.178 = f32[2,32,4096]{2,1,0:T(8,128)S(1)} fusion(f32[1,128,4096]{2,1,0:T(8,128)} %sub.127, f32[1,128,4096]{2,1,0:T(8,128)S(1)} %add.1933, f32[2,32,4096]{2,1,0:T(8,128)S(1)} %get-tuple-element.546, pred[]{:T(512)S(6)} %compare.11, f32[2,2,32,1024]{3,2,1,0:T(8,128)} %get-tuple-element.556, s32[]{:T(128)S(6)} %select_n.167), kind=kOutput, calls=%fused_computation.17.clone.1 | convolution fusion | flops 806879232 | bytes 6356997 | tf_op jit(solution)/shard_map/while/body/eval_jaxpr/dot_general | solution.py:103
  198.1 3.4 %multiply_add_fusion.2 = (f32[128,32,128]{2,1,0:T(8,128)}, f32[128,32,128]{2,1,0:T(8,128)}) fusion(f32[128,128]{1,0:T(8,128)S(1)} %get-tuple-element.500, f32[128,32]{1,0:T(8,128)S(1)} %get-tuple-element.501, f32[128,128]{1,0:T(8,128)S(1)} %get-tuple-element.502, f32[128,32]{1,0:T(8,128)S(1)} %get-tuple-element.503), kind=kLoop, calls=%fused_computation.22.clone.1 | loop fusion | flops 3145728 | bytes 4358144 | tf_op jit(solution)/shard_map/while/body/eval_jaxpr/add | solution.py:99
  201.5 1.7 add.1933
  203.3 2.7 sub.127
  206.0 4.4 %fusion.178 = f32[2,32,4096]{2,1,0:T(8,128)S(1)} fusion(f32[1,128,4096]{2,1,0:T(8,128)} %sub.127, f32[1,128,4096]{2,1,0:T(8,128)S(1)} %add.1933, f32[2,32,4096]{2,1,0:T(8,128)S(1)} %get-tuple-element.546, pred[]{:T(512)S(6)} %compare.11, f32[2,2,32,1024]{3,2,1,0:T(8,128)} %get-tuple-element.556, s32[]{:T(128)S(6)} %select_n.167), kind=kOutput, calls=%fused_computation.17.clone.1 | convolution fusion | flops 806879232 | bytes 6356997 | tf_op jit(solution)/shard_map/while/body/eval_jaxpr/dot_general | solution.py:103
  211.1 3.4 %multiply_add_fusion.2 = (f32[128,32,128]{2,1,0:T(8,128)}, f32[128,32,128]{2,1,0:T(8,128)}) fusion(f32[128,128]{1,0:T(8,128)S(1)} %get-tuple-element.500, f32[128,32]{1,0:T(8,128)S(1)} %get-tuple-element.501, f32[128,128]{1,0:T(8,128)S(1)} %get-tuple-element.502, f32[128,32]{1,0:T(8,128)S(1)} %get-tuple-element.503), kind=kLoop, calls=%fused_computation.22.clone.1 | loop fusion | flops 3145728 | bytes 4358144 | tf_op jit(solution)/shard_map/while/body/eval_jaxpr/add | solution.py:99
  214.5 1.7 add.1933
  216.2 2.7 sub.127
  219.0 4.4 %fusion.178 = f32[2,32,4096]{2,1,0:T(8,128)S(1)} fusion(f32[1,128,4096]{2,1,0:T(8,128)} %sub.127, f32[1,128,4096]{2,1,0:T(8,128)S(1)} %add.1933, f32[2,32,4096]{2,1,0:T(8,128)S(1)} %get-tuple-element.546, pred[]{:T(512)S(6)} %compare.11, f32[2,2,32,1024]{3,2,1,0:T(8,128)} %get-tuple-element.556, s32[]{:T(128)S(6)} %select_n.167), kind=kOutput, calls=%fused_computation.17.clone.1 | convolution fusion | flops 806879232 | bytes 6356997 | tf_op jit(solution)/shard_map/while/body/eval_jaxpr/dot_general | solution.py:103
  224.1 3.4 %multiply_add_fusion.2 = (f32[128,32,128]{2,1,0:T(8,128)}, f32[128,32,128]{2,1,0:T(8,128)}) fusion(f32[128,128]{1,0:T(8,128)S(1)} %get-tuple-element.500, f32[128,32]{1,0:T(8,128)S(1)} %get-tuple-element.501, f32[128,128]{1,0:T(8,128)S(1)} %get-tuple-element.502, f32[128,32]{1,0:T(8,128)S(1)} %get-tuple-element.503), kind=kLoop, calls=%fused_computation.22.clone.1 | loop fusion | flops 3145728 | bytes 4358144 | tf_op jit(solution)/shard_map/while/body/eval_jaxpr/add | solution.py:99
  227.4 1.7 add.1933
  229.2 2.7 sub.127
  231.9 4.4 %fusion.178 = f32[2,32,4096]{2,1,0:T(8,128)S(1)} fusion(f32[1,128,4096]{2,1,0:T(8,128)} %sub.127, f32[1,128,4096]{2,1,0:T(8,128)S(1)} %add.1933, f32[2,32,4096]{2,1,0:T(8,128)S(1)} %get-tuple-element.546, pred[]{:T(512)S(6)} %compare.11, f32[2,2,32,1024]{3,2,1,0:T(8,128)} %get-tuple-element.556, s32[]{:T(128)S(6)} %select_n.167), kind=kOutput, calls=%fused_computation.17.clone.1 | convolution fusion | flops 806879232 | bytes 6356997 | tf_op jit(solution)/shard_map/while/body/eval_jaxpr/dot_general | solution.py:103
  237.0 3.4 %multiply_add_fusion.2 = (f32[128,32,128]{2,1,0:T(8,128)}, f32[128,32,128]{2,1,0:T(8,128)}) fusion(f32[128,128]{1,0:T(8,128)S(1)} %get-tuple-element.500, f32[128,32]{1,0:T(8,128)S(1)} %get-tuple-element.501, f32[128,128]{1,0:T(8,128)S(1)} %get-tuple-element.502, f32[128,32]{1,0:T(8,128)S(1)} %get-tuple-element.503), kind=kLoop, calls=%fused_computation.22.clone.1 | loop fusion | flops 3145728 | bytes 4358144 | tf_op jit(solution)/shard_map/while/body/eval_jaxpr/add | solution.py:99
  240.4 1.7 add.1933
  242.1 2.7 sub.127
  244.9 4.4 %fusion.178 = f32[2,32,4096]{2,1,0:T(8,128)S(1)} fusion(f32[1,128,4096]{2,1,0:T(8,128)} %sub.127, f32[1,128,4096]{2,1,0:T(8,128)S(1)} %add.1933, f32[2,32,4096]{2,1,0:T(8,128)S(1)} %get-tuple-element.546, pred[]{:T(512)S(6)} %compare.11, f32[2,2,32,1024]{3,2,1,0:T(8,128)} %get-tuple-element.556, s32[]{:T(128)S(6)} %select_n.167), kind=kOutput, calls=%fused_computation.17.clone.1 | convolution fusion | flops 806879232 | bytes 6356997 | tf_op jit(solution)/shard_map/while/body/eval_jaxpr/dot_general | solution.py:103
  250.0 3.4 %multiply_add_fusion.2 = (f32[128,32,128]{2,1,0:T(8,128)}, f32[128,32,128]{2,1,0:T(8,128)}) fusion(f32[128,128]{1,0:T(8,128)S(1)} %get-tuple-element.500, f32[128,32]{1,0:T(8,128)S(1)} %get-tuple-element.501, f32[128,128]{1,0:T(8,128)S(1)} %get-tuple-element.502, f32[128,32]{1,0:T(8,128)S(1)} %get-tuple-element.503), kind=kLoop, calls=%fused_computation.22.clone.1 | loop fusion | flops 3145728 | bytes 4358144 | tf_op jit(solution)/shard_map/while/body/eval_jaxpr/add | solution.py:99
  253.4 1.7 add.1933
  255.1 2.7 sub.127
  257.8 4.4 %fusion.178 = f32[2,32,4096]{2,1,0:T(8,128)S(1)} fusion(f32[1,128,4096]{2,1,0:T(8,128)} %sub.127, f32[1,128,4096]{2,1,0:T(8,128)S(1)} %add.1933, f32[2,32,4096]{2,1,0:T(8,128)S(1)} %get-tuple-element.546, pred[]{:T(512)S(6)} %compare.11, f32[2,2,32,1024]{3,2,1,0:T(8,128)} %get-tuple-element.556, s32[]{:T(128)S(6)} %select_n.167), kind=kOutput, calls=%fused_computation.17.clone.1 | convolution fusion | flops 806879232 | bytes 6356997 | tf_op jit(solution)/shard_map/while/body/eval_jaxpr/dot_general | solution.py:103
  262.9 3.4 %multiply_add_fusion.2 = (f32[128,32,128]{2,1,0:T(8,128)}, f32[128,32,128]{2,1,0:T(8,128)}) fusion(f32[128,128]{1,0:T(8,128)S(1)} %get-tuple-element.500, f32[128,32]{1,0:T(8,128)S(1)} %get-tuple-element.501, f32[128,128]{1,0:T(8,128)S(1)} %get-tuple-element.502, f32[128,32]{1,0:T(8,128)S(1)} %get-tuple-element.503), kind=kLoop, calls=%fused_computation.22.clone.1 | loop fusion | flops 3145728 | bytes 4358144 | tf_op jit(solution)/shard_map/while/body/eval_jaxpr/add | solution.py:99
  266.3 1.7 add.1933
  268.1 2.7 sub.127
  270.8 4.4 %fusion.178 = f32[2,32,4096]{2,1,0:T(8,128)S(1)} fusion(f32[1,128,4096]{2,1,0:T(8,128)} %sub.127, f32[1,128,4096]{2,1,0:T(8,128)S(1)} %add.1933, f32[2,32,4096]{2,1,0:T(8,128)S(1)} %get-tuple-element.546, pred[]{:T(512)S(6)} %compare.11, f32[2,2,32,1024]{3,2,1,0:T(8,128)} %get-tuple-element.556, s32[]{:T(128)S(6)} %select_n.167), kind=kOutput, calls=%fused_computation.17.clone.1 | convolution fusion | flops 806879232 | bytes 6356997 | tf_op jit(solution)/shard_map/while/body/eval_jaxpr/dot_general | solution.py:103
  275.9 3.4 %multiply_add_fusion.2 = (f32[128,32,128]{2,1,0:T(8,128)}, f32[128,32,128]{2,1,0:T(8,128)}) fusion(f32[128,128]{1,0:T(8,128)S(1)} %get-tuple-element.500, f32[128,32]{1,0:T(8,128)S(1)} %get-tuple-element.501, f32[128,128]{1,0:T(8,128)S(1)} %get-tuple-element.502, f32[128,32]{1,0:T(8,128)S(1)} %get-tuple-element.503), kind=kLoop, calls=%fused_computation.22.clone.1 | loop fusion | flops 3145728 | bytes 4358144 | tf_op jit(solution)/shard_map/while/body/eval_jaxpr/add | solution.py:99
  279.3 1.7 add.1933
  281.0 2.7 sub.127
  283.8 4.4 %fusion.178 = f32[2,32,4096]{2,1,0:T(8,128)S(1)} fusion(f32[1,128,4096]{2,1,0:T(8,128)} %sub.127, f32[1,128,4096]{2,1,0:T(8,128)S(1)} %add.1933, f32[2,32,4096]{2,1,0:T(8,128)S(1)} %get-tuple-element.546, pred[]{:T(512)S(6)} %compare.11, f32[2,2,32,1024]{3,2,1,0:T(8,128)} %get-tuple-element.556, s32[]{:T(128)S(6)} %select_n.167), kind=kOutput, calls=%fused_computation.17.clone.1 | convolution fusion | flops 806879232 | bytes 6356997 | tf_op jit(solution)/shard_map/while/body/eval_jaxpr/dot_general | solution.py:103
  288.4 4.5 %copy.13 = f32[2,32,32,128]{2,1,0,3:T(8,128)} copy(f32[2,32,32,128]{3,2,1,0:T(8,128)S(1)} %bitcast.45) | data formatting | bytes 2097152
  292.9 4.4 %reshape.243 = f32[128,2048]{1,0:T(8,128)} reshape(f32[128,2,32,32]{3,2,1,0:T(8,128)} %bitcast.44) | data formatting | bytes 2097152
  297.3 26.6 %reduce-scatter.4.cloned.1.call-done = f32[32,2048]{1,0:T(8,128)} async-done(((f32[128,2048]{1,0:T(8,128)}), f32[32,2048]{1,0:T(8,128)}) %reduce-scatter.4.cloned.1.call-update) | async-done | bytes 262160
  324.0 1.3 reshape.244
  325.8 1.1 broadcast_multiply_fusion
  (111 shorter events, 10.1 us)
Async XLA Ops:
  6.5 33.1 %all-gather.2.cloned.1.call-start = ((), (), s32[]{:S(2)}) async-start(), calls=%async_computation.1 | async-start | bytes 1310720 | tf_op jit(solution)/shard_map/all_gather | solution.py:52
  7.3 175.5 %all-reduce.3.cloned.1.call-start = ((), (), s32[]{:S(2)}) async-start(), calls=%async_computation.3 | async-start | bytes 524288 | tf_op jit(solution)/shard_map/psum | solution.py:32
  39.6 83.3 %copy-start = (s32[2]{0:T(128)S(1)}, s32[2]{0:T(128)}, u32[]{:S(2)}) copy-start(s32[2]{0:T(128)} %param.9) | copy-start | bytes 28
  39.6 83.9 %copy-start.1 = (s32[32]{0:T(128)S(1)}, s32[32]{0:T(128)}, u32[]{:S(2)}) copy-start(s32[32]{0:T(128)} %param.8) | copy-start | bytes 388
  118.0 6.7 %collective-permute-start = (f32[32,32]{1,0:T(8,128)S(1)}, f32[32,32]{1,0:T(8,128)S(1)}, u32[]{:S(2)}, u32[]{:S(2)}) collective-permute-start(f32[32,32]{1,0:T(8,128)S(1)} %get-tuple-element.412), channel_id=1, source_target_pairs={{0,1},{1,2},{2,3},{4,5},{5,6},{6,7},{8,9},{9,10},{10,11},{12,13},{... | collective-permute-start | bytes 12296 | tf_op jit(solution)/shard_map/ppermute | solution.py:22
  121.4 5.6 %collective-permute-start.1 = (f32[32,32]{1,0:T(8,128)S(1)}, f32[32,32]{1,0:T(8,128)S(1)}, u32[]{:S(2)}, u32[]{:S(2)}) collective-permute-start(f32[32,32]{1,0:T(8,128)S(1)} %get-tuple-element.413), channel_id=1, source_target_pairs={{1,0},{2,1},{3,2},{5,4},{6,5},{7,6},{9,8},{10,9},{11,10},{13,12},{... | collective-permute-start | bytes 12296 | tf_op jit(solution)/shard_map/ppermute | solution.py:25
  130.3 193.6 %reduce-scatter.4.cloned.1.call-start = ((), (), s32[]{:S(2)}) async-start(), calls=%async_computation.2 | async-start | bytes 1310720
Sparse Core Ops, SparseCore 0:
  8.9 30.6 all-gather.1
  130.5 52.2 all-reduce.2
  297.5 26.4 reduce-scatter.3
where the time goes:
time: 335 us; the launch traced here: 333 us
  matrix products  111 us (33%)
  waiting for transfers between devices  104 us (31%)
  local copies, waits for them, and re-layouts  49.2 us (15%)
  other arithmetic  49.1 us (15%)
  between operations  14.5 us (4%)
  starting transfers between devices  4.9 us (1%)
    dot_general x16, matrix products, add_block(): jnp.dot(sample_block, dft_table, precision=highest, preferred_element_typ...  75.4 us
    psum x1, waiting for transfers between devices, from_root(): return lax.psum(block, axis)  52.4 us
    dot_general x8, matrix products, corr_block(): lax.dot_general(panel_block, kernel, (((1, 3), (0, 1)), ((), ())), precis...  35.6 us
    unnamed x4, waiting for transfers between devices  27.4 us
    add x8, other arithmetic, corr_block(): first_half = res_real * lag_cos[:, None, :] + res_imag * lag_sin[:, None, :]  27.1 us
    sub x8, local copies, waits for them, and re-layouts, corr_block(): second = res_imag * lag_cos[:, None, :] - res_real * lag_sin[:, None, :]  21.8 us
    all_gather x1, waiting for transfers between devices, body(): pieces = lax.all_gather(samples, 'ta', axis=1, tiled=True)  21.6 us
    add x8, local copies, waits for them, and re-layouts, corr_block(): first_half = res_real * lag_cos[:, None, :] + res_imag * lag_sin[:, None, :]  14 us
  transfers between devices with their start and end apart: 5, of which 4 were waited for; matrix products, arithmetic and copies ran while one was open for 3% of the time, Pallas kernels for 0%

commit v1 on v0

v1 whole, which is shorter than its diff:
```python
import math

import jax
import jax.numpy as jnp
import numpy as np
from jax import lax
from jax.experimental import pallas as pl
from jax.experimental.pallas import tpu as pltpu
from jax.sharding import PartitionSpec as P

NT = 8192
BINS = NT // 2
W = 32
LAGS = 128
EPS = 1e-06

N1 = 32
N2 = 256
K2 = BINS // N1
assert N1 == W and K2 == 128


def split_bf16(x):
    high = x.astype(jnp.bfloat16)
    low = (x - high.astype(jnp.float32)).astype(jnp.bfloat16)
    return high, low


def twiddle_tables():
    angle = 2.0 * np.pi * (np.outer(np.arange(N1), np.arange(N2)) % NT) / NT
    return np.cos(angle).astype(np.float32), np.sin(angle).astype(np.float32)


def column_tables():
    angle = 2.0 * np.pi * (np.outer(np.arange(N2), np.arange(K2)) % N2) / N2
    cos, sin = np.cos(angle), np.sin(angle)
    table = np.block([[cos, -sin], [sin, cos]])
    high = table.astype(jnp.bfloat16)
    low = (table - high.astype(np.float64)).astype(jnp.bfloat16)
    return high, low


def lag_table():
    k = np.arange(N1)[:, None] + N1 * np.arange(K2)[None, :]
    turns = (k[:, :, None] * ((np.arange(LAGS) - LAGS // 2) % NT)) % NT
    angle = 2.0 * np.pi * turns / NT
    table = np.stack([np.cos(angle), np.sin(angle)], axis=1) / math.sqrt(BINS)
    return table.reshape(N1 * 2 * K2, LAGS).astype(jnp.bfloat16)


def add(x, y):
    return y if x is None else x if y is None else x + y


def sub(x, y):
    return (None if y is None else -y) if x is None else x if y is None else x - y


def times(z, turn):
    re, im = z
    turn = turn % 1.0
    if turn == 0.0:
        return z
    if turn == 0.25:
        return im, None if re is None else -re
    cos, sin = math.cos(2 * math.pi * turn), math.sin(2 * math.pi * turn)
    if im is None:
        return re * cos, re * -sin
    return re * cos + im * sin, im * cos - re * sin


def real_fft(xs):
    n = len(xs)
    if n == 1:
        return [(xs[0], None)]
    if n == 2:
        return [(xs[0] + xs[1], None), (xs[0] - xs[1], None)]
    even, odd = real_fft(xs[0::2]), real_fft(xs[1::2])
    half = n // 2
    out = [None] * (half + 1)
    for k in range(half // 2 + 1):
        e, o = even[k], times(odd[k], k / n)
        out[k] = (add(e[0], o[0]), add(e[1], o[1]))
        re, im = sub(e[0], o[0]), sub(o[1], e[1])
        if k != half - k:
            out[half - k] = (re, im)
    return out


def spectrum_kernel(
    tparts, samples, *rest
):
    blocks = rest[: tparts - 1]
    mask, cos, sin, high, low, out, series, rows, spec = rest[tparts - 1 :]
    me = lax.axis_index("ta")
    channels = out.shape[1] // 2
    series[me] = samples[pl.ds(pl.multiple_of(me * channels, channels), channels), :]
    for step in range(1, tparts):
        series[me ^ step] = blocks[step - 1][...]
    per_part = N1 // tparts
    for start in range(0, N2, 128):
        lanes = slice(start, start + 128)
        xs = [
            series[a // per_part, :, pl.ds((a % per_part) * N2 + start, 128)] for a in range(N1)
        ]
        bins = real_fft(xs)
        for k1 in range(N1):
            if k1 <= N1 // 2:
                re, im = bins[k1]
            else:
                re, im = bins[N1 - k1]
                im = -im
            c, s = cos[k1 : k1 + 1, lanes], sin[k1 : k1 + 1, lanes]
            if im is None:
                new = re * c, -re * s
            else:
                new = re * c + im * s, im * c - re * s
            at = slice(k1 * channels, (k1 + 1) * channels)
            rows[at, start : start + 128] = new[0]
            rows[at, N2 + start : N2 + start + 128] = new[1]
    chunk = 128
    for start in range(0, N1 * channels, chunk):
        left, left_low = split_bf16(rows[start : start + chunk, :])
        total = jnp.dot(left, high[...], preferred_element_type=jnp.float32)
        total += jnp.dot(left_low, high[...], preferred_element_type=jnp.float32)
        total += jnp.dot(left, low[...], preferred_element_type=jnp.float32)
        spec[start : start + chunk, :] = total

    def parts(k1):
        at = slice(k1 * channels, (k1 + 1) * channels)
        return spec[at, :K2], spec[at, K2:]

    amplitude = []
    for k1 in range(N1):
        re, im = parts(k1)
        amplitude.append(jnp.sqrt(re * re + im * im))
    suffix = [None] * N1
    running = None
    for k1 in reversed(range(N1)):
        running = add(running, amplitude[k1])
        suffix[k1] = running
    column = running
    lane = lax.broadcasted_iota(jnp.int32, (channels, K2), 1)
    row = lax.broadcasted_iota(jnp.int32, (channels, K2), 0)
    alive = jnp.zeros((channels, K2), jnp.float32)
    for c in range(channels):
        alive = jnp.where(row == c, mask[me * channels + c].astype(jnp.float32), alive)
    prefix = None
    for k1 in range(N1):
        prefix = add(prefix, amplitude[k1])
        above = jnp.where(lane == K2 - 1, 0.0, pltpu.roll(prefix, K2 - 1, 1))
        below = jnp.where(lane == 0, 0.0, pltpu.roll(suffix[k1], 1, 1))
        divisor = (column + above + below) / (2 * W + 1) + EPS
        scale = alive / divisor
        re, im = parts(k1)
        out[k1] = jnp.concatenate([re * scale, im * scale], axis=0).astype(jnp.bfloat16)


def spectrum(samples, blocks, dead_mask):
    tparts = lax.axis_size("ta")
    channels = samples.shape[0] // tparts
    cos, sin = twiddle_tables()
    high, low = column_tables()
    vmem = pl.BlockSpec(memory_space=pltpu.VMEM)
    smem = pl.BlockSpec(memory_space=pltpu.SMEM)
    return pl.pallas_call(
        lambda *refs: spectrum_kernel(tparts, *refs),
        out_shape=jax.ShapeDtypeStruct((N1, 2 * channels, K2), jnp.bfloat16),
        in_specs=[vmem] * tparts + [smem] + [vmem] * 4,
        out_specs=vmem,
        scratch_shapes=[
            pltpu.VMEM((tparts, channels, samples.shape[1]), jnp.float32),
            pltpu.VMEM((N1 * channels, 2 * N2), jnp.float32),
            pltpu.VMEM((N1 * channels, 2 * K2), jnp.float32),
        ],
        compiler_params=pltpu.CompilerParams(vmem_limit_bytes=32 * 1024 * 1024),
        cost_estimate=pl.CostEstimate(flops=10**9, bytes_accessed=10**6, transcendentals=10**5),
        name="spectrum",
    )(samples, *blocks, dead_mask, cos, sin, high, low)


GROUP = 4


def correlate_kernel(tparts, panels, *rest):
    residents = rest[:tparts]
    table = rest[tparts]
    outs = rest[tparts + 1 : 2 * tparts + 1]
    cross, total = rest[2 * tparts + 1 :]
    steps, _, rows2, _ = panels.shape
    channels = rows2 // 2
    local = tparts * channels
    me = lax.axis_index("ta")
    total[...] = jnp.zeros_like(total)

    @pl.loop(0, N1 // GROUP)
    def _(group):
        for sub_index in range(GROUP):
            k1 = group * GROUP + sub_index
            col = sub_index * 2 * K2
            res = [r[k1].astype(jnp.float32) for r in residents]
            for s in range(steps):
                panel = panels[s, k1].astype(jnp.float32)
                for i in range(channels):
                    a = jnp.broadcast_to(panel[i : i + 1, :], (channels, K2))
                    b = jnp.broadcast_to(panel[channels + i : channels + i + 1, :], (channels, K2))
                    re, im = [], []
                    for value in res:
                        c, d = value[:channels], value[channels:]
                        re.append(a * c + b * d)
                        im.append(a * d - b * c)
                    at = pl.ds((s * channels + i) * local, local)
                    cross[at, pl.ds(col, K2)] = jnp.concatenate(re, axis=0).astype(jnp.bfloat16)
                    cross[at, pl.ds(col + K2, K2)] = jnp.concatenate(im, axis=0).astype(jnp.bfloat16)
        depth = GROUP * 2 * K2
        total[...] += jnp.dot(
            cross[...],
            table[pl.ds(pl.multiple_of(group * depth, depth), depth), :],
            preferred_element_type=jnp.float32,
        )

    width = LAGS // tparts
    lane = lax.broadcasted_iota(jnp.int32, (channels, LAGS), 1) // width
    for source in range(steps * channels):
        pieces = [
            total[source * local + step * channels : source * local + (step + 1) * channels, :]
            for step in range(tparts)
        ]
        for far in range(tparts):
            dest = me ^ far
            value = None
            for step in range(tparts):
                moved = pltpu.roll(pieces[step], (step - dest + tparts) * width % LAGS, 1)
                value = moved if value is None else jnp.where(lane == step, moved, value)
            outs[far][source * channels : (source + 1) * channels, :] = value.astype(outs[far].dtype)


def correlate(panels, residents):
    tparts = lax.axis_size("ta")
    steps, _, rows2, _ = panels.shape
    channels = rows2 // 2
    vmem = pl.BlockSpec(memory_space=pltpu.VMEM)
    pairs = steps * channels * channels * tparts
    return pl.pallas_call(
        lambda *refs: correlate_kernel(tparts, *refs),
        out_shape=[
            jax.ShapeDtypeStruct((steps * channels * channels, LAGS), jnp.float32)
        ] * tparts,
        in_specs=[vmem] * (tparts + 2),
        out_specs=[vmem] * tparts,
        scratch_shapes=[
            pltpu.VMEM((pairs, GROUP * 2 * K2), jnp.bfloat16),
            pltpu.VMEM((pairs, LAGS), jnp.float32),
        ],
        compiler_params=pltpu.CompilerParams(vmem_limit_bytes=32 * 1024 * 1024),
        cost_estimate=pl.CostEstimate(flops=4 * 10**9, bytes_accessed=3 * 10**6, transcendentals=0),
        name="correlate",
    )(panels, *residents, lag_table())


def place_kernel(tparts, steps, channels, *refs):
    pieces, out = refs[:tparts], refs[tparts]
    me = lax.axis_index("ta")
    width = LAGS // tparts
    for far in range(tparts):
        source = me ^ far
        value = pieces[far][...].astype(jnp.float32)
        for step in range(tparts):
            block = source ^ step
            moved = value if step == 0 else pltpu.roll(value, LAGS - step * width, 1)
            moved = moved[:, :width].reshape(steps, channels, channels, width)
            out[
                :,
                pl.ds(source * channels, channels),
                pl.ds(pl.multiple_of(block * channels, channels), channels),
                :,
            ] = moved


def place(pieces, steps, channels):
    tparts = lax.axis_size("ta")
    vmem = pl.BlockSpec(memory_space=pltpu.VMEM)
    local = tparts * channels
    return pl.pallas_call(
        lambda *refs: place_kernel(tparts, steps, channels, *refs),
        out_shape=jax.ShapeDtypeStruct((steps, local, local, LAGS // tparts), jnp.float32),
        in_specs=[vmem] * tparts,
        out_specs=vmem,
        compiler_params=pltpu.CompilerParams(vmem_limit_bytes=32 * 1024 * 1024),
        name="place",
    )(*pieces)


def flip(axis, mask):
    return [(i, i ^ mask) for i in range(lax.axis_size(axis))]


def owner_panels(block, owners):
    count = lax.axis_size("ch")
    steps = owners.shape[0]
    if count & (count - 1):
        return jnp.take(lax.all_gather(block, "ch"), owners, axis=0)
    me = lax.axis_index("ch")
    if count == 1:
        return jnp.stack([block] * steps)
    away = owners ^ me
    shape = (steps,) + (1,) * block.ndim
    other = lax.ppermute(block, "ch", flip("ch", 1))
    held = jnp.where(((away & 1) != 0).reshape(shape), other[None], block[None])
    masks = [1 << bit for bit in range(1, count.bit_length() - 1)]
    for even, odd in zip(masks, reversed(masks)):
        perm = [(i, i ^ (odd if i & 1 else even)) for i in range(count)]
        mask = jnp.where(me & 1, odd, even)
        other = lax.ppermute(held, "ch", perm)
        held = jnp.where(((away & mask) != 0).reshape(shape), other, held)
    return held


def body(samples, dead_mask, owners):
    tparts = lax.axis_size("ta")
    me = lax.axis_index("ta")
    channels = samples.shape[0] // tparts
    steps = owners.shape[0]

    def rows_for(part):
        return lax.dynamic_slice_in_dim(samples, part * channels, channels, 0)

    blocks = [
        lax.ppermute(rows_for(me ^ far), "ta", flip("ta", far)) for far in range(1, tparts)
    ]
    whitened = spectrum(samples, blocks, dead_mask)
    panels = owner_panels(whitened, owners)
    residents = [whitened] + [
        lax.ppermute(whitened, "ta", flip("ta", far)) for far in range(1, tparts)
    ]
    pieces = correlate(panels, residents)
    pieces = [pieces[0]] + [
        lax.ppermute(pieces[far], "ta", flip("ta", far)) for far in range(1, tparts)
    ]
    return place(pieces, steps, channels)


def solution(mesh):
    return jax.shard_map(
        body,
        mesh=mesh,
        in_specs=(P("ch", "ta"), P("ch"), P()),
        out_specs=P(None, None, "ch", "ta"),
        check_vma=False,
    )
```

time: 335 us -> 57.3 us (0.17)
  matrix products: 111 us -> 0 us
  waiting for transfers between devices: 104 us -> 24.8 us
  other arithmetic: 49.1 us -> 0.29 us
  local copies, waits for them, and re-layouts: 49.2 us -> 5.96 us
  between operations: 14.5 us -> 0.08 us
  starting transfers between devices: 4.9 us -> 17.8 us
  Pallas kernels: 0 us -> 7.98 us
    dot_general x24 -> x0, matrix products: 111 us -> none  [the longest x16 75.4 us: add_block(): jnp.dot(sample_block, dft_table, precision=highest, preferred_element_typ...]
    psum x1 -> x0, waiting for transfers between devices: 52.4 us -> none  [from_root(): return lax.psum(block, axis)]
    add x25 -> x0, other arithmetic: 28.6 us -> none  [the longest x8 27.1 us: corr_block(): first_half = res_real * lag_cos[:, None, :] + res_imag * lag_sin[:, None, :]]
    unnamed x4 -> x0, waiting for transfers between devices: 27.4 us -> none
    ppermute x2 -> x12, waiting for transfers between devices: 2.25 us -> 24.8 us  [the longest x3 8.38 us: body(): lax.ppermute(whitened, 'ta', flip('ta', far))]
    sub x8 -> x0, local copies, waits for them, and re-layouts: 21.8 us -> none  [corr_block(): second = res_imag * lag_cos[:, None, :] - res_real * lag_sin[:, None, :]]
    all_gather x1 -> x0, waiting for transfers between devices: 21.6 us -> none  [body(): pieces = lax.all_gather(samples, 'ta', axis=1, tiled=True)]
    add x8 -> x0, local copies, waits for them, and re-layouts: 14 us -> none  [corr_block(): first_half = res_real * lag_cos[:, None, :] + res_imag * lag_sin[:, None, :]]
  transfers between devices with their start and end apart: 5 -> 12, of which waited for: 4 -> 9; matrix products, arithmetic and copies ran while one was open for 3% -> 0% of each run, Pallas kernels for 0% -> 0%
where the time goes in v1:
time: 57.3 us; the launch traced here: 56.9 us
  waiting for transfers between devices  24.8 us (43%)
  starting transfers between devices  17.8 us (31%)
  Pallas kernels  7.98 us (14%)
  local copies, waits for them, and re-layouts  5.96 us (10%)
    ppermute x3, waiting for transfers between devices, body(): lax.ppermute(whitened, 'ta', flip('ta', far))  8.38 us
    ppermute x3, starting transfers between devices, body(): lax.ppermute(rows_for(me ^ far), 'ta', flip('ta', far))  5.76 us
    pallas_call x1, Pallas kernels, correlate(): pl.pallas_call(lambda *refs: correlate_kernel(tparts, *refs), out_shape=[...  5.56 us
    ppermute x2, waiting for transfers between devices, owner_panels(): other = lax.ppermute(held, 'ch', perm)  5.34 us
    unnamed x16, local copies, waits for them, and re-layouts  5.03 us
    ppermute x3, waiting for transfers between devices, body(): lax.ppermute(rows_for(me ^ far), 'ta', flip('ta', far))  4.96 us
    ppermute x3, waiting for transfers between devices, body(): lax.ppermute(pieces[far], 'ta', flip('ta', far))  4.76 us
    ppermute x3, starting transfers between devices, body(): lax.ppermute(pieces[far], 'ta', flip('ta', far))  4.44 us
  transfers between devices with their start and end apart: 12, of which 9 were waited for; matrix products, arithmetic and copies ran while one was open for 0% of the time, Pallas kernels for 0%

profile of v1, /device:TPU:0, one launch (start us, length us, event | category | flops | bytes accessed | tf_op | source)
XLA Modules:
  0.0 56.9 jit_solution(9137896751602991555)
XLA Ops:
  0.0 0.0 copy-start.7
  0.0 0.9 %constant_dynamic-slice_fusion = (f32[8,2048]{1,0:T(8,128)S(1)}, f32[8,2048]{1,0:T(8,128)S(1)}, f32[8,2048]{1,0:T(8,128)S(1)}) fusion(f32[32,2048]{1,0:T(8,128)} %refs_0_.1, s32[]{:T(128)S(6)} %select_n.31, s32[]{:T(128)S(6)} %select_n.30, s32[]{:T(128)S(6)} %select_n.29), kind=kLoop, calls=%fused_computation.3 | loop fusion | bytes 393228 | tf_op jit(solution)/shard_map/dynamic_slice | solution.py:326
  0.9 5.1 %collective-permute-start.2 = (f32[8,2048]{1,0:T(8,128)S(1)}, f32[8,2048]{1,0:T(8,128)S(1)}, u32[]{:S(2)}, u32[]{:S(2)}) collective-permute-start(f32[8,2048]{1,0:T(8,128)S(1)} %get-tuple-element.13), channel_id=1, source_target_pairs={{0,3},{1,2},{2,1},{3,0},{4,7},{5,6},{6,5},{7,4},{8,11},{9,10},{10,... | collective-permute-start | bytes 196616 | tf_op jit(solution)/shard_map/ppermute | solution.py:329
  6.0 0.0 collective-permute-start.1
  6.1 0.6 %collective-permute-start = (f32[8,2048]{1,0:T(8,128)S(1)}, f32[8,2048]{1,0:T(8,128)S(1)}, u32[]{:S(2)}, u32[]{:S(2)}) collective-permute-start(f32[8,2048]{1,0:T(8,128)S(1)} %get-tuple-element.15), channel_id=1, source_target_pairs={{0,1},{1,0},{2,3},{3,2},{4,5},{5,4},{6,7},{7,6},{8,9},{9,8},{10,11... | collective-permute-start | bytes 196616 | tf_op jit(solution)/shard_map/ppermute | solution.py:329
  6.7 1.9 %collective-permute-done.2.refs_3_ = f32[8,2048]{1,0:T(8,128)S(1)} collective-permute-done((f32[8,2048]{1,0:T(8,128)S(1)}, f32[8,2048]{1,0:T(8,128)S(1)}, u32[]{:S(2)}, u32[]{:S(2)}) %collective-permute-start.2) | collective-permute-done | bytes 65568 | tf_op jit(solution)/shard_map/ppermute | solution.py:329
  8.6 3.0 %collective-permute-done.1.refs_2_ = f32[8,2048]{1,0:T(8,128)S(1)} collective-permute-done((f32[8,2048]{1,0:T(8,128)S(1)}, f32[8,2048]{1,0:T(8,128)S(1)}, u32[]{:S(2)}, u32[]{:S(2)}) %collective-permute-start.1) | collective-permute-done | bytes 65568 | tf_op jit(solution)/shard_map/ppermute | solution.py:329
  11.7 0.0 collective-permute-done.refs_1_
  11.7 0.0 copy-start
  11.7 0.9 %copy-done = f32[32,2048]{1,0:T(8,128)S(1)} copy-done((f32[32,2048]{1,0:T(8,128)S(1)}, f32[32,2048]{1,0:T(8,128)}, u32[]{:S(2)}) %copy-start) | copy-done | bytes 262168
  12.6 0.0 copy-start.1
  12.6 0.7 %copy-done.1 = s32[32]{0:T(128)S(1)} copy-done((s32[32]{0:T(128)S(1)}, s32[32]{0:T(128)}, u32[]{:S(2)}) %copy-start.1) | copy-done | bytes 152
  13.3 0.0 copy-start.3
  13.3 0.9 %copy-done.3 = bf16[512,256]{1,0:T(8,128)(2,1)S(1)} copy-done((bf16[512,256]{1,0:T(8,128)(2,1)S(1)}, bf16[512,256]{1,0:T(8,128)(2,1)}, u32[]{:S(2)}) %copy-start.3) | copy-done | bytes 262168
  14.2 0.0 copy-start.4
  14.2 0.9 %copy-done.4 = bf16[512,256]{1,0:T(8,128)(2,1)S(1)} copy-done((bf16[512,256]{1,0:T(8,128)(2,1)S(1)}, bf16[512,256]{1,0:T(8,128)(2,1)}, u32[]{:S(2)}) %copy-start.4) | copy-done | bytes 262168
  15.2 0.0 copy-start.5
  15.2 0.8 %copy-done.5 = f32[32,256]{1,0:T(8,128)S(1)} copy-done((f32[32,256]{1,0:T(8,128)S(1)}, f32[32,256]{1,0:T(8,128)}, u32[]{:S(2)}) %copy-start.5) | copy-done | bytes 32792
  15.9 0.0 copy-start.6
  15.9 0.8 %copy-done.6 = f32[32,256]{1,0:T(8,128)S(1)} copy-done((f32[32,256]{1,0:T(8,128)S(1)}, f32[32,256]{1,0:T(8,128)}, u32[]{:S(2)}) %copy-start.6) | copy-done | bytes 32792
  16.7 0.0 copy-start.2
  16.7 1.2 %spectrum.1.refs_1_ = bf16[32,16,128]{2,1,0:T(8,128)(2,1)S(1)} custom-call(f32[32,2048]{1,0:T(8,128)S(1)} %copy-done, f32[8,2048]{1,0:T(8,128)S(1)} %collective-permute-done.refs_1_, f32[8,2048]{1,0:T(8,128)S(1)} %collective-permute-done.1.refs_2_, f32[8,2048]{1,0:T(8,128)S(1)} %collective-permute-done.2.refs_3_, s32[32]{0:T(128)S(1)} %copy-done.1, ...), custom_call_target="tpu_custom_call" | custom-call | flops 1000000000 | bytes 1000000 | tf_op jit(solution)/shard_map/spectrum/pallas_call | solution.py:166
  17.9 0.1 collective-permute-start.3
  17.9 0.0 copy-done.7
  18.0 1.3 %collective-permute-done.3 = bf16[32,16,128]{2,1,0:T(8,128)(2,1)S(1)} collective-permute-done((bf16[32,16,128]{2,1,0:T(8,128)(2,1)S(1)}, bf16[32,16,128]{2,1,0:T(8,128)(2,1)S(1)}, u32[]{:S(2)}, u32[]{:S(2)}) %collective-permute-start.3) | collective-permute-done | bytes 131104 | tf_op jit(solution)/shard_map/ppermute | solution.py:308
  19.3 0.1 broadcast_select_fusion
  19.4 1.6 %collective-permute-start.4 = (bf16[2,32,16,128]{3,2,1,0:T(8,128)(2,1)S(1)}, bf16[2,32,16,128]{3,2,1,0:T(8,128)(2,1)S(1)}, u32[]{:S(2)}, u32[]{:S(2)}) collective-permute-start(bf16[2,32,16,128]{3,2,1,0:T(8,128)(2,1)S(1)} %broadcast_select_fusion), channel_id=1, source_target_pairs={{0,8},{4,20},{8,0},{12,28},{16,24},{20,4},{24,16},{28,12},{1,9},{5... | collective-permute-start | bytes 786440 | tf_op jit(solution)/shard_map/ppermute | solution.py:314
  20.9 4.9 %collective-permute-done.4 = bf16[2,32,16,128]{3,2,1,0:T(8,128)(2,1)S(1)} collective-permute-done((bf16[2,32,16,128]{3,2,1,0:T(8,128)(2,1)S(1)}, bf16[2,32,16,128]{3,2,1,0:T(8,128)(2,1)S(1)}, u32[]{:S(2)}, u32[]{:S(2)}) %collective-permute-start.4) | collective-permute-done | bytes 262176 | tf_op jit(solution)/shard_map/ppermute | solution.py:314
  25.8 0.1 broadcast_select_fusion.1
  25.9 1.6 %collective-permute-start.5 = (bf16[2,32,16,128]{3,2,1,0:T(8,128)(2,1)S(1)}, bf16[2,32,16,128]{3,2,1,0:T(8,128)(2,1)S(1)}, u32[]{:S(2)}, u32[]{:S(2)}) collective-permute-start(bf16[2,32,16,128]{3,2,1,0:T(8,128)(2,1)S(1)} %broadcast_select_fusion.1), channel_id=1, source_target_pairs={{0,16},{4,12},{8,24},{12,4},{16,0},{20,28},{24,8},{28,20},{1,17},{... | collective-permute-start | bytes 786440 | tf_op jit(solution)/shard_map/ppermute | solution.py:314
  27.5 2.7 %collective-permute-start.8 = (bf16[32,16,128]{2,1,0:T(8,128)(2,1)S(1)}, bf16[32,16,128]{2,1,0:T(8,128)(2,1)S(1)}, u32[]{:S(2)}, u32[]{:S(2)}) collective-permute-start(bf16[32,16,128]{2,1,0:T(8,128)(2,1)S(1)} %spectrum.1.refs_1_), channel_id=1, source_target_pairs={{0,3},{1,2},{2,1},{3,0},{4,7},{5,6},{6,5},{7,4},{8,11},{9,10},{10,... | collective-permute-start | bytes 393224 | tf_op jit(solution)/shard_map/ppermute | solution.py:334
  30.2 0.0 collective-permute-start.7
  30.2 1.7 %collective-permute-start.6 = (bf16[32,16,128]{2,1,0:T(8,128)(2,1)S(1)}, bf16[32,16,128]{2,1,0:T(8,128)(2,1)S(1)}, u32[]{:S(2)}, u32[]{:S(2)}) collective-permute-start(bf16[32,16,128]{2,1,0:T(8,128)(2,1)S(1)} %spectrum.1.refs_1_), channel_id=1, source_target_pairs={{0,1},{1,0},{2,3},{3,2},{4,5},{5,4},{6,7},{7,6},{8,9},{9,8},{10,11... | collective-permute-start | bytes 393224 | tf_op jit(solution)/shard_map/ppermute | solution.py:334
  31.9 0.5 collective-permute-done.5
  32.4 0.1 broadcast_select_fusion.2.refs_0_
  32.4 3.3 %collective-permute-done.8.refs_4_ = bf16[32,16,128]{2,1,0:T(8,128)(2,1)S(1)} collective-permute-done((bf16[32,16,128]{2,1,0:T(8,128)(2,1)S(1)}, bf16[32,16,128]{2,1,0:T(8,128)(2,1)S(1)}, u32[]{:S(2)}, u32[]{:S(2)}) %collective-permute-start.8) | collective-permute-done | bytes 131104 | tf_op jit(solution)/shard_map/ppermute | solution.py:334
  35.7 5.1 %collective-permute-done.7.refs_3_ = bf16[32,16,128]{2,1,0:T(8,128)(2,1)S(1)} collective-permute-done((bf16[32,16,128]{2,1,0:T(8,128)(2,1)S(1)}, bf16[32,16,128]{2,1,0:T(8,128)(2,1)S(1)}, u32[]{:S(2)}, u32[]{:S(2)}) %collective-permute-start.7) | collective-permute-done | bytes 131104 | tf_op jit(solution)/shard_map/ppermute | solution.py:334
  40.8 0.0 collective-permute-done.6.refs_2_
  40.8 0.0 copy-done.2
  40.8 5.6 %correlate.1 = (f32[128,128]{1,0:T(8,128)S(1)}, f32[128,128]{1,0:T(8,128)S(1)}, f32[128,128]{1,0:T(8,128)S(1)}, f32[128,128]{1,0:T(8,128)S(1)}) custom-call(bf16[2,32,16,128]{3,2,1,0:T(8,128)(2,1)S(1)} %broadcast_select_fusion.2.refs_0_, bf16[32,16,128]{2,1,0:T(8,128)(2,1)S(1)} %spectrum.1.refs_1_, bf16[32,16,128]{2,1,0:T(8,128)(2,1)S(1)} %collective-permute-done.6.refs_2_, ...), custom_call_target="tpu_custom_call" | custom-call | flops 4000000000 | bytes 3000000 | tf_op jit(solution)/shard_map/correlate/pallas_call | solution.py:244
  46.4 0.1 collective-permute-start.9
  46.5 3.1 %collective-permute-start.10 = (f32[128,128]{1,0:T(8,128)S(1)}, f32[128,128]{1,0:T(8,128)S(1)}, u32[]{:S(2)}, u32[]{:S(2)}) collective-permute-start(f32[128,128]{1,0:T(8,128)S(1)} %get-tuple-element.11), channel_id=1, source_target_pairs={{0,2},{1,3},{2,0},{3,1},{4,6},{5,7},{6,4},{7,5},{8,10},{9,11},{10,... | collective-permute-start | bytes 196616 | tf_op jit(solution)/shard_map/ppermute | solution.py:338
  49.6 1.3 %collective-permute-start.11 = (f32[128,128]{1,0:T(8,128)S(1)}, f32[128,128]{1,0:T(8,128)S(1)}, u32[]{:S(2)}, u32[]{:S(2)}) collective-permute-start(f32[128,128]{1,0:T(8,128)S(1)} %get-tuple-element.12), channel_id=1, source_target_pairs={{0,3},{1,2},{2,1},{3,0},{4,7},{5,6},{6,5},{7,4},{8,11},{9,10},{10,... | collective-permute-start | bytes 196616 | tf_op jit(solution)/shard_map/ppermute | solution.py:338
  50.9 0.0 collective-permute-done.9.refs_1_
  50.9 1.0 %collective-permute-done.10.refs_2_ = f32[128,128]{1,0:T(8,128)S(1)} collective-permute-done((f32[128,128]{1,0:T(8,128)S(1)}, f32[128,128]{1,0:T(8,128)S(1)}, u32[]{:S(2)}, u32[]{:S(2)}) %collective-permute-start.10) | collective-permute-done | bytes 65568 | tf_op jit(solution)/shard_map/ppermute | solution.py:338
  51.8 3.8 %collective-permute-done.11.refs_3_ = f32[128,128]{1,0:T(8,128)S(1)} collective-permute-done((f32[128,128]{1,0:T(8,128)S(1)}, f32[128,128]{1,0:T(8,128)S(1)}, u32[]{:S(2)}, u32[]{:S(2)}) %collective-permute-start.11) | collective-permute-done | bytes 65568 | tf_op jit(solution)/shard_map/ppermute | solution.py:338
  55.6 1.2 %place.1 = f32[2,32,32,32]{3,2,1,0:T(8,128)} custom-call(f32[128,128]{1,0:T(8,128)S(1)} %get-tuple-element.9.refs_0_, f32[128,128]{1,0:T(8,128)S(1)} %collective-permute-done.9.refs_1_, f32[128,128]{1,0:T(8,128)S(1)} %collective-permute-done.10.refs_2_, f32[128,128]{1,0:T(8,128)S(1)} %collective-permute-done.11.refs_3_), custom_call_target="tpu_custom_call" | custom-call | tf_op jit(solution)/shard_map/place/pallas_call | solution.py:284
  (1 shorter events, 0.0 us)
Async XLA Ops:
  0.0 17.9 %copy-start.7 = (s32[2]{0:T(128)S(1)}, s32[2]{0:T(128)}, u32[]{:S(2)}) copy-start(s32[2]{0:T(128)} %param.10) | copy-start | bytes 28
  0.9 7.7 %collective-permute-start.2 = (f32[8,2048]{1,0:T(8,128)S(1)}, f32[8,2048]{1,0:T(8,128)S(1)}, u32[]{:S(2)}, u32[]{:S(2)}) collective-permute-start(f32[8,2048]{1,0:T(8,128)S(1)} %get-tuple-element.13), channel_id=1, source_target_pairs={{0,3},{1,2},{2,1},{3,0},{4,7},{5,6},{6,5},{7,4},{8,11},{9,10},{10,... | collective-permute-start | bytes 196616 | tf_op jit(solution)/shard_map/ppermute | solution.py:329
  6.0 5.6 %collective-permute-start.1 = (f32[8,2048]{1,0:T(8,128)S(1)}, f32[8,2048]{1,0:T(8,128)S(1)}, u32[]{:S(2)}, u32[]{:S(2)}) collective-permute-start(f32[8,2048]{1,0:T(8,128)S(1)} %get-tuple-element.14), channel_id=1, source_target_pairs={{0,2},{1,3},{2,0},{3,1},{4,6},{5,7},{6,4},{7,5},{8,10},{9,11},{10,... | collective-permute-start | bytes 196616 | tf_op jit(solution)/shard_map/ppermute | solution.py:329
  6.1 5.6 %collective-permute-start = (f32[8,2048]{1,0:T(8,128)S(1)}, f32[8,2048]{1,0:T(8,128)S(1)}, u32[]{:S(2)}, u32[]{:S(2)}) collective-permute-start(f32[8,2048]{1,0:T(8,128)S(1)} %get-tuple-element.15), channel_id=1, source_target_pairs={{0,1},{1,0},{2,3},{3,2},{4,5},{5,4},{6,7},{7,6},{8,9},{9,8},{10,11... | collective-permute-start | bytes 196616 | tf_op jit(solution)/shard_map/ppermute | solution.py:329
  11.7 1.0 %copy-start = (f32[32,2048]{1,0:T(8,128)S(1)}, f32[32,2048]{1,0:T(8,128)}, u32[]{:S(2)}) copy-start(f32[32,2048]{1,0:T(8,128)} %refs_0_.1) | copy-start | bytes 786436
  12.6 0.7 %copy-start.1 = (s32[32]{0:T(128)S(1)}, s32[32]{0:T(128)}, u32[]{:S(2)}) copy-start(s32[32]{0:T(128)} %refs_4_.1) | copy-start | bytes 388
  13.3 0.9 %copy-start.3 = (bf16[512,256]{1,0:T(8,128)(2,1)S(1)}, bf16[512,256]{1,0:T(8,128)(2,1)}, u32[]{:S(2)}) copy-start(bf16[512,256]{1,0:T(8,128)(2,1)} %constant.41.clone.refs_8_) | copy-start | bytes 786436
  14.2 0.9 %copy-start.4 = (bf16[512,256]{1,0:T(8,128)(2,1)S(1)}, bf16[512,256]{1,0:T(8,128)(2,1)}, u32[]{:S(2)}) copy-start(bf16[512,256]{1,0:T(8,128)(2,1)} %constant.40.clone.refs_7_) | copy-start | bytes 786436
  15.2 0.8 %copy-start.5 = (f32[32,256]{1,0:T(8,128)S(1)}, f32[32,256]{1,0:T(8,128)}, u32[]{:S(2)}) copy-start(f32[32,256]{1,0:T(8,128)} %constant.39.clone.refs_6_) | copy-start | bytes 98308
  15.9 0.8 %copy-start.6 = (f32[32,256]{1,0:T(8,128)S(1)}, f32[32,256]{1,0:T(8,128)}, u32[]{:S(2)}) copy-start(f32[32,256]{1,0:T(8,128)} %constant.38.clone.refs_5_) | copy-start | bytes 98308
  16.7 24.2 %copy-start.2 = (bf16[8192,128]{1,0:T(8,128)(2,1)S(1)}, bf16[8192,128]{1,0:T(8,128)(2,1)}, u32[]{:S(2)}) copy-start(bf16[8192,128]{1,0:T(8,128)(2,1)} %constant.42.clone.refs_5_) | copy-start | bytes 6291460
  17.9 1.4 %collective-permute-start.3 = (bf16[32,16,128]{2,1,0:T(8,128)(2,1)S(1)}, bf16[32,16,128]{2,1,0:T(8,128)(2,1)S(1)}, u32[]{:S(2)}, u32[]{:S(2)}) collective-permute-start(bf16[32,16,128]{2,1,0:T(8,128)(2,1)S(1)} %spectrum.1.refs_1_), channel_id=1, source_target_pairs={{0,4},{4,0},{8,12},{12,8},{16,20},{20,16},{24,28},{28,24},{1,5},{5... | collective-permute-start | bytes 393224 | tf_op jit(solution)/shard_map/ppermute | solution.py:308
  19.4 6.4 %collective-permute-start.4 = (bf16[2,32,16,128]{3,2,1,0:T(8,128)(2,1)S(1)}, bf16[2,32,16,128]{3,2,1,0:T(8,128)(2,1)S(1)}, u32[]{:S(2)}, u32[]{:S(2)}) collective-permute-start(bf16[2,32,16,128]{3,2,1,0:T(8,128)(2,1)S(1)} %broadcast_select_fusion), channel_id=1, source_target_pairs={{0,8},{4,20},{8,0},{12,28},{16,24},{20,4},{24,16},{28,12},{1,9},{5... | collective-permute-start | bytes 786440 | tf_op jit(solution)/shard_map/ppermute | solution.py:314
  25.9 6.4 %collective-permute-start.5 = (bf16[2,32,16,128]{3,2,1,0:T(8,128)(2,1)S(1)}, bf16[2,32,16,128]{3,2,1,0:T(8,128)(2,1)S(1)}, u32[]{:S(2)}, u32[]{:S(2)}) collective-permute-start(bf16[2,32,16,128]{3,2,1,0:T(8,128)(2,1)S(1)} %broadcast_select_fusion.1), channel_id=1, source_target_pairs={{0,16},{4,12},{8,24},{12,4},{16,0},{20,28},{24,8},{28,20},{1,17},{... | collective-permute-start | bytes 786440 | tf_op jit(solution)/shard_map/ppermute | solution.py:314
  27.5 8.2 %collective-permute-start.8 = (bf16[32,16,128]{2,1,0:T(8,128)(2,1)S(1)}, bf16[32,16,128]{2,1,0:T(8,128)(2,1)S(1)}, u32[]{:S(2)}, u32[]{:S(2)}) collective-permute-start(bf16[32,16,128]{2,1,0:T(8,128)(2,1)S(1)} %spectrum.1.refs_1_), channel_id=1, source_target_pairs={{0,3},{1,2},{2,1},{3,0},{4,7},{5,6},{6,5},{7,4},{8,11},{9,10},{10,... | collective-permute-start | bytes 393224 | tf_op jit(solution)/shard_map/ppermute | solution.py:334
  30.2 10.6 %collective-permute-start.7 = (bf16[32,16,128]{2,1,0:T(8,128)(2,1)S(1)}, bf16[32,16,128]{2,1,0:T(8,128)(2,1)S(1)}, u32[]{:S(2)}, u32[]{:S(2)}) collective-permute-start(bf16[32,16,128]{2,1,0:T(8,128)(2,1)S(1)} %spectrum.1.refs_1_), channel_id=1, source_target_pairs={{0,2},{1,3},{2,0},{3,1},{4,6},{5,7},{6,4},{7,5},{8,10},{9,11},{10,... | collective-permute-start | bytes 393224 | tf_op jit(solution)/shard_map/ppermute | solution.py:334
  30.2 10.6 %collective-permute-start.6 = (bf16[32,16,128]{2,1,0:T(8,128)(2,1)S(1)}, bf16[32,16,128]{2,1,0:T(8,128)(2,1)S(1)}, u32[]{:S(2)}, u32[]{:S(2)}) collective-permute-start(bf16[32,16,128]{2,1,0:T(8,128)(2,1)S(1)} %spectrum.1.refs_1_), channel_id=1, source_target_pairs={{0,1},{1,0},{2,3},{3,2},{4,5},{5,4},{6,7},{7,6},{8,9},{9,8},{10,11... | collective-permute-start | bytes 393224 | tf_op jit(solution)/shard_map/ppermute | solution.py:334
  46.4 4.5 %collective-permute-start.9 = (f32[128,128]{1,0:T(8,128)S(1)}, f32[128,128]{1,0:T(8,128)S(1)}, u32[]{:S(2)}, u32[]{:S(2)}) collective-permute-start(f32[128,128]{1,0:T(8,128)S(1)} %get-tuple-element.10), channel_id=1, source_target_pairs={{0,1},{1,0},{2,3},{3,2},{4,5},{5,4},{6,7},{7,6},{8,9},{9,8},{10,11... | collective-permute-start | bytes 196616 | tf_op jit(solution)/shard_map/ppermute | solution.py:338
  46.5 5.3 %collective-permute-start.10 = (f32[128,128]{1,0:T(8,128)S(1)}, f32[128,128]{1,0:T(8,128)S(1)}, u32[]{:S(2)}, u32[]{:S(2)}) collective-permute-start(f32[128,128]{1,0:T(8,128)S(1)} %get-tuple-element.11), channel_id=1, source_target_pairs={{0,2},{1,3},{2,0},{3,1},{4,6},{5,7},{6,4},{7,5},{8,10},{9,11},{10,... | collective-permute-start | bytes 196616 | tf_op jit(solution)/shard_map/ppermute | solution.py:338
  49.6 6.1 %collective-permute-start.11 = (f32[128,128]{1,0:T(8,128)S(1)}, f32[128,128]{1,0:T(8,128)S(1)}, u32[]{:S(2)}, u32[]{:S(2)}) collective-permute-start(f32[128,128]{1,0:T(8,128)S(1)} %get-tuple-element.12), channel_id=1, source_target_pairs={{0,3},{1,2},{2,1},{3,0},{4,7},{5,6},{6,5},{7,4},{8,11},{9,10},{10,... | collective-permute-start | bytes 196616 | tf_op jit(solution)/shard_map/ppermute | solution.py:338

commit v2 on v1

--- a/solution.py
+++ b/solution.py
@@ -26,18 +26,12 @@
     return high, low
 
 
-def twiddle_tables():
-    angle = 2.0 * np.pi * (np.outer(np.arange(N1), np.arange(N2)) % NT) / NT
-    return np.cos(angle).astype(np.float32), np.sin(angle).astype(np.float32)
-
-
-def column_tables():
+def fft_tables():
+    twiddle = 2.0 * np.pi * (np.outer(np.arange(N1), np.arange(N2)) % NT) / NT
     angle = 2.0 * np.pi * (np.outer(np.arange(N2), np.arange(K2)) % N2) / N2
     cos, sin = np.cos(angle), np.sin(angle)
-    table = np.block([[cos, -sin], [sin, cos]])
-    high = table.astype(jnp.bfloat16)
-    low = (table - high.astype(np.float64)).astype(jnp.bfloat16)
-    return high, low
+    columns = np.block([[cos, -sin], [sin, cos]])
+    return np.concatenate([np.cos(twiddle), np.sin(twiddle), columns]).astype(np.float32)
 
 
 def lag_table():
@@ -87,16 +81,14 @@
     return out
 
 
-def spectrum_kernel(
-    tparts, samples, *rest
-):
-    blocks = rest[: tparts - 1]
-    mask, cos, sin, high, low, out, series, rows, spec = rest[tparts - 1 :]
+def spectrum_kernel(tparts, *rest):
+    blocks = rest[:tparts]
+    alive, tables, out, series, rows, spec, high, low = rest[tparts:]
     me = lax.axis_index("ta")
     channels = out.shape[1] // 2
-    series[me] = samples[pl.ds(pl.multiple_of(me * channels, channels), channels), :]
-    for step in range(1, tparts):
-        series[me ^ step] = blocks[step - 1][...]
+    for step in range(tparts):
+        series[me ^ step] = blocks[step][...]
+    high[...], low[...] = split_bf16(tables[2 * N1 :, :])
     per_part = N1 // tparts
     for start in range(0, N2, 128):
         lanes = slice(start, start + 128)
@@ -110,7 +102,7 @@
             else:
                 re, im = bins[N1 - k1]
                 im = -im
-            c, s = cos[k1 : k1 + 1, lanes], sin[k1 : k1 + 1, lanes]
+            c, s = tables[k1 : k1 + 1, lanes], tables[N1 + k1 : N1 + k1 + 1, lanes]
             if im is None:
                 new = re * c, -re * s
             else:
@@ -141,45 +133,40 @@
         suffix[k1] = running
     column = running
     lane = lax.broadcasted_iota(jnp.int32, (channels, K2), 1)
-    row = lax.broadcasted_iota(jnp.int32, (channels, K2), 0)
-    alive = jnp.zeros((channels, K2), jnp.float32)
-    for c in range(channels):
-        alive = jnp.where(row == c, mask[me * channels + c].astype(jnp.float32), alive)
     prefix = None
     for k1 in range(N1):
         prefix = add(prefix, amplitude[k1])
         above = jnp.where(lane == K2 - 1, 0.0, pltpu.roll(prefix, K2 - 1, 1))
         below = jnp.where(lane == 0, 0.0, pltpu.roll(suffix[k1], 1, 1))
         divisor = (column + above + below) / (2 * W + 1) + EPS
-        scale = alive / divisor
+        scale = alive[...] / divisor
         re, im = parts(k1)
         out[k1] = jnp.concatenate([re * scale, im * scale], axis=0).astype(jnp.bfloat16)
 
 
-def spectrum(samples, blocks, dead_mask):
+def spectrum(blocks, alive, tables):
     tparts = lax.axis_size("ta")
-    channels = samples.shape[0] // tparts
-    cos, sin = twiddle_tables()
-    high, low = column_tables()
+    channels, time_rows = blocks[0].shape
     vmem = pl.BlockSpec(memory_space=pltpu.VMEM)
-    smem = pl.BlockSpec(memory_space=pltpu.SMEM)
     return pl.pallas_call(
         lambda *refs: spectrum_kernel(tparts, *refs),
         out_shape=jax.ShapeDtypeStruct((N1, 2 * channels, K2), jnp.bfloat16),
-        in_specs=[vmem] * tparts + [smem] + [vmem] * 4,
+        in_specs=[vmem] * (tparts + 2),
         out_specs=vmem,
         scratch_shapes=[
-            pltpu.VMEM((tparts, channels, samples.shape[1]), jnp.float32),
+            pltpu.VMEM((tparts, channels, time_rows), jnp.float32),
             pltpu.VMEM((N1 * channels, 2 * N2), jnp.float32),
             pltpu.VMEM((N1 * channels, 2 * K2), jnp.float32),
+            pltpu.VMEM((2 * N2, 2 * K2), jnp.bfloat16),
+            pltpu.VMEM((2 * N2, 2 * K2), jnp.bfloat16),
         ],
         compiler_params=pltpu.CompilerParams(vmem_limit_bytes=32 * 1024 * 1024),
         cost_estimate=pl.CostEstimate(flops=10**9, bytes_accessed=10**6, transcendentals=10**5),
         name="spectrum",
-    )(samples, *blocks, dead_mask, cos, sin, high, low)
-
-
-GROUP = 4
+    )(*blocks, alive, tables)
+
+
+GROUP = 8
 
 
 def correlate_kernel(tparts, panels, *rest):
@@ -198,20 +185,19 @@
         for sub_index in range(GROUP):
             k1 = group * GROUP + sub_index
             col = sub_index * 2 * K2
-            res = [r[k1].astype(jnp.float32) for r in residents]
+            halves = [r[k1].astype(jnp.float32) for r in residents]
+            re = jnp.concatenate([v[:channels] for v in halves], axis=0).astype(jnp.bfloat16)
+            im = jnp.concatenate([v[channels:] for v in halves], axis=0).astype(jnp.bfloat16)
             for s in range(steps):
                 panel = panels[s, k1].astype(jnp.float32)
                 for i in range(channels):
-                    a = jnp.broadcast_to(panel[i : i + 1, :], (channels, K2))
-                    b = jnp.broadcast_to(panel[channels + i : channels + i + 1, :], (channels, K2))
-                    re, im = [], []
-                    for value in res:
-                        c, d = value[:channels], value[channels:]
-                        re.append(a * c + b * d)
-                        im.append(a * d - b * c)
+                    a = jnp.broadcast_to(panel[i : i + 1, :], (local, K2)).astype(jnp.bfloat16)
+                    b = jnp.broadcast_to(
+                        panel[channels + i : channels + i + 1, :], (local, K2)
+                    ).astype(jnp.bfloat16)
                     at = pl.ds((s * channels + i) * local, local)
-                    cross[at, pl.ds(col, K2)] = jnp.concatenate(re, axis=0).astype(jnp.bfloat16)
-                    cross[at, pl.ds(col + K2, K2)] = jnp.concatenate(im, axis=0).astype(jnp.bfloat16)
+                    cross[at, pl.ds(col, K2)] = a * re + b * im
+                    cross[at, pl.ds(col + K2, K2)] = a * im - b * re
         depth = GROUP * 2 * K2
         total[...] += jnp.dot(
             cross[...],
@@ -221,18 +207,22 @@
 
     width = LAGS // tparts
     lane = lax.broadcasted_iota(jnp.int32, (channels, LAGS), 1) // width
-    for source in range(steps * channels):
-        pieces = [
-            total[source * local + step * channels : source * local + (step + 1) * channels, :]
-            for step in range(tparts)
-        ]
+    for source in range(0, steps * channels, 2):
         for far in range(tparts):
             dest = me ^ far
-            value = None
-            for step in range(tparts):
-                moved = pltpu.roll(pieces[step], (step - dest + tparts) * width % LAGS, 1)
-                value = moved if value is None else jnp.where(lane == step, moved, value)
-            outs[far][source * channels : (source + 1) * channels, :] = value.astype(outs[far].dtype)
+            pair = []
+            for first in (source * local, (source + 1) * local):
+                value = None
+                for step in range(tparts):
+                    at = first + step * channels
+                    moved = pltpu.roll(
+                        total[at : at + channels, :], (step - dest + tparts) * width % LAGS, 1
+                    )
+                    value = moved if value is None else jnp.where(lane == step, moved, value)
+                pair.append(value)
+            outs[far][source * channels : (source + 2) * channels, :] = jnp.concatenate(
+                pair, axis=0
+            ).astype(outs[far].dtype)
 
 
 def correlate(panels, residents):
@@ -244,7 +234,7 @@
     return pl.pallas_call(
         lambda *refs: correlate_kernel(tparts, *refs),
         out_shape=[
-            jax.ShapeDtypeStruct((steps * channels * channels, LAGS), jnp.float32)
+            jax.ShapeDtypeStruct((steps * channels * channels, LAGS), jnp.bfloat16)
         ] * tparts,
         in_specs=[vmem] * (tparts + 2),
         out_specs=[vmem] * tparts,
@@ -295,25 +285,34 @@
     return [(i, i ^ mask) for i in range(lax.axis_size(axis))]
 
 
-def owner_panels(block, owners):
-    count = lax.axis_size("ch")
+def exchange(block, owners):
+    count, tparts = lax.axis_size("ch"), lax.axis_size("ta")
     steps = owners.shape[0]
-    if count & (count - 1):
-        return jnp.take(lax.all_gather(block, "ch"), owners, axis=0)
     me = lax.axis_index("ch")
-    if count == 1:
-        return jnp.stack([block] * steps)
-    away = owners ^ me
-    shape = (steps,) + (1,) * block.ndim
-    other = lax.ppermute(block, "ch", flip("ch", 1))
-    held = jnp.where(((away & 1) != 0).reshape(shape), other[None], block[None])
-    masks = [1 << bit for bit in range(1, count.bit_length() - 1)]
-    for even, odd in zip(masks, reversed(masks)):
-        perm = [(i, i ^ (odd if i & 1 else even)) for i in range(count)]
-        mask = jnp.where(me & 1, odd, even)
-        other = lax.ppermute(held, "ch", perm)
-        held = jnp.where(((away & mask) != 0).reshape(shape), other, held)
-    return held
+    odd = (me & 1) != 0
+    if count & (count - 1) or count < 8 or tparts != 4:
+        residents = [lax.ppermute(block, "ta", flip("ta", far)) for far in range(1, tparts)]
+        return jnp.take(lax.all_gather(block, "ch"), owners, axis=0), residents
+    away = (owners ^ me).reshape((steps,) + (1,) * block.ndim)
+    held = jnp.broadcast_to(block[None], (steps,) + block.shape)
+    residents = [None] * (tparts - 1)
+    for far, mask in ((3, 6), (2, 4), (1, 2)):
+        got = []
+        for parity in (0, 1):
+            perm = []
+            for ch in range(count):
+                for ta in range(tparts):
+                    if ch & 1 == parity:
+                        perm.append((ch * tparts + ta, ch * tparts + (ta ^ far)))
+                    else:
+                        perm.append((ch * tparts + ta, (ch ^ mask) * tparts + ta))
+            got.append(lax.ppermute(block, ("ch", "ta"), perm))
+        residents[far - 1] = jnp.where(odd, got[1], got[0])
+        held = jnp.where((away & 6) == mask, jnp.where(odd, got[0], got[1])[None], held)
+    for bit in [*range(3, count.bit_length() - 1), 0]:
+        other = lax.ppermute(held, "ch", flip("ch", 1 << bit))
+        held = jnp.where((away & (1 << bit)) != 0, other, held)
+    return held, residents
 
 
 def body(samples, dead_mask, owners):
@@ -321,19 +320,19 @@
     me = lax.axis_index("ta")
     channels = samples.shape[0] // tparts
     steps = owners.shape[0]
-
-    def rows_for(part):
-        return lax.dynamic_slice_in_dim(samples, part * channels, channels, 0)
-
-    blocks = [
-        lax.ppermute(rows_for(me ^ far), "ta", flip("ta", far)) for far in range(1, tparts)
+    own = [
+        lax.dynamic_slice_in_dim(samples, (me ^ far) * channels, channels, 0)
+        for far in range(tparts)
     ]
-    whitened = spectrum(samples, blocks, dead_mask)
-    panels = owner_panels(whitened, owners)
-    residents = [whitened] + [
-        lax.ppermute(whitened, "ta", flip("ta", far)) for far in range(1, tparts)
+    blocks = [own[0]] + [
+        lax.ppermute(own[far], "ta", flip("ta", far)) for far in range(1, tparts)
     ]
-    pieces = correlate(panels, residents)
+    mask = lax.dynamic_slice_in_dim(dead_mask, me * channels, channels, 0)
+    alive = jnp.broadcast_to(mask.astype(jnp.float32)[:, None], (channels, K2))
+    tables = jnp.asarray(fft_tables()) * lax.optimization_barrier(jnp.float32(1))
+    whitened = spectrum(blocks, alive, tables)
+    panels, others = exchange(whitened, owners)
+    pieces = correlate(panels, [whitened] + others)
     pieces = [pieces[0]] + [
         lax.ppermute(pieces[far], "ta", flip("ta", far)) for far in range(1, tparts)
     ]

time: 57.3 us -> 42 us (0.73)
  waiting for transfers between devices: 24.8 us -> 15.7 us
  local copies, waits for them, and re-layouts: 5.96 us -> 1.03 us
  Pallas kernels: 7.98 us -> 5.29 us
  other arithmetic: 0.29 us -> 2.16 us
    ppermute x9 -> x10, waiting for transfers between devices: 20 us -> 11.9 us  [the longest x6 7.25 us: exchange(): got.append(lax.ppermute(block, ('ch', 'ta'), perm))]
    unnamed x16 -> x4, local copies, waits for them, and re-layouts: 5.03 us -> 0.01 us
    pallas_call x1, Pallas kernels: 5.56 us -> 3.49 us  [correlate(): pl.pallas_call(lambda *refs: correlate_kernel(tparts, *refs), out_shape=[...]
    mul x0 -> x1, other arithmetic: none -> 1.1 us  [body(): jnp.asarray(fft_tables()) * lax.optimization_barrier(jnp.float32(1))]
    ppermute x3, waiting for transfers between devices: 4.76 us -> 3.75 us  [body(): lax.ppermute(pieces[far], 'ta', flip('ta', far))]
    convert_element_type x0 -> x1, other arithmetic: none -> 0.74 us  [body(): alive = jnp.broadcast_to(mask.astype(jnp.float32)[:, None], (channels, K2))]
    ppermute x9 -> x10, starting transfers between devices: 13.4 us -> 13.1 us  [the longest x6 7.24 us: exchange(): got.append(lax.ppermute(block, ('ch', 'ta'), perm))]
  transfers between devices with their start and end apart: 12 -> 13, of which waited for: 9 -> 9; matrix products, arithmetic and copies ran while one was open for 0% -> 5% of each run, Pallas kernels for 0% -> 0%
where the time goes in v2:
time: 42 us; the launch traced here: 41.8 us
  starting transfers between devices  17.5 us (42%)
  waiting for transfers between devices  15.7 us (37%)
  Pallas kernels  5.29 us (13%)
  other arithmetic  2.16 us (5%)
  local copies, waits for them, and re-layouts  1.03 us (2%)
    ppermute x6, waiting for transfers between devices, exchange(): got.append(lax.ppermute(block, ('ch', 'ta'), perm))  7.25 us
    ppermute x6, starting transfers between devices, exchange(): got.append(lax.ppermute(block, ('ch', 'ta'), perm))  7.24 us
    ppermute x3, starting transfers between devices, body(): lax.ppermute(own[far], 'ta', flip('ta', far))  5.76 us
    ppermute x3, starting transfers between devices, body(): lax.ppermute(pieces[far], 'ta', flip('ta', far))  4.44 us
    ppermute x3, waiting for transfers between devices, body(): lax.ppermute(pieces[far], 'ta', flip('ta', far))  3.75 us
    pallas_call x1, Pallas kernels, correlate(): pl.pallas_call(lambda *refs: correlate_kernel(tparts, *refs), out_shape=[...  3.49 us
    ppermute x3, waiting for transfers between devices, body(): lax.ppermute(own[far], 'ta', flip('ta', far))  3.13 us
    ppermute x1, waiting for transfers between devices, exchange(): other = lax.ppermute(held, 'ch', flip('ch', 1 << bit))  1.52 us
  transfers between devices with their start and end apart: 13, of which 9 were waited for; matrix products, arithmetic and copies ran while one was open for 5% of the time, Pallas kernels for 0%

profile of v2, /device:TPU:0, one launch (start us, length us, event | category | flops | bytes accessed | tf_op | source)
XLA Modules:
  0.0 41.8 jit_solution(16604808986881539170)
XLA Ops:
  0.0 1.0 %constant_dynamic-slice_fusion = (f32[8,2048]{1,0:T(8,128)S(1)}, f32[8,2048]{1,0:T(8,128)S(1)}, f32[8,2048]{1,0:T(8,128)S(1)}, f32[8,2048]{1,0:T(8,128)S(1)}) fusion(f32[32,2048]{1,0:T(8,128)} %param.5, s32[]{:T(128)S(6)} %select_n.59, s32[]{:T(128)S(6)} %select_n.57, s32[]{:T(128)S(6)} %select_n.56, s32[]{:T(128)S(6)} %select_n.58), kind=kLoop, calls=%fused_computation.9 | loop fusion | bytes 524304 | tf_op jit(solution)/shard_map/dynamic_slice | solution.py:324
  1.0 5.1 %collective-permute-start.2 = (f32[8,2048]{1,0:T(8,128)S(1)}, f32[8,2048]{1,0:T(8,128)S(1)}, u32[]{:S(2)}, u32[]{:S(2)}) collective-permute-start(f32[8,2048]{1,0:T(8,128)S(1)} %get-tuple-element.19), channel_id=1, source_target_pairs={{0,3},{1,2},{2,1},{3,0},{4,7},{5,6},{6,5},{7,4},{8,11},{9,10},{10,... | collective-permute-start | bytes 196616 | tf_op jit(solution)/shard_map/ppermute | solution.py:328
  6.1 0.0 collective-permute-start
  6.1 0.6 %collective-permute-start.1 = (f32[8,2048]{1,0:T(8,128)S(1)}, f32[8,2048]{1,0:T(8,128)S(1)}, u32[]{:S(2)}, u32[]{:S(2)}) collective-permute-start(f32[8,2048]{1,0:T(8,128)S(1)} %get-tuple-element.22), channel_id=1, source_target_pairs={{0,2},{1,3},{2,0},{3,1},{4,6},{5,7},{6,4},{7,5},{8,10},{9,11},{10,... | collective-permute-start | bytes 196616 | tf_op jit(solution)/shard_map/ppermute | solution.py:328
  6.7 1.1 %broadcast_multiply_fusion.refs_5_ = f32[576,256]{1,0:T(8,128)S(1)} fusion(f32[576,256]{1,0:T(8,128)} %constant.34.clone, f32[]{:T(128)} %constant.12.clone.1), kind=kLoop, calls=%fused_computation | loop fusion | flops 147456 | bytes 1179652 | tf_op jit(solution)/shard_map/mul | solution.py:332
  7.8 0.0 copy-start.1
  7.8 0.7 %dynamic-slice_convert_fusion = f32[8]{0:T(128)S(1)} fusion(s32[32]{0:T(128)} %param.6, s32[]{:T(128)S(6)} %select_n.56), kind=kLoop, calls=%fused_computation.13 | loop fusion | flops 8 | bytes 68 | tf_op jit(solution)/shard_map/convert_element_type | solution.py:331
  8.6 0.4 collective-permute-done.2.refs_3_
  9.0 1.8 %collective-permute-done.refs_1_ = f32[8,2048]{1,0:T(8,128)S(1)} collective-permute-done((f32[8,2048]{1,0:T(8,128)S(1)}, f32[8,2048]{1,0:T(8,128)S(1)}, u32[]{:S(2)}, u32[]{:S(2)}) %collective-permute-start) | collective-permute-done | bytes 65568 | tf_op jit(solution)/shard_map/ppermute | solution.py:328
  10.7 1.0 %collective-permute-done.1.refs_2_ = f32[8,2048]{1,0:T(8,128)S(1)} collective-permute-done((f32[8,2048]{1,0:T(8,128)S(1)}, f32[8,2048]{1,0:T(8,128)S(1)}, u32[]{:S(2)}, u32[]{:S(2)}) %collective-permute-start.1) | collective-permute-done | bytes 65568 | tf_op jit(solution)/shard_map/ppermute | solution.py:328
  11.7 0.1 broadcast_in_dim.61.refs_4_
  11.8 0.6 %spectrum.1.refs_1_ = bf16[32,16,128]{2,1,0:T(8,128)(2,1)S(1)} custom-call(f32[8,2048]{1,0:T(8,128)S(1)} %get-tuple-element.21.refs_0_, f32[8,2048]{1,0:T(8,128)S(1)} %collective-permute-done.refs_1_, f32[8,2048]{1,0:T(8,128)S(1)} %collective-permute-done.1.refs_2_, f32[8,2048]{1,0:T(8,128)S(1)} %collective-permute-done.2.refs_3_, ...), custom_call_target="tpu_custom_call" | custom-call | flops 1000000000 | bytes 1000000 | tf_op jit(solution)/shard_map/spectrum/pallas_call | solution.py:151
  12.4 0.0 copy-start
  12.4 2.5 %collective-permute-start.8 = (bf16[32,16,128]{2,1,0:T(8,128)(2,1)S(1)}, bf16[32,16,128]{2,1,0:T(8,128)(2,1)S(1)}, u32[]{:S(2)}, u32[]{:S(2)}) collective-permute-start(bf16[32,16,128]{2,1,0:T(8,128)(2,1)S(1)} %spectrum.1.refs_1_), channel_id=1, source_target_pairs={{0,24},{1,25},{2,26},{3,27},{4,7},{5,6},{6,5},{7,4},{8,16},{9,17},... | collective-permute-start | bytes 393224 | tf_op jit(solution)/shard_map/ppermute | solution.py:309
  15.0 2.2 %collective-permute-start.7 = (bf16[32,16,128]{2,1,0:T(8,128)(2,1)S(1)}, bf16[32,16,128]{2,1,0:T(8,128)(2,1)S(1)}, u32[]{:S(2)}, u32[]{:S(2)}) collective-permute-start(bf16[32,16,128]{2,1,0:T(8,128)(2,1)S(1)} %spectrum.1.refs_1_), channel_id=1, source_target_pairs={{0,3},{1,2},{2,1},{3,0},{4,28},{5,29},{6,30},{7,31},{8,11},{9,10},... | collective-permute-start | bytes 393224 | tf_op jit(solution)/shard_map/ppermute | solution.py:309
  17.1 0.0 copy-done.1
  17.1 0.6 %collective-permute-start.6 = (bf16[32,16,128]{2,1,0:T(8,128)(2,1)S(1)}, bf16[32,16,128]{2,1,0:T(8,128)(2,1)S(1)}, u32[]{:S(2)}, u32[]{:S(2)}) collective-permute-start(bf16[32,16,128]{2,1,0:T(8,128)(2,1)S(1)} %spectrum.1.refs_1_), channel_id=1, source_target_pairs={{0,16},{1,17},{2,18},{3,19},{4,6},{5,7},{6,4},{7,5},{8,24},{9,25},... | collective-permute-start | bytes 393224 | tf_op jit(solution)/shard_map/ppermute | solution.py:309
  17.7 0.9 %collective-permute-start.5 = (bf16[32,16,128]{2,1,0:T(8,128)(2,1)S(1)}, bf16[32,16,128]{2,1,0:T(8,128)(2,1)S(1)}, u32[]{:S(2)}, u32[]{:S(2)}) collective-permute-start(bf16[32,16,128]{2,1,0:T(8,128)(2,1)S(1)} %spectrum.1.refs_1_), channel_id=1, source_target_pairs={{0,2},{1,3},{2,0},{3,1},{4,20},{5,21},{6,22},{7,23},{8,10},{9,11},... | collective-permute-start | bytes 393224 | tf_op jit(solution)/shard_map/ppermute | solution.py:309
  18.6 0.5 %collective-permute-start.4 = (bf16[32,16,128]{2,1,0:T(8,128)(2,1)S(1)}, bf16[32,16,128]{2,1,0:T(8,128)(2,1)S(1)}, u32[]{:S(2)}, u32[]{:S(2)}) collective-permute-start(bf16[32,16,128]{2,1,0:T(8,128)(2,1)S(1)} %spectrum.1.refs_1_), channel_id=1, source_target_pairs={{0,8},{1,9},{2,10},{3,11},{4,5},{5,4},{6,7},{7,6},{8,0},{9,1},{10,... | collective-permute-start | bytes 393224 | tf_op jit(solution)/shard_map/ppermute | solution.py:309
  19.1 0.8 %collective-permute-done.8 = bf16[32,16,128]{2,1,0:T(8,128)(2,1)S(1)} collective-permute-done((bf16[32,16,128]{2,1,0:T(8,128)(2,1)S(1)}, bf16[32,16,128]{2,1,0:T(8,128)(2,1)S(1)}, u32[]{:S(2)}, u32[]{:S(2)}) %collective-permute-start.8) | collective-permute-done | bytes 131104 | tf_op jit(solution)/shard_map/ppermute | solution.py:309
  19.9 0.6 %collective-permute-start.3 = (bf16[32,16,128]{2,1,0:T(8,128)(2,1)S(1)}, bf16[32,16,128]{2,1,0:T(8,128)(2,1)S(1)}, u32[]{:S(2)}, u32[]{:S(2)}) collective-permute-start(bf16[32,16,128]{2,1,0:T(8,128)(2,1)S(1)} %spectrum.1.refs_1_), channel_id=1, source_target_pairs={{0,1},{1,0},{2,3},{3,2},{4,12},{5,13},{6,14},{7,15},{8,9},{9,8},{1... | collective-permute-start | bytes 393224 | tf_op jit(solution)/shard_map/ppermute | solution.py:309
  20.5 2.3 %collective-permute-done.7 = bf16[32,16,128]{2,1,0:T(8,128)(2,1)S(1)} collective-permute-done((bf16[32,16,128]{2,1,0:T(8,128)(2,1)S(1)}, bf16[32,16,128]{2,1,0:T(8,128)(2,1)S(1)}, u32[]{:S(2)}, u32[]{:S(2)}) %collective-permute-start.7) | collective-permute-done | bytes 131104 | tf_op jit(solution)/shard_map/ppermute | solution.py:309
  22.8 0.0 collective-permute-done.6
  22.8 4.1 %collective-permute-done.5 = bf16[32,16,128]{2,1,0:T(8,128)(2,1)S(1)} collective-permute-done((bf16[32,16,128]{2,1,0:T(8,128)(2,1)S(1)}, bf16[32,16,128]{2,1,0:T(8,128)(2,1)S(1)}, u32[]{:S(2)}, u32[]{:S(2)}) %collective-permute-start.5) | collective-permute-done | bytes 131104 | tf_op jit(solution)/shard_map/ppermute | solution.py:309
  27.0 0.0 collective-permute-done.4
  27.0 0.0 collective-permute-done.3
  27.0 0.1 select_select_fusion
  27.2 0.1 collective-permute-start.9
  27.2 1.5 %collective-permute-done.9 = bf16[2,32,16,128]{3,2,1,0:T(8,128)(2,1)S(1)} collective-permute-done((bf16[2,32,16,128]{3,2,1,0:T(8,128)(2,1)S(1)}, bf16[2,32,16,128]{3,2,1,0:T(8,128)(2,1)S(1)}, u32[]{:S(2)}, u32[]{:S(2)}) %collective-permute-start.9) | collective-permute-done | bytes 262176 | tf_op jit(solution)/shard_map/ppermute | solution.py:313
  28.8 0.1 broadcast_select_fusion.refs_0_
  28.9 0.0 copy-done
  28.9 3.5 %correlate.1 = (bf16[128,128]{1,0:T(8,128)(2,1)S(1)}, bf16[128,128]{1,0:T(8,128)(2,1)S(1)}, bf16[128,128]{1,0:T(8,128)(2,1)S(1)}, bf16[128,128]{1,0:T(8,128)(2,1)S(1)}) custom-call(bf16[2,32,16,128]{3,2,1,0:T(8,128)(2,1)S(1)} %broadcast_select_fusion.refs_0_, bf16[32,16,128]{2,1,0:T(8,128)(2,1)S(1)} %spectrum.1.refs_1_, ...), custom_call_target="tpu_custom_call" | custom-call | flops 4000000000 | bytes 3000000 | tf_op jit(solution)/shard_map/correlate/pallas_call | solution.py:234
  32.4 0.1 collective-permute-start.10
  32.5 2.4 %collective-permute-start.11 = (bf16[128,128]{1,0:T(8,128)(2,1)S(1)}, bf16[128,128]{1,0:T(8,128)(2,1)S(1)}, u32[]{:S(2)}, u32[]{:S(2)}) collective-permute-start(bf16[128,128]{1,0:T(8,128)(2,1)S(1)} %get-tuple-element.11), channel_id=1, source_target_pairs={{0,2},{1,3},{2,0},{3,1},{4,6},{5,7},{6,4},{7,5},{8,10},{9,11},{10,... | collective-permute-start | bytes 98312 | tf_op jit(solution)/shard_map/ppermute | solution.py:337
  34.9 2.0 %collective-permute-start.12 = (bf16[128,128]{1,0:T(8,128)(2,1)S(1)}, bf16[128,128]{1,0:T(8,128)(2,1)S(1)}, u32[]{:S(2)}, u32[]{:S(2)}) collective-permute-start(bf16[128,128]{1,0:T(8,128)(2,1)S(1)} %get-tuple-element.12), channel_id=1, source_target_pairs={{0,3},{1,2},{2,1},{3,0},{4,7},{5,6},{6,5},{7,4},{8,11},{9,10},{10,... | collective-permute-start | bytes 98312 | tf_op jit(solution)/shard_map/ppermute | solution.py:337
  36.9 0.0 collective-permute-done.10.refs_1_
  36.9 1.1 %collective-permute-done.11.refs_2_ = bf16[128,128]{1,0:T(8,128)(2,1)S(1)} collective-permute-done((bf16[128,128]{1,0:T(8,128)(2,1)S(1)}, bf16[128,128]{1,0:T(8,128)(2,1)S(1)}, u32[]{:S(2)}, u32[]{:S(2)}) %collective-permute-start.11) | collective-permute-done | bytes 32800 | tf_op jit(solution)/shard_map/ppermute | solution.py:337
  37.9 2.7 %collective-permute-done.12.refs_3_ = bf16[128,128]{1,0:T(8,128)(2,1)S(1)} collective-permute-done((bf16[128,128]{1,0:T(8,128)(2,1)S(1)}, bf16[128,128]{1,0:T(8,128)(2,1)S(1)}, u32[]{:S(2)}, u32[]{:S(2)}) %collective-permute-start.12) | collective-permute-done | bytes 32800 | tf_op jit(solution)/shard_map/ppermute | solution.py:337
  40.6 1.2 %place.1 = f32[2,32,32,32]{3,2,1,0:T(8,128)} custom-call(bf16[128,128]{1,0:T(8,128)(2,1)S(1)} %get-tuple-element.9.refs_0_, bf16[128,128]{1,0:T(8,128)(2,1)S(1)} %collective-permute-done.10.refs_1_, bf16[128,128]{1,0:T(8,128)(2,1)S(1)} %collective-permute-done.11.refs_2_, bf16[128,128]{1,0:T(8,128)(2,1)S(1)} %collective-permute-done.12.refs_3_), custom_call_target="tpu_custom_call" | custom-call | tf_op jit(solution)/shard_map/place/pallas_call | solution.py:274
  (4 shorter events, 0.1 us)
Async XLA Ops:
  1.0 8.0 %collective-permute-start.2 = (f32[8,2048]{1,0:T(8,128)S(1)}, f32[8,2048]{1,0:T(8,128)S(1)}, u32[]{:S(2)}, u32[]{:S(2)}) collective-permute-start(f32[8,2048]{1,0:T(8,128)S(1)} %get-tuple-element.19), channel_id=1, source_target_pairs={{0,3},{1,2},{2,1},{3,0},{4,7},{5,6},{6,5},{7,4},{8,11},{9,10},{10,... | collective-permute-start | bytes 196616 | tf_op jit(solution)/shard_map/ppermute | solution.py:328
  6.1 4.7 %collective-permute-start = (f32[8,2048]{1,0:T(8,128)S(1)}, f32[8,2048]{1,0:T(8,128)S(1)}, u32[]{:S(2)}, u32[]{:S(2)}) collective-permute-start(f32[8,2048]{1,0:T(8,128)S(1)} %get-tuple-element.20), channel_id=1, source_target_pairs={{0,1},{1,0},{2,3},{3,2},{4,5},{5,4},{6,7},{7,6},{8,9},{9,8},{10,11... | collective-permute-start | bytes 196616 | tf_op jit(solution)/shard_map/ppermute | solution.py:328
  6.1 5.6 %collective-permute-start.1 = (f32[8,2048]{1,0:T(8,128)S(1)}, f32[8,2048]{1,0:T(8,128)S(1)}, u32[]{:S(2)}, u32[]{:S(2)}) collective-permute-start(f32[8,2048]{1,0:T(8,128)S(1)} %get-tuple-element.22), channel_id=1, source_target_pairs={{0,2},{1,3},{2,0},{3,1},{4,6},{5,7},{6,4},{7,5},{8,10},{9,11},{10,... | collective-permute-start | bytes 196616 | tf_op jit(solution)/shard_map/ppermute | solution.py:328
  7.8 9.3 %copy-start.1 = (s32[2]{0:T(128)S(1)}, s32[2]{0:T(128)}, u32[]{:S(2)}) copy-start(s32[2]{0:T(128)} %param.7) | copy-start | bytes 28
  12.4 16.5 %copy-start = (bf16[8192,128]{1,0:T(8,128)(2,1)S(1)}, bf16[8192,128]{1,0:T(8,128)(2,1)}, u32[]{:S(2)}) copy-start(bf16[8192,128]{1,0:T(8,128)(2,1)} %constant.35.clone.refs_5_) | copy-start | bytes 6291460
  12.4 7.4 %collective-permute-start.8 = (bf16[32,16,128]{2,1,0:T(8,128)(2,1)S(1)}, bf16[32,16,128]{2,1,0:T(8,128)(2,1)S(1)}, u32[]{:S(2)}, u32[]{:S(2)}) collective-permute-start(bf16[32,16,128]{2,1,0:T(8,128)(2,1)S(1)} %spectrum.1.refs_1_), channel_id=1, source_target_pairs={{0,24},{1,25},{2,26},{3,27},{4,7},{5,6},{6,5},{7,4},{8,16},{9,17},... | collective-permute-start | bytes 393224 | tf_op jit(solution)/shard_map/ppermute | solution.py:309
  15.0 7.9 %collective-permute-start.7 = (bf16[32,16,128]{2,1,0:T(8,128)(2,1)S(1)}, bf16[32,16,128]{2,1,0:T(8,128)(2,1)S(1)}, u32[]{:S(2)}, u32[]{:S(2)}) collective-permute-start(bf16[32,16,128]{2,1,0:T(8,128)(2,1)S(1)} %spectrum.1.refs_1_), channel_id=1, source_target_pairs={{0,3},{1,2},{2,1},{3,0},{4,28},{5,29},{6,30},{7,31},{8,11},{9,10},... | collective-permute-start | bytes 393224 | tf_op jit(solution)/shard_map/ppermute | solution.py:309
  17.1 5.7 %collective-permute-start.6 = (bf16[32,16,128]{2,1,0:T(8,128)(2,1)S(1)}, bf16[32,16,128]{2,1,0:T(8,128)(2,1)S(1)}, u32[]{:S(2)}, u32[]{:S(2)}) collective-permute-start(bf16[32,16,128]{2,1,0:T(8,128)(2,1)S(1)} %spectrum.1.refs_1_), channel_id=1, source_target_pairs={{0,16},{1,17},{2,18},{3,19},{4,6},{5,7},{6,4},{7,5},{8,24},{9,25},... | collective-permute-start | bytes 393224 | tf_op jit(solution)/shard_map/ppermute | solution.py:309
  17.7 9.3 %collective-permute-start.5 = (bf16[32,16,128]{2,1,0:T(8,128)(2,1)S(1)}, bf16[32,16,128]{2,1,0:T(8,128)(2,1)S(1)}, u32[]{:S(2)}, u32[]{:S(2)}) collective-permute-start(bf16[32,16,128]{2,1,0:T(8,128)(2,1)S(1)} %spectrum.1.refs_1_), channel_id=1, source_target_pairs={{0,2},{1,3},{2,0},{3,1},{4,20},{5,21},{6,22},{7,23},{8,10},{9,11},... | collective-permute-start | bytes 393224 | tf_op jit(solution)/shard_map/ppermute | solution.py:309
  18.6 8.4 %collective-permute-start.4 = (bf16[32,16,128]{2,1,0:T(8,128)(2,1)S(1)}, bf16[32,16,128]{2,1,0:T(8,128)(2,1)S(1)}, u32[]{:S(2)}, u32[]{:S(2)}) collective-permute-start(bf16[32,16,128]{2,1,0:T(8,128)(2,1)S(1)} %spectrum.1.refs_1_), channel_id=1, source_target_pairs={{0,8},{1,9},{2,10},{3,11},{4,5},{5,4},{6,7},{7,6},{8,0},{9,1},{10,... | collective-permute-start | bytes 393224 | tf_op jit(solution)/shard_map/ppermute | solution.py:309
  19.9 7.1 %collective-permute-start.3 = (bf16[32,16,128]{2,1,0:T(8,128)(2,1)S(1)}, bf16[32,16,128]{2,1,0:T(8,128)(2,1)S(1)}, u32[]{:S(2)}, u32[]{:S(2)}) collective-permute-start(bf16[32,16,128]{2,1,0:T(8,128)(2,1)S(1)} %spectrum.1.refs_1_), channel_id=1, source_target_pairs={{0,1},{1,0},{2,3},{3,2},{4,12},{5,13},{6,14},{7,15},{8,9},{9,8},{1... | collective-permute-start | bytes 393224 | tf_op jit(solution)/shard_map/ppermute | solution.py:309
  27.2 1.6 %collective-permute-start.9 = (bf16[2,32,16,128]{3,2,1,0:T(8,128)(2,1)S(1)}, bf16[2,32,16,128]{3,2,1,0:T(8,128)(2,1)S(1)}, u32[]{:S(2)}, u32[]{:S(2)}) collective-permute-start(bf16[2,32,16,128]{3,2,1,0:T(8,128)(2,1)S(1)} %select_select_fusion), channel_id=1, source_target_pairs={{0,4},{4,0},{8,12},{12,8},{16,20},{20,16},{24,28},{28,24},{1,5},{5... | collective-permute-start | bytes 786440 | tf_op jit(solution)/shard_map/ppermute | solution.py:313
  32.4 4.5 %collective-permute-start.10 = (bf16[128,128]{1,0:T(8,128)(2,1)S(1)}, bf16[128,128]{1,0:T(8,128)(2,1)S(1)}, u32[]{:S(2)}, u32[]{:S(2)}) collective-permute-start(bf16[128,128]{1,0:T(8,128)(2,1)S(1)} %get-tuple-element.10), channel_id=1, source_target_pairs={{0,1},{1,0},{2,3},{3,2},{4,5},{5,4},{6,7},{7,6},{8,9},{9,8},{10,11... | collective-permute-start | bytes 98312 | tf_op jit(solution)/shard_map/ppermute | solution.py:337
  32.5 5.4 %collective-permute-start.11 = (bf16[128,128]{1,0:T(8,128)(2,1)S(1)}, bf16[128,128]{1,0:T(8,128)(2,1)S(1)}, u32[]{:S(2)}, u32[]{:S(2)}) collective-permute-start(bf16[128,128]{1,0:T(8,128)(2,1)S(1)} %get-tuple-element.11), channel_id=1, source_target_pairs={{0,2},{1,3},{2,0},{3,1},{4,6},{5,7},{6,4},{7,5},{8,10},{9,11},{10,... | collective-permute-start | bytes 98312 | tf_op jit(solution)/shard_map/ppermute | solution.py:337
  34.9 5.7 %collective-permute-start.12 = (bf16[128,128]{1,0:T(8,128)(2,1)S(1)}, bf16[128,128]{1,0:T(8,128)(2,1)S(1)}, u32[]{:S(2)}, u32[]{:S(2)}) collective-permute-start(bf16[128,128]{1,0:T(8,128)(2,1)S(1)} %get-tuple-element.12), channel_id=1, source_target_pairs={{0,3},{1,2},{2,1},{3,0},{4,7},{5,6},{6,5},{7,4},{8,11},{9,10},{10,... | collective-permute-start | bytes 98312 | tf_op jit(solution)/shard_map/ppermute | solution.py:337

commit v3 on v2

--- a/solution.py
+++ b/solution.py
@@ -18,6 +18,9 @@
 N2 = 256
 K2 = BINS // N1
 assert N1 == W and K2 == 128
+
+
+SUMS_PLAN = (0, 2, 3, 1)
 
 
 def split_bf16(x):
@@ -209,7 +212,7 @@
     lane = lax.broadcasted_iota(jnp.int32, (channels, LAGS), 1) // width
     for source in range(0, steps * channels, 2):
         for far in range(tparts):
-            dest = me ^ far
+            dest = me ^ SUMS_PLAN[far]
             pair = []
             for first in (source * local, (source + 1) * local):
                 value = None
@@ -253,7 +256,7 @@
     me = lax.axis_index("ta")
     width = LAGS // tparts
     for far in range(tparts):
-        source = me ^ far
+        source = me ^ SUMS_PLAN[far]
         value = pieces[far][...].astype(jnp.float32)
         for step in range(tparts):
             block = source ^ step
@@ -294,21 +297,26 @@
         residents = [lax.ppermute(block, "ta", flip("ta", far)) for far in range(1, tparts)]
         return jnp.take(lax.all_gather(block, "ch"), owners, axis=0), residents
     away = (owners ^ me).reshape((steps,) + (1,) * block.ndim)
+    even_plan = [('ta', 3), ('ta', 2), ('ch', 2), ('ch', 4), ('ta', 1), ('ch', 6)]
+    odd_plan = [('ch', 2), ('ch', 4), ('ta', 3), ('ta', 2), ('ch', 6), ('ta', 1)]
+    got = []
+    for even_move, odd_move in zip(even_plan, odd_plan):
+        perm = []
+        for ch in range(count):
+            axis, mask = odd_move if ch & 1 else even_move
+            for ta in range(tparts):
+                to = (ch, ta ^ mask) if axis == "ta" else (ch ^ mask, ta)
+                perm.append((ch * tparts + ta, to[0] * tparts + to[1]))
+        got.append(lax.ppermute(block, ("ch", "ta"), perm))
+
+    def result(move):
+        first, second = got[even_plan.index(move)], got[odd_plan.index(move)]
+        return first if first is second else jnp.where(odd, second, first)
+
+    residents = [result(("ta", far)) for far in range(1, tparts)]
     held = jnp.broadcast_to(block[None], (steps,) + block.shape)
-    residents = [None] * (tparts - 1)
-    for far, mask in ((3, 6), (2, 4), (1, 2)):
-        got = []
-        for parity in (0, 1):
-            perm = []
-            for ch in range(count):
-                for ta in range(tparts):
-                    if ch & 1 == parity:
-                        perm.append((ch * tparts + ta, ch * tparts + (ta ^ far)))
-                    else:
-                        perm.append((ch * tparts + ta, (ch ^ mask) * tparts + ta))
-            got.append(lax.ppermute(block, ("ch", "ta"), perm))
-        residents[far - 1] = jnp.where(odd, got[1], got[0])
-        held = jnp.where((away & 6) == mask, jnp.where(odd, got[0], got[1])[None], held)
+    for mask in (2, 4, 6):
+        held = jnp.where((away & 6) == mask, result(("ch", mask))[None], held)
     for bit in [*range(3, count.bit_length() - 1), 0]:
         other = lax.ppermute(held, "ch", flip("ch", 1 << bit))
         held = jnp.where((away & (1 << bit)) != 0, other, held)
@@ -334,7 +342,8 @@
     panels, others = exchange(whitened, owners)
     pieces = correlate(panels, [whitened] + others)
     pieces = [pieces[0]] + [
-        lax.ppermute(pieces[far], "ta", flip("ta", far)) for far in range(1, tparts)
+        lax.ppermute(piece, "ta", flip("ta", far))
+        for piece, far in zip(pieces[1:], SUMS_PLAN[1:])
     ]
     return place(pieces, steps, channels)
 

time: 42 us -> 39.3 us (0.936)
  waiting for transfers between devices: 15.7 us -> 13.1 us
    ppermute x6, waiting for transfers between devices: 7.25 us -> 5.57 us  [exchange(): got.append(lax.ppermute(block, ('ch', 'ta'), perm))]
    ppermute x3, starting transfers between devices: 4.44 us -> 3.55 us  [body(): lax.ppermute(piece, 'ta', flip('ta', far))]
    ppermute x3, waiting for transfers between devices: 3.75 us -> 2.88 us  [body(): lax.ppermute(piece, 'ta', flip('ta', far))]
    ppermute x6, starting transfers between devices: 7.24 us -> 8.01 us  [exchange(): got.append(lax.ppermute(block, ('ch', 'ta'), perm))]
  transfers between devices with their start and end apart: 13 -> 13, of which waited for: 9 -> 10; matrix products, arithmetic and copies ran while one was open for 5% -> 5% of each run, Pallas kernels for 0% -> 0%
where the time goes in v3:
time: 39.3 us; the launch traced here: 39.1 us
  starting transfers between devices  17.4 us (44%)
  waiting for transfers between devices  13.1 us (33%)
  Pallas kernels  5.29 us (13%)
  other arithmetic  2.16 us (5%)
  local copies, waits for them, and re-layouts  1.03 us (3%)
    ppermute x6, starting transfers between devices, exchange(): got.append(lax.ppermute(block, ('ch', 'ta'), perm))  8.01 us
    ppermute x3, starting transfers between devices, body(): lax.ppermute(own[far], 'ta', flip('ta', far))  5.76 us
    ppermute x6, waiting for transfers between devices, exchange(): got.append(lax.ppermute(block, ('ch', 'ta'), perm))  5.57 us
    ppermute x3, starting transfers between devices, body(): lax.ppermute(piece, 'ta', flip('ta', far))  3.55 us
    pallas_call x1, Pallas kernels, correlate(): pl.pallas_call(lambda *refs: correlate_kernel(tparts, *refs), out_shape=[...  3.49 us
    ppermute x3, waiting for transfers between devices, body(): lax.ppermute(own[far], 'ta', flip('ta', far))  3.13 us
    ppermute x3, waiting for transfers between devices, body(): lax.ppermute(piece, 'ta', flip('ta', far))  2.88 us
    ppermute x1, waiting for transfers between devices, exchange(): other = lax.ppermute(held, 'ch', flip('ch', 1 << bit))  1.52 us
  transfers between devices with their start and end apart: 13, of which 10 were waited for; matrix products, arithmetic and copies ran while one was open for 5% of the time, Pallas kernels for 0%

profile of v3, /device:TPU:0, one launch (start us, length us, event | category | flops | bytes accessed | tf_op | source)
XLA Modules:
  0.0 39.1 jit_solution(5374259546576006017)
XLA Ops:
  0.0 1.0 %constant_dynamic-slice_fusion = (f32[8,2048]{1,0:T(8,128)S(1)}, f32[8,2048]{1,0:T(8,128)S(1)}, f32[8,2048]{1,0:T(8,128)S(1)}, f32[8,2048]{1,0:T(8,128)S(1)}) fusion(f32[32,2048]{1,0:T(8,128)} %param.5, s32[]{:T(128)S(6)} %select_n.59, s32[]{:T(128)S(6)} %select_n.57, s32[]{:T(128)S(6)} %select_n.56, s32[]{:T(128)S(6)} %select_n.58), kind=kLoop, calls=%fused_computation.9 | loop fusion | bytes 524304 | tf_op jit(solution)/shard_map/dynamic_slice | solution.py:332
  1.0 5.1 %collective-permute-start.2 = (f32[8,2048]{1,0:T(8,128)S(1)}, f32[8,2048]{1,0:T(8,128)S(1)}, u32[]{:S(2)}, u32[]{:S(2)}) collective-permute-start(f32[8,2048]{1,0:T(8,128)S(1)} %get-tuple-element.19), channel_id=1, source_target_pairs={{0,3},{1,2},{2,1},{3,0},{4,7},{5,6},{6,5},{7,4},{8,11},{9,10},{10,... | collective-permute-start | bytes 196616 | tf_op jit(solution)/shard_map/ppermute | solution.py:336
  6.1 0.0 collective-permute-start
  6.1 0.6 %collective-permute-start.1 = (f32[8,2048]{1,0:T(8,128)S(1)}, f32[8,2048]{1,0:T(8,128)S(1)}, u32[]{:S(2)}, u32[]{:S(2)}) collective-permute-start(f32[8,2048]{1,0:T(8,128)S(1)} %get-tuple-element.22), channel_id=1, source_target_pairs={{0,2},{1,3},{2,0},{3,1},{4,6},{5,7},{6,4},{7,5},{8,10},{9,11},{10,... | collective-permute-start | bytes 196616 | tf_op jit(solution)/shard_map/ppermute | solution.py:336
  6.7 1.1 %broadcast_multiply_fusion.refs_5_ = f32[576,256]{1,0:T(8,128)S(1)} fusion(f32[576,256]{1,0:T(8,128)} %constant.34.clone, f32[]{:T(128)} %constant.12.clone.1), kind=kLoop, calls=%fused_computation | loop fusion | flops 147456 | bytes 1179652 | tf_op jit(solution)/shard_map/mul | solution.py:340
  7.8 0.0 copy-start.1
  7.8 0.7 %dynamic-slice_convert_fusion = f32[8]{0:T(128)S(1)} fusion(s32[32]{0:T(128)} %param.6, s32[]{:T(128)S(6)} %select_n.56), kind=kLoop, calls=%fused_computation.13 | loop fusion | flops 8 | bytes 68 | tf_op jit(solution)/shard_map/convert_element_type | solution.py:339
  8.6 0.4 %collective-permute-done.2.refs_3_ = f32[8,2048]{1,0:T(8,128)S(1)} collective-permute-done((f32[8,2048]{1,0:T(8,128)S(1)}, f32[8,2048]{1,0:T(8,128)S(1)}, u32[]{:S(2)}, u32[]{:S(2)}) %collective-permute-start.2) | collective-permute-done | bytes 65568 | tf_op jit(solution)/shard_map/ppermute | solution.py:336
  9.0 1.8 %collective-permute-done.refs_1_ = f32[8,2048]{1,0:T(8,128)S(1)} collective-permute-done((f32[8,2048]{1,0:T(8,128)S(1)}, f32[8,2048]{1,0:T(8,128)S(1)}, u32[]{:S(2)}, u32[]{:S(2)}) %collective-permute-start) | collective-permute-done | bytes 65568 | tf_op jit(solution)/shard_map/ppermute | solution.py:336
  10.7 1.0 %collective-permute-done.1.refs_2_ = f32[8,2048]{1,0:T(8,128)S(1)} collective-permute-done((f32[8,2048]{1,0:T(8,128)S(1)}, f32[8,2048]{1,0:T(8,128)S(1)}, u32[]{:S(2)}, u32[]{:S(2)}) %collective-permute-start.1) | collective-permute-done | bytes 65568 | tf_op jit(solution)/shard_map/ppermute | solution.py:336
  11.7 0.1 broadcast_in_dim.61.refs_4_
  11.8 0.6 %spectrum.1.refs_1_ = bf16[32,16,128]{2,1,0:T(8,128)(2,1)S(1)} custom-call(f32[8,2048]{1,0:T(8,128)S(1)} %get-tuple-element.21.refs_0_, f32[8,2048]{1,0:T(8,128)S(1)} %collective-permute-done.refs_1_, f32[8,2048]{1,0:T(8,128)S(1)} %collective-permute-done.1.refs_2_, f32[8,2048]{1,0:T(8,128)S(1)} %collective-permute-done.2.refs_3_, ...), custom_call_target="tpu_custom_call" | custom-call | flops 1000000000 | bytes 1000000 | tf_op jit(solution)/shard_map/spectrum/pallas_call | solution.py:154
  12.4 0.0 copy-start
  12.4 1.6 %collective-permute-start.8 = (bf16[32,16,128]{2,1,0:T(8,128)(2,1)S(1)}, bf16[32,16,128]{2,1,0:T(8,128)(2,1)S(1)}, u32[]{:S(2)}, u32[]{:S(2)}) collective-permute-start(bf16[32,16,128]{2,1,0:T(8,128)(2,1)S(1)} %spectrum.1.refs_1_), channel_id=1, source_target_pairs={{0,8},{1,9},{2,10},{3,11},{4,7},{5,6},{6,5},{7,4},{8,0},{9,1},{10,... | collective-permute-start | bytes 393224 | tf_op jit(solution)/shard_map/ppermute | solution.py:310
  14.0 2.2 %collective-permute-start.7 = (bf16[32,16,128]{2,1,0:T(8,128)(2,1)S(1)}, bf16[32,16,128]{2,1,0:T(8,128)(2,1)S(1)}, u32[]{:S(2)}, u32[]{:S(2)}) collective-permute-start(bf16[32,16,128]{2,1,0:T(8,128)(2,1)S(1)} %spectrum.1.refs_1_), channel_id=1, source_target_pairs={{0,3},{1,2},{2,1},{3,0},{4,12},{5,13},{6,14},{7,15},{8,11},{9,10},... | collective-permute-start | bytes 393224 | tf_op jit(solution)/shard_map/ppermute | solution.py:310
  16.2 0.0 copy-done.1
  16.2 1.6 %collective-permute-start.6 = (bf16[32,16,128]{2,1,0:T(8,128)(2,1)S(1)}, bf16[32,16,128]{2,1,0:T(8,128)(2,1)S(1)}, u32[]{:S(2)}, u32[]{:S(2)}) collective-permute-start(bf16[32,16,128]{2,1,0:T(8,128)(2,1)S(1)} %spectrum.1.refs_1_), channel_id=1, source_target_pairs={{0,16},{1,17},{2,18},{3,19},{4,6},{5,7},{6,4},{7,5},{8,24},{9,25},... | collective-permute-start | bytes 393224 | tf_op jit(solution)/shard_map/ppermute | solution.py:310
  17.8 0.9 %collective-permute-start.5 = (bf16[32,16,128]{2,1,0:T(8,128)(2,1)S(1)}, bf16[32,16,128]{2,1,0:T(8,128)(2,1)S(1)}, u32[]{:S(2)}, u32[]{:S(2)}) collective-permute-start(bf16[32,16,128]{2,1,0:T(8,128)(2,1)S(1)} %spectrum.1.refs_1_), channel_id=1, source_target_pairs={{0,2},{1,3},{2,0},{3,1},{4,20},{5,21},{6,22},{7,23},{8,10},{9,11},... | collective-permute-start | bytes 393224 | tf_op jit(solution)/shard_map/ppermute | solution.py:310
  18.6 0.5 %collective-permute-start.4 = (bf16[32,16,128]{2,1,0:T(8,128)(2,1)S(1)}, bf16[32,16,128]{2,1,0:T(8,128)(2,1)S(1)}, u32[]{:S(2)}, u32[]{:S(2)}) collective-permute-start(bf16[32,16,128]{2,1,0:T(8,128)(2,1)S(1)} %spectrum.1.refs_1_), channel_id=1, source_target_pairs={{0,24},{1,25},{2,26},{3,27},{4,5},{5,4},{6,7},{7,6},{8,16},{9,17},... | collective-permute-start | bytes 393224 | tf_op jit(solution)/shard_map/ppermute | solution.py:310
  19.1 0.0 collective-permute-done.8
  19.1 1.4 %collective-permute-start.3 = (bf16[32,16,128]{2,1,0:T(8,128)(2,1)S(1)}, bf16[32,16,128]{2,1,0:T(8,128)(2,1)S(1)}, u32[]{:S(2)}, u32[]{:S(2)}) collective-permute-start(bf16[32,16,128]{2,1,0:T(8,128)(2,1)S(1)} %spectrum.1.refs_1_), channel_id=1, source_target_pairs={{0,1},{1,0},{2,3},{3,2},{4,28},{5,29},{6,30},{7,31},{8,9},{9,8},{1... | collective-permute-start | bytes 393224 | tf_op jit(solution)/shard_map/ppermute | solution.py:310
  20.5 0.4 %collective-permute-done.7 = bf16[32,16,128]{2,1,0:T(8,128)(2,1)S(1)} collective-permute-done((bf16[32,16,128]{2,1,0:T(8,128)(2,1)S(1)}, bf16[32,16,128]{2,1,0:T(8,128)(2,1)S(1)}, u32[]{:S(2)}, u32[]{:S(2)}) %collective-permute-start.7) | collective-permute-done | bytes 131104 | tf_op jit(solution)/shard_map/ppermute | solution.py:310
  20.9 2.2 %collective-permute-done.6 = bf16[32,16,128]{2,1,0:T(8,128)(2,1)S(1)} collective-permute-done((bf16[32,16,128]{2,1,0:T(8,128)(2,1)S(1)}, bf16[32,16,128]{2,1,0:T(8,128)(2,1)S(1)}, u32[]{:S(2)}, u32[]{:S(2)}) %collective-permute-start.6) | collective-permute-done | bytes 131104 | tf_op jit(solution)/shard_map/ppermute | solution.py:310
  23.1 3.0 %collective-permute-done.5 = bf16[32,16,128]{2,1,0:T(8,128)(2,1)S(1)} collective-permute-done((bf16[32,16,128]{2,1,0:T(8,128)(2,1)S(1)}, bf16[32,16,128]{2,1,0:T(8,128)(2,1)S(1)}, u32[]{:S(2)}, u32[]{:S(2)}) %collective-permute-start.5) | collective-permute-done | bytes 131104 | tf_op jit(solution)/shard_map/ppermute | solution.py:310
  26.1 0.0 collective-permute-done.4
  26.1 0.0 collective-permute-done.3
  26.1 0.1 select_select_fusion
  26.3 0.1 collective-permute-start.9
  26.3 1.5 %collective-permute-done.9 = bf16[2,32,16,128]{3,2,1,0:T(8,128)(2,1)S(1)} collective-permute-done((bf16[2,32,16,128]{3,2,1,0:T(8,128)(2,1)S(1)}, bf16[2,32,16,128]{3,2,1,0:T(8,128)(2,1)S(1)}, u32[]{:S(2)}, u32[]{:S(2)}) %collective-permute-start.9) | collective-permute-done | bytes 262176 | tf_op jit(solution)/shard_map/ppermute | solution.py:321
  27.9 0.1 broadcast_select_fusion.refs_0_
  28.0 0.0 copy-done
  28.0 3.5 %correlate.1 = (bf16[128,128]{1,0:T(8,128)(2,1)S(1)}, bf16[128,128]{1,0:T(8,128)(2,1)S(1)}, bf16[128,128]{1,0:T(8,128)(2,1)S(1)}, bf16[128,128]{1,0:T(8,128)(2,1)S(1)}) custom-call(bf16[2,32,16,128]{3,2,1,0:T(8,128)(2,1)S(1)} %broadcast_select_fusion.refs_0_, bf16[32,16,128]{2,1,0:T(8,128)(2,1)S(1)} %spectrum.1.refs_1_, ...), custom_call_target="tpu_custom_call" | custom-call | flops 4000000000 | bytes 3000000 | tf_op jit(solution)/shard_map/correlate/pallas_call | solution.py:237
  31.5 0.5 %collective-permute-start.10 = (bf16[128,128]{1,0:T(8,128)(2,1)S(1)}, bf16[128,128]{1,0:T(8,128)(2,1)S(1)}, u32[]{:S(2)}, u32[]{:S(2)}) collective-permute-start(bf16[128,128]{1,0:T(8,128)(2,1)S(1)} %get-tuple-element.10), channel_id=1, source_target_pairs={{0,2},{1,3},{2,0},{3,1},{4,6},{5,7},{6,4},{7,5},{8,10},{9,11},{10,... | collective-permute-start | bytes 98312 | tf_op jit(solution)/shard_map/ppermute | solution.py:345
  32.0 1.7 %collective-permute-start.11 = (bf16[128,128]{1,0:T(8,128)(2,1)S(1)}, bf16[128,128]{1,0:T(8,128)(2,1)S(1)}, u32[]{:S(2)}, u32[]{:S(2)}) collective-permute-start(bf16[128,128]{1,0:T(8,128)(2,1)S(1)} %get-tuple-element.11), channel_id=1, source_target_pairs={{0,3},{1,2},{2,1},{3,0},{4,7},{5,6},{6,5},{7,4},{8,11},{9,10},{10,... | collective-permute-start | bytes 98312 | tf_op jit(solution)/shard_map/ppermute | solution.py:345
  33.7 1.4 %collective-permute-start.12 = (bf16[128,128]{1,0:T(8,128)(2,1)S(1)}, bf16[128,128]{1,0:T(8,128)(2,1)S(1)}, u32[]{:S(2)}, u32[]{:S(2)}) collective-permute-start(bf16[128,128]{1,0:T(8,128)(2,1)S(1)} %get-tuple-element.12), channel_id=1, source_target_pairs={{0,1},{1,0},{2,3},{3,2},{4,5},{5,4},{6,7},{7,6},{8,9},{9,8},{10,11... | collective-permute-start | bytes 98312 | tf_op jit(solution)/shard_map/ppermute | solution.py:345
  35.0 1.9 %collective-permute-done.10.refs_1_ = bf16[128,128]{1,0:T(8,128)(2,1)S(1)} collective-permute-done((bf16[128,128]{1,0:T(8,128)(2,1)S(1)}, bf16[128,128]{1,0:T(8,128)(2,1)S(1)}, u32[]{:S(2)}, u32[]{:S(2)}) %collective-permute-start.10) | collective-permute-done | bytes 32800 | tf_op jit(solution)/shard_map/ppermute | solution.py:345
  37.0 0.8 %collective-permute-done.11.refs_2_ = bf16[128,128]{1,0:T(8,128)(2,1)S(1)} collective-permute-done((bf16[128,128]{1,0:T(8,128)(2,1)S(1)}, bf16[128,128]{1,0:T(8,128)(2,1)S(1)}, u32[]{:S(2)}, u32[]{:S(2)}) %collective-permute-start.11) | collective-permute-done | bytes 32800 | tf_op jit(solution)/shard_map/ppermute | solution.py:345
  37.8 0.1 collective-permute-done.12.refs_3_
  37.9 1.2 %place.1 = f32[2,32,32,32]{3,2,1,0:T(8,128)} custom-call(bf16[128,128]{1,0:T(8,128)(2,1)S(1)} %get-tuple-element.9.refs_0_, bf16[128,128]{1,0:T(8,128)(2,1)S(1)} %collective-permute-done.10.refs_1_, bf16[128,128]{1,0:T(8,128)(2,1)S(1)} %collective-permute-done.11.refs_2_, bf16[128,128]{1,0:T(8,128)(2,1)S(1)} %collective-permute-done.12.refs_3_), custom_call_target="tpu_custom_call" | custom-call | tf_op jit(solution)/shard_map/place/pallas_call | solution.py:277
  (4 shorter events, 0.1 us)
Async XLA Ops:
  1.0 8.0 %collective-permute-start.2 = (f32[8,2048]{1,0:T(8,128)S(1)}, f32[8,2048]{1,0:T(8,128)S(1)}, u32[]{:S(2)}, u32[]{:S(2)}) collective-permute-start(f32[8,2048]{1,0:T(8,128)S(1)} %get-tuple-element.19), channel_id=1, source_target_pairs={{0,3},{1,2},{2,1},{3,0},{4,7},{5,6},{6,5},{7,4},{8,11},{9,10},{10,... | collective-permute-start | bytes 196616 | tf_op jit(solution)/shard_map/ppermute | solution.py:336
  6.1 4.7 %collective-permute-start = (f32[8,2048]{1,0:T(8,128)S(1)}, f32[8,2048]{1,0:T(8,128)S(1)}, u32[]{:S(2)}, u32[]{:S(2)}) collective-permute-start(f32[8,2048]{1,0:T(8,128)S(1)} %get-tuple-element.20), channel_id=1, source_target_pairs={{0,1},{1,0},{2,3},{3,2},{4,5},{5,4},{6,7},{7,6},{8,9},{9,8},{10,11... | collective-permute-start | bytes 196616 | tf_op jit(solution)/shard_map/ppermute | solution.py:336
  6.1 5.6 %collective-permute-start.1 = (f32[8,2048]{1,0:T(8,128)S(1)}, f32[8,2048]{1,0:T(8,128)S(1)}, u32[]{:S(2)}, u32[]{:S(2)}) collective-permute-start(f32[8,2048]{1,0:T(8,128)S(1)} %get-tuple-element.22), channel_id=1, source_target_pairs={{0,2},{1,3},{2,0},{3,1},{4,6},{5,7},{6,4},{7,5},{8,10},{9,11},{10,... | collective-permute-start | bytes 196616 | tf_op jit(solution)/shard_map/ppermute | solution.py:336
  7.8 8.3 %copy-start.1 = (s32[2]{0:T(128)S(1)}, s32[2]{0:T(128)}, u32[]{:S(2)}) copy-start(s32[2]{0:T(128)} %param.7) | copy-start | bytes 28
  12.4 15.6 %copy-start = (bf16[8192,128]{1,0:T(8,128)(2,1)S(1)}, bf16[8192,128]{1,0:T(8,128)(2,1)}, u32[]{:S(2)}) copy-start(bf16[8192,128]{1,0:T(8,128)(2,1)} %constant.35.clone.refs_5_) | copy-start | bytes 6291460
  12.4 6.7 %collective-permute-start.8 = (bf16[32,16,128]{2,1,0:T(8,128)(2,1)S(1)}, bf16[32,16,128]{2,1,0:T(8,128)(2,1)S(1)}, u32[]{:S(2)}, u32[]{:S(2)}) collective-permute-start(bf16[32,16,128]{2,1,0:T(8,128)(2,1)S(1)} %spectrum.1.refs_1_), channel_id=1, source_target_pairs={{0,8},{1,9},{2,10},{3,11},{4,7},{5,6},{6,5},{7,4},{8,0},{9,1},{10,... | collective-permute-start | bytes 393224 | tf_op jit(solution)/shard_map/ppermute | solution.py:310
  14.0 6.9 %collective-permute-start.7 = (bf16[32,16,128]{2,1,0:T(8,128)(2,1)S(1)}, bf16[32,16,128]{2,1,0:T(8,128)(2,1)S(1)}, u32[]{:S(2)}, u32[]{:S(2)}) collective-permute-start(bf16[32,16,128]{2,1,0:T(8,128)(2,1)S(1)} %spectrum.1.refs_1_), channel_id=1, source_target_pairs={{0,3},{1,2},{2,1},{3,0},{4,12},{5,13},{6,14},{7,15},{8,11},{9,10},... | collective-permute-start | bytes 393224 | tf_op jit(solution)/shard_map/ppermute | solution.py:310
  16.2 6.9 %collective-permute-start.6 = (bf16[32,16,128]{2,1,0:T(8,128)(2,1)S(1)}, bf16[32,16,128]{2,1,0:T(8,128)(2,1)S(1)}, u32[]{:S(2)}, u32[]{:S(2)}) collective-permute-start(bf16[32,16,128]{2,1,0:T(8,128)(2,1)S(1)} %spectrum.1.refs_1_), channel_id=1, source_target_pairs={{0,16},{1,17},{2,18},{3,19},{4,6},{5,7},{6,4},{7,5},{8,24},{9,25},... | collective-permute-start | bytes 393224 | tf_op jit(solution)/shard_map/ppermute | solution.py:310
  17.8 8.3 %collective-permute-start.5 = (bf16[32,16,128]{2,1,0:T(8,128)(2,1)S(1)}, bf16[32,16,128]{2,1,0:T(8,128)(2,1)S(1)}, u32[]{:S(2)}, u32[]{:S(2)}) collective-permute-start(bf16[32,16,128]{2,1,0:T(8,128)(2,1)S(1)} %spectrum.1.refs_1_), channel_id=1, source_target_pairs={{0,2},{1,3},{2,0},{3,1},{4,20},{5,21},{6,22},{7,23},{8,10},{9,11},... | collective-permute-start | bytes 393224 | tf_op jit(solution)/shard_map/ppermute | solution.py:310
  18.6 7.5 %collective-permute-start.4 = (bf16[32,16,128]{2,1,0:T(8,128)(2,1)S(1)}, bf16[32,16,128]{2,1,0:T(8,128)(2,1)S(1)}, u32[]{:S(2)}, u32[]{:S(2)}) collective-permute-start(bf16[32,16,128]{2,1,0:T(8,128)(2,1)S(1)} %spectrum.1.refs_1_), channel_id=1, source_target_pairs={{0,24},{1,25},{2,26},{3,27},{4,5},{5,4},{6,7},{7,6},{8,16},{9,17},... | collective-permute-start | bytes 393224 | tf_op jit(solution)/shard_map/ppermute | solution.py:310
  19.1 7.0 %collective-permute-start.3 = (bf16[32,16,128]{2,1,0:T(8,128)(2,1)S(1)}, bf16[32,16,128]{2,1,0:T(8,128)(2,1)S(1)}, u32[]{:S(2)}, u32[]{:S(2)}) collective-permute-start(bf16[32,16,128]{2,1,0:T(8,128)(2,1)S(1)} %spectrum.1.refs_1_), channel_id=1, source_target_pairs={{0,1},{1,0},{2,3},{3,2},{4,28},{5,29},{6,30},{7,31},{8,9},{9,8},{1... | collective-permute-start | bytes 393224 | tf_op jit(solution)/shard_map/ppermute | solution.py:310
  26.3 1.6 %collective-permute-start.9 = (bf16[2,32,16,128]{3,2,1,0:T(8,128)(2,1)S(1)}, bf16[2,32,16,128]{3,2,1,0:T(8,128)(2,1)S(1)}, u32[]{:S(2)}, u32[]{:S(2)}) collective-permute-start(bf16[2,32,16,128]{3,2,1,0:T(8,128)(2,1)S(1)} %select_select_fusion), channel_id=1, source_target_pairs={{0,4},{4,0},{8,12},{12,8},{16,20},{20,16},{24,28},{28,24},{1,5},{5... | collective-permute-start | bytes 786440 | tf_op jit(solution)/shard_map/ppermute | solution.py:321
  31.5 5.5 %collective-permute-start.10 = (bf16[128,128]{1,0:T(8,128)(2,1)S(1)}, bf16[128,128]{1,0:T(8,128)(2,1)S(1)}, u32[]{:S(2)}, u32[]{:S(2)}) collective-permute-start(bf16[128,128]{1,0:T(8,128)(2,1)S(1)} %get-tuple-element.10), channel_id=1, source_target_pairs={{0,2},{1,3},{2,0},{3,1},{4,6},{5,7},{6,4},{7,5},{8,10},{9,11},{10,... | collective-permute-start | bytes 98312 | tf_op jit(solution)/shard_map/ppermute | solution.py:345
  32.0 5.8 %collective-permute-start.11 = (bf16[128,128]{1,0:T(8,128)(2,1)S(1)}, bf16[128,128]{1,0:T(8,128)(2,1)S(1)}, u32[]{:S(2)}, u32[]{:S(2)}) collective-permute-start(bf16[128,128]{1,0:T(8,128)(2,1)S(1)} %get-tuple-element.11), channel_id=1, source_target_pairs={{0,3},{1,2},{2,1},{3,0},{4,7},{5,6},{6,5},{7,4},{8,11},{9,10},{10,... | collective-permute-start | bytes 98312 | tf_op jit(solution)/shard_map/ppermute | solution.py:345
  33.7 4.3 %collective-permute-start.12 = (bf16[128,128]{1,0:T(8,128)(2,1)S(1)}, bf16[128,128]{1,0:T(8,128)(2,1)S(1)}, u32[]{:S(2)}, u32[]{:S(2)}) collective-permute-start(bf16[128,128]{1,0:T(8,128)(2,1)S(1)} %get-tuple-element.12), channel_id=1, source_target_pairs={{0,1},{1,0},{2,3},{3,2},{4,5},{5,4},{6,7},{7,6},{8,9},{9,8},{10,11... | collective-permute-start | bytes 98312 | tf_op jit(solution)/shard_map/ppermute | solution.py:345

commit v4 on v3

--- a/solution.py
+++ b/solution.py
@@ -169,25 +169,23 @@
     )(*blocks, alive, tables)
 
 
-GROUP = 8
+GROUPS = (2, 6, 12, 12)
 
 
 def correlate_kernel(tparts, panels, *rest):
     residents = rest[:tparts]
     table = rest[tparts]
     outs = rest[tparts + 1 : 2 * tparts + 1]
-    cross, total = rest[2 * tparts + 1 :]
+    *crosses, total = rest[2 * tparts + 1 :]
     steps, _, rows2, _ = panels.shape
     channels = rows2 // 2
     local = tparts * channels
     me = lax.axis_index("ta")
-    total[...] = jnp.zeros_like(total)
-
-    @pl.loop(0, N1 // GROUP)
-    def _(group):
-        for sub_index in range(GROUP):
-            k1 = group * GROUP + sub_index
-            col = sub_index * 2 * K2
+    starts = [sum(GROUPS[:index]) for index in range(len(GROUPS) + 1)]
+
+    def fill(cross, group):
+        for k1 in range(starts[group], starts[group + 1]):
+            col = (k1 - starts[group]) * 2 * K2
             halves = [r[k1].astype(jnp.float32) for r in residents]
             re = jnp.concatenate([v[:channels] for v in halves], axis=0).astype(jnp.bfloat16)
             im = jnp.concatenate([v[channels:] for v in halves], axis=0).astype(jnp.bfloat16)
@@ -201,12 +199,20 @@
                     at = pl.ds((s * channels + i) * local, local)
                     cross[at, pl.ds(col, K2)] = a * re + b * im
                     cross[at, pl.ds(col + K2, K2)] = a * im - b * re
-        depth = GROUP * 2 * K2
-        total[...] += jnp.dot(
-            cross[...],
-            table[pl.ds(pl.multiple_of(group * depth, depth), depth), :],
+
+    fill(crosses[0], 0)
+    for group in range(len(GROUPS)):
+        if group + 1 < len(GROUPS):
+            fill(crosses[group + 1], group + 1)
+        part = jnp.dot(
+            crosses[group][...],
+            table[starts[group] * 2 * K2 : starts[group + 1] * 2 * K2, :],
             preferred_element_type=jnp.float32,
         )
+        if group == 0:
+            total[...] = part
+        else:
+            total[...] += part
 
     width = LAGS // tparts
     lane = lax.broadcasted_iota(jnp.int32, (channels, LAGS), 1) // width
@@ -242,9 +248,9 @@
         in_specs=[vmem] * (tparts + 2),
         out_specs=[vmem] * tparts,
         scratch_shapes=[
-            pltpu.VMEM((pairs, GROUP * 2 * K2), jnp.bfloat16),
-            pltpu.VMEM((pairs, LAGS), jnp.float32),
-        ],
+            pltpu.VMEM((pairs, group * 2 * K2), jnp.bfloat16) for group in GROUPS
+        ]
+        + [pltpu.VMEM((pairs, LAGS), jnp.float32)],
         compiler_params=pltpu.CompilerParams(vmem_limit_bytes=32 * 1024 * 1024),
         cost_estimate=pl.CostEstimate(flops=4 * 10**9, bytes_accessed=3 * 10**6, transcendentals=0),
         name="correlate",
@@ -297,8 +303,8 @@
         residents = [lax.ppermute(block, "ta", flip("ta", far)) for far in range(1, tparts)]
         return jnp.take(lax.all_gather(block, "ch"), owners, axis=0), residents
     away = (owners ^ me).reshape((steps,) + (1,) * block.ndim)
-    even_plan = [('ta', 3), ('ta', 2), ('ch', 2), ('ch', 4), ('ta', 1), ('ch', 6)]
-    odd_plan = [('ch', 2), ('ch', 4), ('ta', 3), ('ta', 2), ('ch', 6), ('ta', 1)]
+    even_plan = [("ta", 3), ("ta", 2), ("ta", 1), ("ch", 2), ("ch", 4), ("ch", 6)]
+    odd_plan = even_plan[3:] + even_plan[:3]
     got = []
     for even_move, odd_move in zip(even_plan, odd_plan):
         perm = []

time: 39.3 us -> 38.3 us (0.975)
  Pallas kernels: 5.29 us -> 4.26 us
    pallas_call x1, Pallas kernels: 3.49 us -> 2.45 us  [correlate(): pl.pallas_call(lambda *refs: correlate_kernel(tparts, *refs), out_shape=[...]
where the time goes in v4:
time: 38.3 us; the launch traced here: 38.1 us
  starting transfers between devices  17.4 us (45%)
  waiting for transfers between devices  13.1 us (34%)
  Pallas kernels  4.26 us (11%)
  other arithmetic  2.16 us (6%)
  local copies, waits for them, and re-layouts  1.03 us (3%)
    ppermute x6, starting transfers between devices, exchange(): got.append(lax.ppermute(block, ('ch', 'ta'), perm))  8.01 us
    ppermute x3, starting transfers between devices, body(): lax.ppermute(own[far], 'ta', flip('ta', far))  5.76 us
    ppermute x6, waiting for transfers between devices, exchange(): got.append(lax.ppermute(block, ('ch', 'ta'), perm))  5.57 us
    ppermute x3, starting transfers between devices, body(): lax.ppermute(piece, 'ta', flip('ta', far))  3.55 us
    ppermute x3, waiting for transfers between devices, body(): lax.ppermute(own[far], 'ta', flip('ta', far))  3.13 us
    ppermute x3, waiting for transfers between devices, body(): lax.ppermute(piece, 'ta', flip('ta', far))  2.88 us
    pallas_call x1, Pallas kernels, correlate(): pl.pallas_call(lambda *refs: correlate_kernel(tparts, *refs), out_shape=[...  2.45 us
    ppermute x1, waiting for transfers between devices, exchange(): other = lax.ppermute(held, 'ch', flip('ch', 1 << bit))  1.52 us
  transfers between devices with their start and end apart: 13, of which 10 were waited for; matrix products, arithmetic and copies ran while one was open for 5% of the time, Pallas kernels for 0%

profile of v4, /device:TPU:0, one launch (start us, length us, event | category | flops | bytes accessed | tf_op | source)
XLA Modules:
  0.0 38.1 jit_solution(15791793475435280612)
XLA Ops:
  0.0 1.0 %constant_dynamic-slice_fusion = (f32[8,2048]{1,0:T(8,128)S(1)}, f32[8,2048]{1,0:T(8,128)S(1)}, f32[8,2048]{1,0:T(8,128)S(1)}, f32[8,2048]{1,0:T(8,128)S(1)}) fusion(f32[32,2048]{1,0:T(8,128)} %param.5, s32[]{:T(128)S(6)} %select_n.59, s32[]{:T(128)S(6)} %select_n.57, s32[]{:T(128)S(6)} %select_n.56, s32[]{:T(128)S(6)} %select_n.58), kind=kLoop, calls=%fused_computation.9 | loop fusion | bytes 524304 | tf_op jit(solution)/shard_map/dynamic_slice | solution.py:338
  1.0 5.1 %collective-permute-start.2 = (f32[8,2048]{1,0:T(8,128)S(1)}, f32[8,2048]{1,0:T(8,128)S(1)}, u32[]{:S(2)}, u32[]{:S(2)}) collective-permute-start(f32[8,2048]{1,0:T(8,128)S(1)} %get-tuple-element.19), channel_id=1, source_target_pairs={{0,3},{1,2},{2,1},{3,0},{4,7},{5,6},{6,5},{7,4},{8,11},{9,10},{10,... | collective-permute-start | bytes 196616 | tf_op jit(solution)/shard_map/ppermute | solution.py:342
  6.1 0.0 collective-permute-start
  6.1 0.6 %collective-permute-start.1 = (f32[8,2048]{1,0:T(8,128)S(1)}, f32[8,2048]{1,0:T(8,128)S(1)}, u32[]{:S(2)}, u32[]{:S(2)}) collective-permute-start(f32[8,2048]{1,0:T(8,128)S(1)} %get-tuple-element.22), channel_id=1, source_target_pairs={{0,2},{1,3},{2,0},{3,1},{4,6},{5,7},{6,4},{7,5},{8,10},{9,11},{10,... | collective-permute-start | bytes 196616 | tf_op jit(solution)/shard_map/ppermute | solution.py:342
  6.7 1.1 %broadcast_multiply_fusion.refs_5_ = f32[576,256]{1,0:T(8,128)S(1)} fusion(f32[576,256]{1,0:T(8,128)} %constant.34.clone, f32[]{:T(128)} %constant.12.clone.1), kind=kLoop, calls=%fused_computation | loop fusion | flops 147456 | bytes 1179652 | tf_op jit(solution)/shard_map/mul | solution.py:346
  7.8 0.0 copy-start.1
  7.8 0.7 %dynamic-slice_convert_fusion = f32[8]{0:T(128)S(1)} fusion(s32[32]{0:T(128)} %param.6, s32[]{:T(128)S(6)} %select_n.56), kind=kLoop, calls=%fused_computation.13 | loop fusion | flops 8 | bytes 68 | tf_op jit(solution)/shard_map/convert_element_type | solution.py:345
  8.6 0.4 %collective-permute-done.2.refs_3_ = f32[8,2048]{1,0:T(8,128)S(1)} collective-permute-done((f32[8,2048]{1,0:T(8,128)S(1)}, f32[8,2048]{1,0:T(8,128)S(1)}, u32[]{:S(2)}, u32[]{:S(2)}) %collective-permute-start.2) | collective-permute-done | bytes 65568 | tf_op jit(solution)/shard_map/ppermute | solution.py:342
  9.0 1.8 %collective-permute-done.refs_1_ = f32[8,2048]{1,0:T(8,128)S(1)} collective-permute-done((f32[8,2048]{1,0:T(8,128)S(1)}, f32[8,2048]{1,0:T(8,128)S(1)}, u32[]{:S(2)}, u32[]{:S(2)}) %collective-permute-start) | collective-permute-done | bytes 65568 | tf_op jit(solution)/shard_map/ppermute | solution.py:342
  10.7 1.0 %collective-permute-done.1.refs_2_ = f32[8,2048]{1,0:T(8,128)S(1)} collective-permute-done((f32[8,2048]{1,0:T(8,128)S(1)}, f32[8,2048]{1,0:T(8,128)S(1)}, u32[]{:S(2)}, u32[]{:S(2)}) %collective-permute-start.1) | collective-permute-done | bytes 65568 | tf_op jit(solution)/shard_map/ppermute | solution.py:342
  11.7 0.1 broadcast_in_dim.61.refs_4_
  11.8 0.6 %spectrum.1.refs_1_ = bf16[32,16,128]{2,1,0:T(8,128)(2,1)S(1)} custom-call(f32[8,2048]{1,0:T(8,128)S(1)} %get-tuple-element.21.refs_0_, f32[8,2048]{1,0:T(8,128)S(1)} %collective-permute-done.refs_1_, f32[8,2048]{1,0:T(8,128)S(1)} %collective-permute-done.1.refs_2_, f32[8,2048]{1,0:T(8,128)S(1)} %collective-permute-done.2.refs_3_, ...), custom_call_target="tpu_custom_call" | custom-call | flops 1000000000 | bytes 1000000 | tf_op jit(solution)/shard_map/spectrum/pallas_call | solution.py:154
  12.4 0.0 copy-start
  12.4 1.6 %collective-permute-start.8 = (bf16[32,16,128]{2,1,0:T(8,128)(2,1)S(1)}, bf16[32,16,128]{2,1,0:T(8,128)(2,1)S(1)}, u32[]{:S(2)}, u32[]{:S(2)}) collective-permute-start(bf16[32,16,128]{2,1,0:T(8,128)(2,1)S(1)} %spectrum.1.refs_1_), channel_id=1, source_target_pairs={{0,8},{1,9},{2,10},{3,11},{4,7},{5,6},{6,5},{7,4},{8,0},{9,1},{10,... | collective-permute-start | bytes 393224 | tf_op jit(solution)/shard_map/ppermute | solution.py:316
  14.0 2.2 %collective-permute-start.7 = (bf16[32,16,128]{2,1,0:T(8,128)(2,1)S(1)}, bf16[32,16,128]{2,1,0:T(8,128)(2,1)S(1)}, u32[]{:S(2)}, u32[]{:S(2)}) collective-permute-start(bf16[32,16,128]{2,1,0:T(8,128)(2,1)S(1)} %spectrum.1.refs_1_), channel_id=1, source_target_pairs={{0,3},{1,2},{2,1},{3,0},{4,12},{5,13},{6,14},{7,15},{8,11},{9,10},... | collective-permute-start | bytes 393224 | tf_op jit(solution)/shard_map/ppermute | solution.py:316
  16.2 0.0 copy-done.1
  16.2 1.6 %collective-permute-start.6 = (bf16[32,16,128]{2,1,0:T(8,128)(2,1)S(1)}, bf16[32,16,128]{2,1,0:T(8,128)(2,1)S(1)}, u32[]{:S(2)}, u32[]{:S(2)}) collective-permute-start(bf16[32,16,128]{2,1,0:T(8,128)(2,1)S(1)} %spectrum.1.refs_1_), channel_id=1, source_target_pairs={{0,16},{1,17},{2,18},{3,19},{4,6},{5,7},{6,4},{7,5},{8,24},{9,25},... | collective-permute-start | bytes 393224 | tf_op jit(solution)/shard_map/ppermute | solution.py:316
  17.8 0.9 %collective-permute-start.5 = (bf16[32,16,128]{2,1,0:T(8,128)(2,1)S(1)}, bf16[32,16,128]{2,1,0:T(8,128)(2,1)S(1)}, u32[]{:S(2)}, u32[]{:S(2)}) collective-permute-start(bf16[32,16,128]{2,1,0:T(8,128)(2,1)S(1)} %spectrum.1.refs_1_), channel_id=1, source_target_pairs={{0,2},{1,3},{2,0},{3,1},{4,20},{5,21},{6,22},{7,23},{8,10},{9,11},... | collective-permute-start | bytes 393224 | tf_op jit(solution)/shard_map/ppermute | solution.py:316
  18.6 0.5 %collective-permute-start.4 = (bf16[32,16,128]{2,1,0:T(8,128)(2,1)S(1)}, bf16[32,16,128]{2,1,0:T(8,128)(2,1)S(1)}, u32[]{:S(2)}, u32[]{:S(2)}) collective-permute-start(bf16[32,16,128]{2,1,0:T(8,128)(2,1)S(1)} %spectrum.1.refs_1_), channel_id=1, source_target_pairs={{0,24},{1,25},{2,26},{3,27},{4,5},{5,4},{6,7},{7,6},{8,16},{9,17},... | collective-permute-start | bytes 393224 | tf_op jit(solution)/shard_map/ppermute | solution.py:316
  19.1 0.0 collective-permute-done.8
  19.1 1.4 %collective-permute-start.3 = (bf16[32,16,128]{2,1,0:T(8,128)(2,1)S(1)}, bf16[32,16,128]{2,1,0:T(8,128)(2,1)S(1)}, u32[]{:S(2)}, u32[]{:S(2)}) collective-permute-start(bf16[32,16,128]{2,1,0:T(8,128)(2,1)S(1)} %spectrum.1.refs_1_), channel_id=1, source_target_pairs={{0,1},{1,0},{2,3},{3,2},{4,28},{5,29},{6,30},{7,31},{8,9},{9,8},{1... | collective-permute-start | bytes 393224 | tf_op jit(solution)/shard_map/ppermute | solution.py:316
  20.5 0.4 %collective-permute-done.7 = bf16[32,16,128]{2,1,0:T(8,128)(2,1)S(1)} collective-permute-done((bf16[32,16,128]{2,1,0:T(8,128)(2,1)S(1)}, bf16[32,16,128]{2,1,0:T(8,128)(2,1)S(1)}, u32[]{:S(2)}, u32[]{:S(2)}) %collective-permute-start.7) | collective-permute-done | bytes 131104 | tf_op jit(solution)/shard_map/ppermute | solution.py:316
  20.9 2.2 %collective-permute-done.6 = bf16[32,16,128]{2,1,0:T(8,128)(2,1)S(1)} collective-permute-done((bf16[32,16,128]{2,1,0:T(8,128)(2,1)S(1)}, bf16[32,16,128]{2,1,0:T(8,128)(2,1)S(1)}, u32[]{:S(2)}, u32[]{:S(2)}) %collective-permute-start.6) | collective-permute-done | bytes 131104 | tf_op jit(solution)/shard_map/ppermute | solution.py:316
  23.1 3.0 %collective-permute-done.5 = bf16[32,16,128]{2,1,0:T(8,128)(2,1)S(1)} collective-permute-done((bf16[32,16,128]{2,1,0:T(8,128)(2,1)S(1)}, bf16[32,16,128]{2,1,0:T(8,128)(2,1)S(1)}, u32[]{:S(2)}, u32[]{:S(2)}) %collective-permute-start.5) | collective-permute-done | bytes 131104 | tf_op jit(solution)/shard_map/ppermute | solution.py:316
  26.1 0.0 collective-permute-done.4
  26.1 0.0 collective-permute-done.3
  26.1 0.1 select_select_fusion
  26.3 0.1 collective-permute-start.9
  26.3 1.5 %collective-permute-done.9 = bf16[2,32,16,128]{3,2,1,0:T(8,128)(2,1)S(1)} collective-permute-done((bf16[2,32,16,128]{3,2,1,0:T(8,128)(2,1)S(1)}, bf16[2,32,16,128]{3,2,1,0:T(8,128)(2,1)S(1)}, u32[]{:S(2)}, u32[]{:S(2)}) %collective-permute-start.9) | collective-permute-done | bytes 262176 | tf_op jit(solution)/shard_map/ppermute | solution.py:327
  27.9 0.1 broadcast_select_fusion.refs_0_
  28.0 0.0 copy-done
  28.0 2.5 %correlate.1 = (bf16[128,128]{1,0:T(8,128)(2,1)S(1)}, bf16[128,128]{1,0:T(8,128)(2,1)S(1)}, bf16[128,128]{1,0:T(8,128)(2,1)S(1)}, bf16[128,128]{1,0:T(8,128)(2,1)S(1)}) custom-call(bf16[2,32,16,128]{3,2,1,0:T(8,128)(2,1)S(1)} %broadcast_select_fusion.refs_0_, bf16[32,16,128]{2,1,0:T(8,128)(2,1)S(1)} %spectrum.1.refs_1_, ...), custom_call_target="tpu_custom_call" | custom-call | flops 4000000000 | bytes 3000000 | tf_op jit(solution)/shard_map/correlate/pallas_call | solution.py:243
  30.5 0.5 %collective-permute-start.10 = (bf16[128,128]{1,0:T(8,128)(2,1)S(1)}, bf16[128,128]{1,0:T(8,128)(2,1)S(1)}, u32[]{:S(2)}, u32[]{:S(2)}) collective-permute-start(bf16[128,128]{1,0:T(8,128)(2,1)S(1)} %get-tuple-element.10), channel_id=1, source_target_pairs={{0,2},{1,3},{2,0},{3,1},{4,6},{5,7},{6,4},{7,5},{8,10},{9,11},{10,... | collective-permute-start | bytes 98312 | tf_op jit(solution)/shard_map/ppermute | solution.py:351
  31.0 1.7 %collective-permute-start.11 = (bf16[128,128]{1,0:T(8,128)(2,1)S(1)}, bf16[128,128]{1,0:T(8,128)(2,1)S(1)}, u32[]{:S(2)}, u32[]{:S(2)}) collective-permute-start(bf16[128,128]{1,0:T(8,128)(2,1)S(1)} %get-tuple-element.11), channel_id=1, source_target_pairs={{0,3},{1,2},{2,1},{3,0},{4,7},{5,6},{6,5},{7,4},{8,11},{9,10},{10,... | collective-permute-start | bytes 98312 | tf_op jit(solution)/shard_map/ppermute | solution.py:351
  32.6 1.4 %collective-permute-start.12 = (bf16[128,128]{1,0:T(8,128)(2,1)S(1)}, bf16[128,128]{1,0:T(8,128)(2,1)S(1)}, u32[]{:S(2)}, u32[]{:S(2)}) collective-permute-start(bf16[128,128]{1,0:T(8,128)(2,1)S(1)} %get-tuple-element.12), channel_id=1, source_target_pairs={{0,1},{1,0},{2,3},{3,2},{4,5},{5,4},{6,7},{7,6},{8,9},{9,8},{10,11... | collective-permute-start | bytes 98312 | tf_op jit(solution)/shard_map/ppermute | solution.py:351
  34.0 1.9 %collective-permute-done.10.refs_1_ = bf16[128,128]{1,0:T(8,128)(2,1)S(1)} collective-permute-done((bf16[128,128]{1,0:T(8,128)(2,1)S(1)}, bf16[128,128]{1,0:T(8,128)(2,1)S(1)}, u32[]{:S(2)}, u32[]{:S(2)}) %collective-permute-start.10) | collective-permute-done | bytes 32800 | tf_op jit(solution)/shard_map/ppermute | solution.py:351
  36.0 0.8 %collective-permute-done.11.refs_2_ = bf16[128,128]{1,0:T(8,128)(2,1)S(1)} collective-permute-done((bf16[128,128]{1,0:T(8,128)(2,1)S(1)}, bf16[128,128]{1,0:T(8,128)(2,1)S(1)}, u32[]{:S(2)}, u32[]{:S(2)}) %collective-permute-start.11) | collective-permute-done | bytes 32800 | tf_op jit(solution)/shard_map/ppermute | solution.py:351
  36.8 0.1 collective-permute-done.12.refs_3_
  36.9 1.2 %place.1 = f32[2,32,32,32]{3,2,1,0:T(8,128)} custom-call(bf16[128,128]{1,0:T(8,128)(2,1)S(1)} %get-tuple-element.9.refs_0_, bf16[128,128]{1,0:T(8,128)(2,1)S(1)} %collective-permute-done.10.refs_1_, bf16[128,128]{1,0:T(8,128)(2,1)S(1)} %collective-permute-done.11.refs_2_, bf16[128,128]{1,0:T(8,128)(2,1)S(1)} %collective-permute-done.12.refs_3_), custom_call_target="tpu_custom_call" | custom-call | tf_op jit(solution)/shard_map/place/pallas_call | solution.py:283
  (4 shorter events, 0.1 us)
Async XLA Ops:
  1.0 8.0 %collective-permute-start.2 = (f32[8,2048]{1,0:T(8,128)S(1)}, f32[8,2048]{1,0:T(8,128)S(1)}, u32[]{:S(2)}, u32[]{:S(2)}) collective-permute-start(f32[8,2048]{1,0:T(8,128)S(1)} %get-tuple-element.19), channel_id=1, source_target_pairs={{0,3},{1,2},{2,1},{3,0},{4,7},{5,6},{6,5},{7,4},{8,11},{9,10},{10,... | collective-permute-start | bytes 196616 | tf_op jit(solution)/shard_map/ppermute | solution.py:342
  6.1 4.7 %collective-permute-start = (f32[8,2048]{1,0:T(8,128)S(1)}, f32[8,2048]{1,0:T(8,128)S(1)}, u32[]{:S(2)}, u32[]{:S(2)}) collective-permute-start(f32[8,2048]{1,0:T(8,128)S(1)} %get-tuple-element.20), channel_id=1, source_target_pairs={{0,1},{1,0},{2,3},{3,2},{4,5},{5,4},{6,7},{7,6},{8,9},{9,8},{10,11... | collective-permute-start | bytes 196616 | tf_op jit(solution)/shard_map/ppermute | solution.py:342
  6.1 5.6 %collective-permute-start.1 = (f32[8,2048]{1,0:T(8,128)S(1)}, f32[8,2048]{1,0:T(8,128)S(1)}, u32[]{:S(2)}, u32[]{:S(2)}) collective-permute-start(f32[8,2048]{1,0:T(8,128)S(1)} %get-tuple-element.22), channel_id=1, source_target_pairs={{0,2},{1,3},{2,0},{3,1},{4,6},{5,7},{6,4},{7,5},{8,10},{9,11},{10,... | collective-permute-start | bytes 196616 | tf_op jit(solution)/shard_map/ppermute | solution.py:342
  7.8 8.3 %copy-start.1 = (s32[2]{0:T(128)S(1)}, s32[2]{0:T(128)}, u32[]{:S(2)}) copy-start(s32[2]{0:T(128)} %param.7) | copy-start | bytes 28
  12.4 15.6 %copy-start = (bf16[8192,128]{1,0:T(8,128)(2,1)S(1)}, bf16[8192,128]{1,0:T(8,128)(2,1)}, u32[]{:S(2)}) copy-start(bf16[8192,128]{1,0:T(8,128)(2,1)} %constant.35.clone.refs_5_) | copy-start | bytes 6291460
  12.4 6.7 %collective-permute-start.8 = (bf16[32,16,128]{2,1,0:T(8,128)(2,1)S(1)}, bf16[32,16,128]{2,1,0:T(8,128)(2,1)S(1)}, u32[]{:S(2)}, u32[]{:S(2)}) collective-permute-start(bf16[32,16,128]{2,1,0:T(8,128)(2,1)S(1)} %spectrum.1.refs_1_), channel_id=1, source_target_pairs={{0,8},{1,9},{2,10},{3,11},{4,7},{5,6},{6,5},{7,4},{8,0},{9,1},{10,... | collective-permute-start | bytes 393224 | tf_op jit(solution)/shard_map/ppermute | solution.py:316
  14.0 6.9 %collective-permute-start.7 = (bf16[32,16,128]{2,1,0:T(8,128)(2,1)S(1)}, bf16[32,16,128]{2,1,0:T(8,128)(2,1)S(1)}, u32[]{:S(2)}, u32[]{:S(2)}) collective-permute-start(bf16[32,16,128]{2,1,0:T(8,128)(2,1)S(1)} %spectrum.1.refs_1_), channel_id=1, source_target_pairs={{0,3},{1,2},{2,1},{3,0},{4,12},{5,13},{6,14},{7,15},{8,11},{9,10},... | collective-permute-start | bytes 393224 | tf_op jit(solution)/shard_map/ppermute | solution.py:316
  16.2 6.9 %collective-permute-start.6 = (bf16[32,16,128]{2,1,0:T(8,128)(2,1)S(1)}, bf16[32,16,128]{2,1,0:T(8,128)(2,1)S(1)}, u32[]{:S(2)}, u32[]{:S(2)}) collective-permute-start(bf16[32,16,128]{2,1,0:T(8,128)(2,1)S(1)} %spectrum.1.refs_1_), channel_id=1, source_target_pairs={{0,16},{1,17},{2,18},{3,19},{4,6},{5,7},{6,4},{7,5},{8,24},{9,25},... | collective-permute-start | bytes 393224 | tf_op jit(solution)/shard_map/ppermute | solution.py:316
  17.8 8.3 %collective-permute-start.5 = (bf16[32,16,128]{2,1,0:T(8,128)(2,1)S(1)}, bf16[32,16,128]{2,1,0:T(8,128)(2,1)S(1)}, u32[]{:S(2)}, u32[]{:S(2)}) collective-permute-start(bf16[32,16,128]{2,1,0:T(8,128)(2,1)S(1)} %spectrum.1.refs_1_), channel_id=1, source_target_pairs={{0,2},{1,3},{2,0},{3,1},{4,20},{5,21},{6,22},{7,23},{8,10},{9,11},... | collective-permute-start | bytes 393224 | tf_op jit(solution)/shard_map/ppermute | solution.py:316
  18.6 7.5 %collective-permute-start.4 = (bf16[32,16,128]{2,1,0:T(8,128)(2,1)S(1)}, bf16[32,16,128]{2,1,0:T(8,128)(2,1)S(1)}, u32[]{:S(2)}, u32[]{:S(2)}) collective-permute-start(bf16[32,16,128]{2,1,0:T(8,128)(2,1)S(1)} %spectrum.1.refs_1_), channel_id=1, source_target_pairs={{0,24},{1,25},{2,26},{3,27},{4,5},{5,4},{6,7},{7,6},{8,16},{9,17},... | collective-permute-start | bytes 393224 | tf_op jit(solution)/shard_map/ppermute | solution.py:316
  19.1 7.0 %collective-permute-start.3 = (bf16[32,16,128]{2,1,0:T(8,128)(2,1)S(1)}, bf16[32,16,128]{2,1,0:T(8,128)(2,1)S(1)}, u32[]{:S(2)}, u32[]{:S(2)}) collective-permute-start(bf16[32,16,128]{2,1,0:T(8,128)(2,1)S(1)} %spectrum.1.refs_1_), channel_id=1, source_target_pairs={{0,1},{1,0},{2,3},{3,2},{4,28},{5,29},{6,30},{7,31},{8,9},{9,8},{1... | collective-permute-start | bytes 393224 | tf_op jit(solution)/shard_map/ppermute | solution.py:316
  26.3 1.6 %collective-permute-start.9 = (bf16[2,32,16,128]{3,2,1,0:T(8,128)(2,1)S(1)}, bf16[2,32,16,128]{3,2,1,0:T(8,128)(2,1)S(1)}, u32[]{:S(2)}, u32[]{:S(2)}) collective-permute-start(bf16[2,32,16,128]{3,2,1,0:T(8,128)(2,1)S(1)} %select_select_fusion), channel_id=1, source_target_pairs={{0,4},{4,0},{8,12},{12,8},{16,20},{20,16},{24,28},{28,24},{1,5},{5... | collective-permute-start | bytes 786440 | tf_op jit(solution)/shard_map/ppermute | solution.py:327
  30.5 5.5 %collective-permute-start.10 = (bf16[128,128]{1,0:T(8,128)(2,1)S(1)}, bf16[128,128]{1,0:T(8,128)(2,1)S(1)}, u32[]{:S(2)}, u32[]{:S(2)}) collective-permute-start(bf16[128,128]{1,0:T(8,128)(2,1)S(1)} %get-tuple-element.10), channel_id=1, source_target_pairs={{0,2},{1,3},{2,0},{3,1},{4,6},{5,7},{6,4},{7,5},{8,10},{9,11},{10,... | collective-permute-start | bytes 98312 | tf_op jit(solution)/shard_map/ppermute | solution.py:351
  31.0 5.8 %collective-permute-start.11 = (bf16[128,128]{1,0:T(8,128)(2,1)S(1)}, bf16[128,128]{1,0:T(8,128)(2,1)S(1)}, u32[]{:S(2)}, u32[]{:S(2)}) collective-permute-start(bf16[128,128]{1,0:T(8,128)(2,1)S(1)} %get-tuple-element.11), channel_id=1, source_target_pairs={{0,3},{1,2},{2,1},{3,0},{4,7},{5,6},{6,5},{7,4},{8,11},{9,10},{10,... | collective-permute-start | bytes 98312 | tf_op jit(solution)/shard_map/ppermute | solution.py:351
  32.6 4.3 %collective-permute-start.12 = (bf16[128,128]{1,0:T(8,128)(2,1)S(1)}, bf16[128,128]{1,0:T(8,128)(2,1)S(1)}, u32[]{:S(2)}, u32[]{:S(2)}) collective-permute-start(bf16[128,128]{1,0:T(8,128)(2,1)S(1)} %get-tuple-element.12), channel_id=1, source_target_pairs={{0,1},{1,0},{2,3},{3,2},{4,5},{5,4},{6,7},{7,6},{8,9},{9,8},{10,11... | collective-permute-start | bytes 98312 | tf_op jit(solution)/shard_map/ppermute | solution.py:351

commit v5 on v4

--- a/solution.py
+++ b/solution.py
@@ -169,7 +169,7 @@
     )(*blocks, alive, tables)
 
 
-GROUPS = (2, 6, 12, 12)
+GROUPS = (1, 3, 8, 10, 10)
 
 
 def correlate_kernel(tparts, panels, *rest):
@@ -257,37 +257,51 @@
     )(panels, *residents, lag_table())
 
 
-def place_kernel(tparts, steps, channels, *refs):
-    pieces, out = refs[:tparts], refs[tparts]
+def place_kernel(slots, steps, channels, tparts, *refs):
+    count = len(slots)
+    pieces = refs[:count]
+    out, stage, sems = refs[-3:]
     me = lax.axis_index("ta")
     width = LAGS // tparts
-    for far in range(tparts):
-        source = me ^ SUMS_PLAN[far]
-        value = pieces[far][...].astype(jnp.float32)
+    copies = []
+    for index, slot in enumerate(slots):
+        source = me ^ SUMS_PLAN[slot]
+        value = pieces[index][...].astype(jnp.float32)
         for step in range(tparts):
             block = source ^ step
             moved = value if step == 0 else pltpu.roll(value, LAGS - step * width, 1)
-            moved = moved[:, :width].reshape(steps, channels, channels, width)
-            out[
-                :,
-                pl.ds(source * channels, channels),
-                pl.ds(pl.multiple_of(block * channels, channels), channels),
-                :,
-            ] = moved
-
-
-def place(pieces, steps, channels):
+            stage[index, :, :, pl.ds(pl.multiple_of(block * channels, channels), channels), :] = (
+                moved[:, :width].reshape(steps, channels, channels, width)
+            )
+        copy = pltpu.make_async_copy(
+            stage.at[index], out.at[:, pl.ds(source * channels, channels)], sems.at[index]
+        )
+        copy.start()
+        copies.append(copy)
+    for copy in copies:
+        copy.wait()
+
+
+def place(pieces, slots, steps, channels, held=None):
     tparts = lax.axis_size("ta")
+    count = len(slots)
     vmem = pl.BlockSpec(memory_space=pltpu.VMEM)
+    hbm = pl.BlockSpec(memory_space=pltpu.HBM)
     local = tparts * channels
+    more = [] if held is None else [held]
     return pl.pallas_call(
-        lambda *refs: place_kernel(tparts, steps, channels, *refs),
+        lambda *refs: place_kernel(slots, steps, channels, tparts, *refs),
         out_shape=jax.ShapeDtypeStruct((steps, local, local, LAGS // tparts), jnp.float32),
-        in_specs=[vmem] * tparts,
-        out_specs=vmem,
+        in_specs=[vmem] * count + [hbm] * len(more),
+        out_specs=hbm,
+        scratch_shapes=[
+            pltpu.VMEM((count, steps, channels, local, LAGS // tparts), jnp.float32),
+            pltpu.SemaphoreType.DMA((count,)),
+        ],
+        input_output_aliases={count: 0} if more else {},
         compiler_params=pltpu.CompilerParams(vmem_limit_bytes=32 * 1024 * 1024),
         name="place",
-    )(*pieces)
+    )(*[pieces[slot] for slot in slots], *more)
 
 
 def flip(axis, mask):
@@ -351,7 +365,8 @@
         lax.ppermute(piece, "ta", flip("ta", far))
         for piece, far in zip(pieces[1:], SUMS_PLAN[1:])
     ]
-    return place(pieces, steps, channels)
+    held = place(pieces, range(2), steps, channels)
+    return place(pieces, range(2, tparts), steps, channels, held)
 
 
 def solution(mesh):

time: 38.3 us -> 38 us (level)
  waiting for transfers between devices: 13.1 us -> 12.2 us
  Pallas kernels: 4.26 us -> 4.88 us
    ppermute x3, waiting for transfers between devices: 2.88 us -> 1.96 us  [body(): lax.ppermute(piece, 'ta', flip('ta', far))]
    pallas_call x1 -> x2, Pallas kernels: 1.16 us -> 1.81 us  [place(): pl.pallas_call(lambda *refs: place_kernel(slots, steps, channels, tparts,...]
  transfers between devices with their start and end apart: 13 -> 13, of which waited for: 10 -> 8; matrix products, arithmetic and copies ran while one was open for 5% -> 5% of each run, Pallas kernels for 0% -> 2%
where the time goes in v5:
time: 38 us; the launch traced here: 37.8 us
  starting transfers between devices  17.4 us (46%)
  waiting for transfers between devices  12.2 us (32%)
  Pallas kernels  4.88 us (13%)
  other arithmetic  2.16 us (6%)
  local copies, waits for them, and re-layouts  1.03 us (3%)
    ppermute x6, starting transfers between devices, exchange(): got.append(lax.ppermute(block, ('ch', 'ta'), perm))  8.01 us
    ppermute x3, starting transfers between devices, body(): lax.ppermute(own[far], 'ta', flip('ta', far))  5.76 us
    ppermute x6, waiting for transfers between devices, exchange(): got.append(lax.ppermute(block, ('ch', 'ta'), perm))  5.57 us
    ppermute x3, starting transfers between devices, body(): lax.ppermute(piece, 'ta', flip('ta', far))  3.55 us
    ppermute x3, waiting for transfers between devices, body(): lax.ppermute(own[far], 'ta', flip('ta', far))  3.13 us
    pallas_call x1, Pallas kernels, correlate(): pl.pallas_call(lambda *refs: correlate_kernel(tparts, *refs), out_shape=[...  2.43 us
    ppermute x3, waiting for transfers between devices, body(): lax.ppermute(piece, 'ta', flip('ta', far))  1.96 us
    pallas_call x2, Pallas kernels, place(): pl.pallas_call(lambda *refs: place_kernel(slots, steps, channels, tparts,...  1.81 us
  transfers between devices with their start and end apart: 13, of which 8 were waited for; matrix products, arithmetic and copies ran while one was open for 5% of the time, Pallas kernels for 2%

profile of v5, /device:TPU:0, one launch (start us, length us, event | category | flops | bytes accessed | tf_op | source)
XLA Modules:
  0.0 37.8 jit_solution(14770596597632795425)
XLA Ops:
  0.0 1.0 %constant_dynamic-slice_fusion = (f32[8,2048]{1,0:T(8,128)S(1)}, f32[8,2048]{1,0:T(8,128)S(1)}, f32[8,2048]{1,0:T(8,128)S(1)}, f32[8,2048]{1,0:T(8,128)S(1)}) fusion(f32[32,2048]{1,0:T(8,128)} %param.5, s32[]{:T(128)S(6)} %select_n.59, s32[]{:T(128)S(6)} %select_n.57, s32[]{:T(128)S(6)} %select_n.56, s32[]{:T(128)S(6)} %select_n.58), kind=kLoop, calls=%fused_computation.9 | loop fusion | bytes 524304 | tf_op jit(solution)/shard_map/dynamic_slice | solution.py:352
  1.0 5.1 %collective-permute-start.2 = (f32[8,2048]{1,0:T(8,128)S(1)}, f32[8,2048]{1,0:T(8,128)S(1)}, u32[]{:S(2)}, u32[]{:S(2)}) collective-permute-start(f32[8,2048]{1,0:T(8,128)S(1)} %get-tuple-element.19), channel_id=1, source_target_pairs={{0,3},{1,2},{2,1},{3,0},{4,7},{5,6},{6,5},{7,4},{8,11},{9,10},{10,... | collective-permute-start | bytes 196616 | tf_op jit(solution)/shard_map/ppermute | solution.py:356
  6.1 0.0 collective-permute-start
  6.1 0.6 %collective-permute-start.1 = (f32[8,2048]{1,0:T(8,128)S(1)}, f32[8,2048]{1,0:T(8,128)S(1)}, u32[]{:S(2)}, u32[]{:S(2)}) collective-permute-start(f32[8,2048]{1,0:T(8,128)S(1)} %get-tuple-element.22), channel_id=1, source_target_pairs={{0,2},{1,3},{2,0},{3,1},{4,6},{5,7},{6,4},{7,5},{8,10},{9,11},{10,... | collective-permute-start | bytes 196616 | tf_op jit(solution)/shard_map/ppermute | solution.py:356
  6.7 1.1 %broadcast_multiply_fusion.refs_5_ = f32[576,256]{1,0:T(8,128)S(1)} fusion(f32[576,256]{1,0:T(8,128)} %constant.34.clone, f32[]{:T(128)} %constant.12.clone.1), kind=kLoop, calls=%fused_computation | loop fusion | flops 147456 | bytes 1179652 | tf_op jit(solution)/shard_map/mul | solution.py:360
  7.8 0.0 copy-start.1
  7.8 0.7 %dynamic-slice_convert_fusion = f32[8]{0:T(128)S(1)} fusion(s32[32]{0:T(128)} %param.6, s32[]{:T(128)S(6)} %select_n.56), kind=kLoop, calls=%fused_computation.13 | loop fusion | flops 8 | bytes 68 | tf_op jit(solution)/shard_map/convert_element_type | solution.py:359
  8.6 0.4 %collective-permute-done.2.refs_3_ = f32[8,2048]{1,0:T(8,128)S(1)} collective-permute-done((f32[8,2048]{1,0:T(8,128)S(1)}, f32[8,2048]{1,0:T(8,128)S(1)}, u32[]{:S(2)}, u32[]{:S(2)}) %collective-permute-start.2) | collective-permute-done | bytes 65568 | tf_op jit(solution)/shard_map/ppermute | solution.py:356
  9.0 1.8 %collective-permute-done.refs_1_ = f32[8,2048]{1,0:T(8,128)S(1)} collective-permute-done((f32[8,2048]{1,0:T(8,128)S(1)}, f32[8,2048]{1,0:T(8,128)S(1)}, u32[]{:S(2)}, u32[]{:S(2)}) %collective-permute-start) | collective-permute-done | bytes 65568 | tf_op jit(solution)/shard_map/ppermute | solution.py:356
  10.7 1.0 %collective-permute-done.1.refs_2_ = f32[8,2048]{1,0:T(8,128)S(1)} collective-permute-done((f32[8,2048]{1,0:T(8,128)S(1)}, f32[8,2048]{1,0:T(8,128)S(1)}, u32[]{:S(2)}, u32[]{:S(2)}) %collective-permute-start.1) | collective-permute-done | bytes 65568 | tf_op jit(solution)/shard_map/ppermute | solution.py:356
  11.7 0.1 broadcast_in_dim.61.refs_4_
  11.8 0.6 %spectrum.1.refs_1_ = bf16[32,16,128]{2,1,0:T(8,128)(2,1)S(1)} custom-call(f32[8,2048]{1,0:T(8,128)S(1)} %get-tuple-element.21.refs_0_, f32[8,2048]{1,0:T(8,128)S(1)} %collective-permute-done.refs_1_, f32[8,2048]{1,0:T(8,128)S(1)} %collective-permute-done.1.refs_2_, f32[8,2048]{1,0:T(8,128)S(1)} %collective-permute-done.2.refs_3_, ...), custom_call_target="tpu_custom_call" | custom-call | flops 1000000000 | bytes 1000000 | tf_op jit(solution)/shard_map/spectrum/pallas_call | solution.py:154
  12.4 0.0 copy-start
  12.4 1.6 %collective-permute-start.8 = (bf16[32,16,128]{2,1,0:T(8,128)(2,1)S(1)}, bf16[32,16,128]{2,1,0:T(8,128)(2,1)S(1)}, u32[]{:S(2)}, u32[]{:S(2)}) collective-permute-start(bf16[32,16,128]{2,1,0:T(8,128)(2,1)S(1)} %spectrum.1.refs_1_), channel_id=1, source_target_pairs={{0,8},{1,9},{2,10},{3,11},{4,7},{5,6},{6,5},{7,4},{8,0},{9,1},{10,... | collective-permute-start | bytes 393224 | tf_op jit(solution)/shard_map/ppermute | solution.py:330
  14.0 2.2 %collective-permute-start.7 = (bf16[32,16,128]{2,1,0:T(8,128)(2,1)S(1)}, bf16[32,16,128]{2,1,0:T(8,128)(2,1)S(1)}, u32[]{:S(2)}, u32[]{:S(2)}) collective-permute-start(bf16[32,16,128]{2,1,0:T(8,128)(2,1)S(1)} %spectrum.1.refs_1_), channel_id=1, source_target_pairs={{0,3},{1,2},{2,1},{3,0},{4,12},{5,13},{6,14},{7,15},{8,11},{9,10},... | collective-permute-start | bytes 393224 | tf_op jit(solution)/shard_map/ppermute | solution.py:330
  16.2 0.0 copy-done.1
  16.2 1.6 %collective-permute-start.6 = (bf16[32,16,128]{2,1,0:T(8,128)(2,1)S(1)}, bf16[32,16,128]{2,1,0:T(8,128)(2,1)S(1)}, u32[]{:S(2)}, u32[]{:S(2)}) collective-permute-start(bf16[32,16,128]{2,1,0:T(8,128)(2,1)S(1)} %spectrum.1.refs_1_), channel_id=1, source_target_pairs={{0,16},{1,17},{2,18},{3,19},{4,6},{5,7},{6,4},{7,5},{8,24},{9,25},... | collective-permute-start | bytes 393224 | tf_op jit(solution)/shard_map/ppermute | solution.py:330
  17.8 0.9 %collective-permute-start.5 = (bf16[32,16,128]{2,1,0:T(8,128)(2,1)S(1)}, bf16[32,16,128]{2,1,0:T(8,128)(2,1)S(1)}, u32[]{:S(2)}, u32[]{:S(2)}) collective-permute-start(bf16[32,16,128]{2,1,0:T(8,128)(2,1)S(1)} %spectrum.1.refs_1_), channel_id=1, source_target_pairs={{0,2},{1,3},{2,0},{3,1},{4,20},{5,21},{6,22},{7,23},{8,10},{9,11},... | collective-permute-start | bytes 393224 | tf_op jit(solution)/shard_map/ppermute | solution.py:330
  18.6 0.5 %collective-permute-start.4 = (bf16[32,16,128]{2,1,0:T(8,128)(2,1)S(1)}, bf16[32,16,128]{2,1,0:T(8,128)(2,1)S(1)}, u32[]{:S(2)}, u32[]{:S(2)}) collective-permute-start(bf16[32,16,128]{2,1,0:T(8,128)(2,1)S(1)} %spectrum.1.refs_1_), channel_id=1, source_target_pairs={{0,24},{1,25},{2,26},{3,27},{4,5},{5,4},{6,7},{7,6},{8,16},{9,17},... | collective-permute-start | bytes 393224 | tf_op jit(solution)/shard_map/ppermute | solution.py:330
  19.1 0.0 collective-permute-done.8
  19.1 1.4 %collective-permute-start.3 = (bf16[32,16,128]{2,1,0:T(8,128)(2,1)S(1)}, bf16[32,16,128]{2,1,0:T(8,128)(2,1)S(1)}, u32[]{:S(2)}, u32[]{:S(2)}) collective-permute-start(bf16[32,16,128]{2,1,0:T(8,128)(2,1)S(1)} %spectrum.1.refs_1_), channel_id=1, source_target_pairs={{0,1},{1,0},{2,3},{3,2},{4,28},{5,29},{6,30},{7,31},{8,9},{9,8},{1... | collective-permute-start | bytes 393224 | tf_op jit(solution)/shard_map/ppermute | solution.py:330
  20.5 0.4 %collective-permute-done.7 = bf16[32,16,128]{2,1,0:T(8,128)(2,1)S(1)} collective-permute-done((bf16[32,16,128]{2,1,0:T(8,128)(2,1)S(1)}, bf16[32,16,128]{2,1,0:T(8,128)(2,1)S(1)}, u32[]{:S(2)}, u32[]{:S(2)}) %collective-permute-start.7) | collective-permute-done | bytes 131104 | tf_op jit(solution)/shard_map/ppermute | solution.py:330
  20.9 2.2 %collective-permute-done.6 = bf16[32,16,128]{2,1,0:T(8,128)(2,1)S(1)} collective-permute-done((bf16[32,16,128]{2,1,0:T(8,128)(2,1)S(1)}, bf16[32,16,128]{2,1,0:T(8,128)(2,1)S(1)}, u32[]{:S(2)}, u32[]{:S(2)}) %collective-permute-start.6) | collective-permute-done | bytes 131104 | tf_op jit(solution)/shard_map/ppermute | solution.py:330
  23.1 3.0 %collective-permute-done.5 = bf16[32,16,128]{2,1,0:T(8,128)(2,1)S(1)} collective-permute-done((bf16[32,16,128]{2,1,0:T(8,128)(2,1)S(1)}, bf16[32,16,128]{2,1,0:T(8,128)(2,1)S(1)}, u32[]{:S(2)}, u32[]{:S(2)}) %collective-permute-start.5) | collective-permute-done | bytes 131104 | tf_op jit(solution)/shard_map/ppermute | solution.py:330
  26.1 0.0 collective-permute-done.4
  26.1 0.0 collective-permute-done.3
  26.1 0.1 select_select_fusion
  26.3 0.1 collective-permute-start.9
  26.3 1.5 %collective-permute-done.9 = bf16[2,32,16,128]{3,2,1,0:T(8,128)(2,1)S(1)} collective-permute-done((bf16[2,32,16,128]{3,2,1,0:T(8,128)(2,1)S(1)}, bf16[2,32,16,128]{3,2,1,0:T(8,128)(2,1)S(1)}, u32[]{:S(2)}, u32[]{:S(2)}) %collective-permute-start.9) | collective-permute-done | bytes 262176 | tf_op jit(solution)/shard_map/ppermute | solution.py:341
  27.9 0.1 broadcast_select_fusion.refs_0_
  28.0 0.0 copy-done
  28.0 2.4 %correlate.1 = (bf16[128,128]{1,0:T(8,128)(2,1)S(1)}, bf16[128,128]{1,0:T(8,128)(2,1)S(1)}, bf16[128,128]{1,0:T(8,128)(2,1)S(1)}, bf16[128,128]{1,0:T(8,128)(2,1)S(1)}) custom-call(bf16[2,32,16,128]{3,2,1,0:T(8,128)(2,1)S(1)} %broadcast_select_fusion.refs_0_, bf16[32,16,128]{2,1,0:T(8,128)(2,1)S(1)} %spectrum.1.refs_1_, ...), custom_call_target="tpu_custom_call" | custom-call | flops 4000000000 | bytes 3000000 | tf_op jit(solution)/shard_map/correlate/pallas_call | solution.py:243
  30.4 0.5 %collective-permute-start.12 = (bf16[128,128]{1,0:T(8,128)(2,1)S(1)}, bf16[128,128]{1,0:T(8,128)(2,1)S(1)}, u32[]{:S(2)}, u32[]{:S(2)}) collective-permute-start(bf16[128,128]{1,0:T(8,128)(2,1)S(1)} %get-tuple-element.12), channel_id=1, source_target_pairs={{0,2},{1,3},{2,0},{3,1},{4,6},{5,7},{6,4},{7,5},{8,10},{9,11},{10,... | collective-permute-start | bytes 98312 | tf_op jit(solution)/shard_map/ppermute | solution.py:365
  30.9 1.7 %collective-permute-start.10 = (bf16[128,128]{1,0:T(8,128)(2,1)S(1)}, bf16[128,128]{1,0:T(8,128)(2,1)S(1)}, u32[]{:S(2)}, u32[]{:S(2)}) collective-permute-start(bf16[128,128]{1,0:T(8,128)(2,1)S(1)} %get-tuple-element.9), channel_id=1, source_target_pairs={{0,3},{1,2},{2,1},{3,0},{4,7},{5,6},{6,5},{7,4},{8,11},{9,10},{10,... | collective-permute-start | bytes 98312 | tf_op jit(solution)/shard_map/ppermute | solution.py:365
  32.6 1.4 %collective-permute-start.11 = (bf16[128,128]{1,0:T(8,128)(2,1)S(1)}, bf16[128,128]{1,0:T(8,128)(2,1)S(1)}, u32[]{:S(2)}, u32[]{:S(2)}) collective-permute-start(bf16[128,128]{1,0:T(8,128)(2,1)S(1)} %get-tuple-element.10), channel_id=1, source_target_pairs={{0,1},{1,0},{2,3},{3,2},{4,5},{5,4},{6,7},{7,6},{8,9},{9,8},{10,11... | collective-permute-start | bytes 98312 | tf_op jit(solution)/shard_map/ppermute | solution.py:365
  34.0 2.0 %collective-permute-done.12.refs_1_ = bf16[128,128]{1,0:T(8,128)(2,1)S(1)} collective-permute-done((bf16[128,128]{1,0:T(8,128)(2,1)S(1)}, bf16[128,128]{1,0:T(8,128)(2,1)S(1)}, u32[]{:S(2)}, u32[]{:S(2)}) %collective-permute-start.12) | collective-permute-done | bytes 32800 | tf_op jit(solution)/shard_map/ppermute | solution.py:365
  35.9 0.9 %place.2.refs_2_ = f32[2,32,32,32]{3,2,1,0:T(8,128)} custom-call(bf16[128,128]{1,0:T(8,128)(2,1)S(1)} %get-tuple-element.11.refs_0_, bf16[128,128]{1,0:T(8,128)(2,1)S(1)} %collective-permute-done.12.refs_1_), custom_call_target="tpu_custom_call" | custom-call | tf_op jit(solution)/shard_map/place/pallas_call | solution.py:292
  36.9 0.0 collective-permute-done.10.refs_0_
  36.9 0.0 collective-permute-done.11.refs_1_
  36.9 0.9 %place.3 = f32[2,32,32,32]{3,2,1,0:T(8,128)} custom-call(bf16[128,128]{1,0:T(8,128)(2,1)S(1)} %collective-permute-done.10.refs_0_, bf16[128,128]{1,0:T(8,128)(2,1)S(1)} %collective-permute-done.11.refs_1_, f32[2,32,32,32]{3,2,1,0:T(8,128)} %place.2.refs_2_), custom_call_target="tpu_custom_call", output_to_operand_aliasing={{}: (2, {})} | custom-call | tf_op jit(solution)/shard_map/place/pallas_call | solution.py:292
  (4 shorter events, 0.1 us)
Async XLA Ops:
  1.0 8.0 %collective-permute-start.2 = (f32[8,2048]{1,0:T(8,128)S(1)}, f32[8,2048]{1,0:T(8,128)S(1)}, u32[]{:S(2)}, u32[]{:S(2)}) collective-permute-start(f32[8,2048]{1,0:T(8,128)S(1)} %get-tuple-element.19), channel_id=1, source_target_pairs={{0,3},{1,2},{2,1},{3,0},{4,7},{5,6},{6,5},{7,4},{8,11},{9,10},{10,... | collective-permute-start | bytes 196616 | tf_op jit(solution)/shard_map/ppermute | solution.py:356
  6.1 4.7 %collective-permute-start = (f32[8,2048]{1,0:T(8,128)S(1)}, f32[8,2048]{1,0:T(8,128)S(1)}, u32[]{:S(2)}, u32[]{:S(2)}) collective-permute-start(f32[8,2048]{1,0:T(8,128)S(1)} %get-tuple-element.20), channel_id=1, source_target_pairs={{0,1},{1,0},{2,3},{3,2},{4,5},{5,4},{6,7},{7,6},{8,9},{9,8},{10,11... | collective-permute-start | bytes 196616 | tf_op jit(solution)/shard_map/ppermute | solution.py:356
  6.1 5.6 %collective-permute-start.1 = (f32[8,2048]{1,0:T(8,128)S(1)}, f32[8,2048]{1,0:T(8,128)S(1)}, u32[]{:S(2)}, u32[]{:S(2)}) collective-permute-start(f32[8,2048]{1,0:T(8,128)S(1)} %get-tuple-element.22), channel_id=1, source_target_pairs={{0,2},{1,3},{2,0},{3,1},{4,6},{5,7},{6,4},{7,5},{8,10},{9,11},{10,... | collective-permute-start | bytes 196616 | tf_op jit(solution)/shard_map/ppermute | solution.py:356
  7.8 8.3 %copy-start.1 = (s32[2]{0:T(128)S(1)}, s32[2]{0:T(128)}, u32[]{:S(2)}) copy-start(s32[2]{0:T(128)} %param.7) | copy-start | bytes 28
  12.4 15.6 %copy-start = (bf16[8192,128]{1,0:T(8,128)(2,1)S(1)}, bf16[8192,128]{1,0:T(8,128)(2,1)}, u32[]{:S(2)}) copy-start(bf16[8192,128]{1,0:T(8,128)(2,1)} %constant.35.clone.refs_5_) | copy-start | bytes 6291460
  12.4 6.7 %collective-permute-start.8 = (bf16[32,16,128]{2,1,0:T(8,128)(2,1)S(1)}, bf16[32,16,128]{2,1,0:T(8,128)(2,1)S(1)}, u32[]{:S(2)}, u32[]{:S(2)}) collective-permute-start(bf16[32,16,128]{2,1,0:T(8,128)(2,1)S(1)} %spectrum.1.refs_1_), channel_id=1, source_target_pairs={{0,8},{1,9},{2,10},{3,11},{4,7},{5,6},{6,5},{7,4},{8,0},{9,1},{10,... | collective-permute-start | bytes 393224 | tf_op jit(solution)/shard_map/ppermute | solution.py:330
  14.0 6.9 %collective-permute-start.7 = (bf16[32,16,128]{2,1,0:T(8,128)(2,1)S(1)}, bf16[32,16,128]{2,1,0:T(8,128)(2,1)S(1)}, u32[]{:S(2)}, u32[]{:S(2)}) collective-permute-start(bf16[32,16,128]{2,1,0:T(8,128)(2,1)S(1)} %spectrum.1.refs_1_), channel_id=1, source_target_pairs={{0,3},{1,2},{2,1},{3,0},{4,12},{5,13},{6,14},{7,15},{8,11},{9,10},... | collective-permute-start | bytes 393224 | tf_op jit(solution)/shard_map/ppermute | solution.py:330
  16.2 6.9 %collective-permute-start.6 = (bf16[32,16,128]{2,1,0:T(8,128)(2,1)S(1)}, bf16[32,16,128]{2,1,0:T(8,128)(2,1)S(1)}, u32[]{:S(2)}, u32[]{:S(2)}) collective-permute-start(bf16[32,16,128]{2,1,0:T(8,128)(2,1)S(1)} %spectrum.1.refs_1_), channel_id=1, source_target_pairs={{0,16},{1,17},{2,18},{3,19},{4,6},{5,7},{6,4},{7,5},{8,24},{9,25},... | collective-permute-start | bytes 393224 | tf_op jit(solution)/shard_map/ppermute | solution.py:330
  17.8 8.3 %collective-permute-start.5 = (bf16[32,16,128]{2,1,0:T(8,128)(2,1)S(1)}, bf16[32,16,128]{2,1,0:T(8,128)(2,1)S(1)}, u32[]{:S(2)}, u32[]{:S(2)}) collective-permute-start(bf16[32,16,128]{2,1,0:T(8,128)(2,1)S(1)} %spectrum.1.refs_1_), channel_id=1, source_target_pairs={{0,2},{1,3},{2,0},{3,1},{4,20},{5,21},{6,22},{7,23},{8,10},{9,11},... | collective-permute-start | bytes 393224 | tf_op jit(solution)/shard_map/ppermute | solution.py:330
  18.6 7.5 %collective-permute-start.4 = (bf16[32,16,128]{2,1,0:T(8,128)(2,1)S(1)}, bf16[32,16,128]{2,1,0:T(8,128)(2,1)S(1)}, u32[]{:S(2)}, u32[]{:S(2)}) collective-permute-start(bf16[32,16,128]{2,1,0:T(8,128)(2,1)S(1)} %spectrum.1.refs_1_), channel_id=1, source_target_pairs={{0,24},{1,25},{2,26},{3,27},{4,5},{5,4},{6,7},{7,6},{8,16},{9,17},... | collective-permute-start | bytes 393224 | tf_op jit(solution)/shard_map/ppermute | solution.py:330
  19.1 7.0 %collective-permute-start.3 = (bf16[32,16,128]{2,1,0:T(8,128)(2,1)S(1)}, bf16[32,16,128]{2,1,0:T(8,128)(2,1)S(1)}, u32[]{:S(2)}, u32[]{:S(2)}) collective-permute-start(bf16[32,16,128]{2,1,0:T(8,128)(2,1)S(1)} %spectrum.1.refs_1_), channel_id=1, source_target_pairs={{0,1},{1,0},{2,3},{3,2},{4,28},{5,29},{6,30},{7,31},{8,9},{9,8},{1... | collective-permute-start | bytes 393224 | tf_op jit(solution)/shard_map/ppermute | solution.py:330
  26.3 1.6 %collective-permute-start.9 = (bf16[2,32,16,128]{3,2,1,0:T(8,128)(2,1)S(1)}, bf16[2,32,16,128]{3,2,1,0:T(8,128)(2,1)S(1)}, u32[]{:S(2)}, u32[]{:S(2)}) collective-permute-start(bf16[2,32,16,128]{3,2,1,0:T(8,128)(2,1)S(1)} %select_select_fusion), channel_id=1, source_target_pairs={{0,4},{4,0},{8,12},{12,8},{16,20},{20,16},{24,28},{28,24},{1,5},{5... | collective-permute-start | bytes 786440 | tf_op jit(solution)/shard_map/ppermute | solution.py:341
  30.4 5.5 %collective-permute-start.12 = (bf16[128,128]{1,0:T(8,128)(2,1)S(1)}, bf16[128,128]{1,0:T(8,128)(2,1)S(1)}, u32[]{:S(2)}, u32[]{:S(2)}) collective-permute-start(bf16[128,128]{1,0:T(8,128)(2,1)S(1)} %get-tuple-element.12), channel_id=1, source_target_pairs={{0,2},{1,3},{2,0},{3,1},{4,6},{5,7},{6,4},{7,5},{8,10},{9,11},{10,... | collective-permute-start | bytes 98312 | tf_op jit(solution)/shard_map/ppermute | solution.py:365
  30.9 5.9 %collective-permute-start.10 = (bf16[128,128]{1,0:T(8,128)(2,1)S(1)}, bf16[128,128]{1,0:T(8,128)(2,1)S(1)}, u32[]{:S(2)}, u32[]{:S(2)}) collective-permute-start(bf16[128,128]{1,0:T(8,128)(2,1)S(1)} %get-tuple-element.9), channel_id=1, source_target_pairs={{0,3},{1,2},{2,1},{3,0},{4,7},{5,6},{6,5},{7,4},{8,11},{9,10},{10,... | collective-permute-start | bytes 98312 | tf_op jit(solution)/shard_map/ppermute | solution.py:365
  32.6 4.3 %collective-permute-start.11 = (bf16[128,128]{1,0:T(8,128)(2,1)S(1)}, bf16[128,128]{1,0:T(8,128)(2,1)S(1)}, u32[]{:S(2)}, u32[]{:S(2)}) collective-permute-start(bf16[128,128]{1,0:T(8,128)(2,1)S(1)} %get-tuple-element.10), channel_id=1, source_target_pairs={{0,1},{1,0},{2,3},{3,2},{4,5},{5,4},{6,7},{7,6},{8,9},{9,8},{10,11... | collective-permute-start | bytes 98312 | tf_op jit(solution)/shard_map/ppermute | solution.py:365
